TPU v7x, 128 devices: a whole 4x4x4 slice. The times are simulated.
128 devices in a mesh: blk: 32 (over y, x, core), ax: 4 (over z).
Axes of the slice: x: 4, y: 4, z: 4, core: 2. Of those that a mesh axis runs over, the one named last changes fastest.
Arguments:
- adjoint: bfloat16 [5, 32, 256, 64, 128], P(None, 'blk', 'ax'), may hold values from -6 to 6
- density: bfloat16 [32, 256, 64, 128], P('blk', 'ax'), may hold values from 0.5 to 1.5
- velocity: bfloat16 [3, 32, 256, 64, 128], P(None, 'blk', 'ax'), may hold values from -3 to 3
- pressure: bfloat16 [32, 256, 64, 128], P('blk', 'ax'), may hold values from 0.5 to 1.5
- metrics: bfloat16 [9, 32, 256, 64, 128], P(None, 'blk', 'ax'), may hold values from -6 to 6
- links: int32 [3, 32, 48], replicated, may hold values from -1 to 47, as said below
Outputs:
- rhs: bfloat16 [5, 32, 256, 64, 128], P(None, 'blk', 'ax')
Inputs may be any that keep to these rules, and one draw needn't show every extreme that they name: links[0] is a source block or -1 (a physical boundary), links[1] a patch of that block, links[2] an orientation 0 or 1. No source patch is named twice. A block names at most 2 patches of any one source block, and some pair of blocks reaches exactly 2. The number of live patches differs between blocks, and at least one block has all 48 live.
All inputs are finite; a program needn't handle non-finite values.
Results may differ from a plain program's by a relative error of at most 0.001.
Values may be sent and summed in bfloat16 or wider, within the bound.
No kernel may reach another device: no remote copies, remote signals or barrier semaphores. Data moves between devices by JAX's collectives and lax.ppermute only.
A program may use at most 256 MiB of HBM per device.

v0:
```python
import jax
import jax.numpy as jnp
from jax import lax
from jax.sharding import PartitionSpec as P

PW = 8


lhs_alpha = 1.0 / 3.0
near_coef = 7.0 / 9.0
far_coef = 1.0 / 36.0
heat_ratio = 1.4
penalty_weight = 1.0


def extended(cells, sides, width):
    for axis, dim in sides:
        count = lax.axis_size(axis)
        ends = count - 1
        head = lax.slice_in_dim(cells, 0, width, axis=dim)
        tail = lax.slice_in_dim(cells, cells.shape[dim] - width, cells.shape[dim], axis=dim)
        cells = jnp.concatenate(
            [
                lax.ppermute(tail, axis, [(i, (i + 1) % count) for i in range(ends)]),
                cells,
                lax.ppermute(head, axis, [((i + 1) % count, i) for i in range(ends)]),
            ],
            axis=dim,
        )
    return cells


def prefix(shard, axis, combine, identity, reverse):
    devices, place = (lax.axis_size(axis), lax.axis_index(axis))
    everything = jax.tree.map(
        lambda part, kind: lax.all_gather(part.astype(kind), axis),
        shard,
        jax.tree.map(lambda a: jnp.bfloat16 if a.dtype == jnp.float32 else a.dtype, shard),
    )
    start = jax.tree.map(
        lambda part, zero: jnp.broadcast_to(jnp.asarray(zero, part.dtype), part.shape),
        shard,
        identity,
    )

    def lap(k, before):
        at = devices - 1 - k if reverse else k
        reached = at > place if reverse else at < place
        new = combine(
            before, jax.tree.map(lambda part, own: part[at].astype(own.dtype), everything, shard)
        )
        return jax.tree.map(lambda a, b: jnp.where(reached, a, b), new, before)

    return lax.fori_loop(0, devices, lap, start)


def line_tables(line_cells):
    position = jnp.arange(line_cells, dtype=jnp.int32)
    middle = jnp.ones((line_cells,), jnp.float32)
    sub_diag = jnp.where(position > 0, lhs_alpha, 0.0).astype(jnp.float32)
    super_diag = jnp.where(position < line_cells - 1, lhs_alpha, 0.0).astype(jnp.float32)
    offset = position[None, :] - position[:, None]
    stencil = near_coef * ((offset == 1).astype(jnp.float32) - (offset == -1).astype(jnp.float32))
    stencil = stencil + far_coef * (
        (offset == 2).astype(jnp.float32) - (offset == -2).astype(jnp.float32)
    )
    inverse = lax.linalg.tridiagonal_solve(
        sub_diag, middle, super_diag, jnp.eye(line_cells, dtype=jnp.float32)
    )
    derivative = lax.linalg.tridiagonal_solve(sub_diag, middle, super_diag, stencil)
    return (inverse, derivative)


def widen(values):
    return values.astype(jnp.float32)


def flux_parts(gradient, metric, density_f, velocity, pressure_f):
    metric_a = widen(metric[0])
    metric_b = widen(metric[1])
    metric_c = widen(metric[2])
    contravariant = (
        metric_a * widen(velocity[0])
        + metric_b * widen(velocity[1])
        + metric_c * widen(velocity[2])
    )
    coupled = density_f * gradient[0] + heat_ratio * pressure_f * gradient[4]
    turned = (metric_a * gradient[1] + metric_b * gradient[2] + metric_c * gradient[3]) / density_f
    return [
        contravariant * gradient[0],
        contravariant * gradient[1] + metric_a * coupled,
        contravariant * gradient[2] + metric_b * coupled,
        contravariant * gradient[3] + metric_c * coupled,
        contravariant * gradient[4] + turned,
    ]


def face_patches(source_field):
    pieces = []
    for surface in (
        source_field[:, :, 0, :],
        source_field[:, :, -1, :],
        source_field[:, :, :, 0],
        source_field[:, :, :, -1],
    ):
        fields, row_count, length = surface.shape
        grouped = surface.reshape(fields, row_count, length // PW, PW)
        pieces.append(jnp.transpose(grouped, (2, 0, 1, 3)))
    return jnp.concatenate(pieces, axis=0)


def compose(earlier, later):
    return (earlier[0] * later[0], later[0] * earlier[1] + later[1])


def body(adjoint, density, velocity, pressure, metrics, links):
    highest = lax.Precision.HIGHEST
    field_bf = adjoint[:, 0]
    density_f = widen(density[0])
    velocity_b = velocity[:, 0]
    pressure_f = widen(pressure[0])
    metric_b = metrics[:, 0]
    field_count, local_cells, y_cells, z_cells = field_bf.shape
    local_inverse = line_tables(local_cells)[0]
    cross_table = line_tables(y_cells)[1]
    depth_table = line_tables(z_cells)[1]
    padded = extended(field_bf, (("ax", 1),), 2).astype(jnp.float32)
    stencil_sum = near_coef * (padded[:, 3 : local_cells + 3] - padded[:, 1 : local_cells + 1])
    stencil_sum = stencil_sum + far_coef * (
        padded[:, 4 : local_cells + 4] - padded[:, 0:local_cells]
    )
    batch_inverse = jnp.broadcast_to(local_inverse, (field_count, local_cells, local_cells))
    partial_value = lax.dot_general(
        batch_inverse,
        stencil_sum.reshape(field_count, local_cells, y_cells * z_cells),
        (((2,), (1,)), ((0,), (0,))),
        precision=highest,
    )
    partial_value = partial_value.reshape(field_count, local_cells, y_cells, z_cells)
    first_end = partial_value[:, 0]
    last_end = partial_value[:, -1]
    corner_first = local_inverse[0, 0]
    corner_cross = local_inverse[0, -1]
    corner_back = local_inverse[-1, 0]
    corner_last = local_inverse[-1, -1]
    segment = lax.axis_index("ax")
    segments = lax.axis_size("ax")
    carry_h = jnp.zeros((), jnp.float32)
    prior_list = []
    pivot_list = []
    for position in range(segments):
        pivot_scale = 1.0 - lhs_alpha * corner_first * carry_h
        prior_list.append(carry_h)
        pivot_list.append(pivot_scale)
        carry_h = (
            lhs_alpha * corner_back * carry_h * (lhs_alpha * corner_cross / pivot_scale)
            + lhs_alpha * corner_last
        )
    prior_h = jnp.stack(prior_list)[segment]
    pivot_scale = jnp.stack(pivot_list)[segment]
    forward_slope = (
        -lhs_alpha * corner_back * (1.0 + lhs_alpha * corner_first * prior_h / pivot_scale)
    )
    forward_shift = last_end + lhs_alpha * corner_back * prior_h * first_end / pivot_scale
    identity = (jnp.ones((1,), jnp.float32), jnp.zeros_like(first_end))
    left_carry = prefix((forward_slope.reshape(1), forward_shift), "ax", compose, identity, False)[
        1
    ]
    middle = (first_end - lhs_alpha * corner_first * left_carry) / pivot_scale
    back_slope = -lhs_alpha * corner_cross / pivot_scale
    right_value = prefix((back_slope.reshape(1), middle), "ax", compose, identity, True)[1]
    own_first = middle + back_slope * right_value
    left_value = left_carry - prior_h * own_first
    grad_x = partial_value - lhs_alpha * (
        left_value[:, None] * local_inverse[:, 0][None, :, None, None]
        + right_value[:, None] * local_inverse[:, -1][None, :, None, None]
    )
    field_rows = widen(field_bf).reshape(field_count * local_cells, y_cells, z_cells)
    batch_cross = jnp.broadcast_to(cross_table, (field_count * local_cells, y_cells, y_cells))
    grad_y = lax.dot_general(
        batch_cross, field_rows, (((2,), (1,)), ((0,), (0,))), precision=highest
    )
    grad_y = grad_y.reshape(field_count, local_cells, y_cells, z_cells)
    grad_z = jnp.dot(widen(field_bf).reshape(-1, z_cells), depth_table.T, precision=highest)
    grad_z = grad_z.reshape(field_count, local_cells, y_cells, z_cells)
    parts_x = flux_parts(grad_x, metric_b[0:3], density_f, velocity_b, pressure_f)
    parts_y = flux_parts(grad_y, metric_b[3:6], density_f, velocity_b, pressure_f)
    parts_z = flux_parts(grad_z, metric_b[6:9], density_f, velocity_b, pressure_f)
    own_faces = face_patches(field_bf)
    patch_count = own_faces.shape[0]
    flat_faces = own_faces.reshape(patch_count, -1)
    own_block = lax.axis_index("blk")
    own_links = lax.dynamic_index_in_dim(links, own_block, 1, keepdims=False)
    source = own_links[0]
    source_face = own_links[1]
    reversed_flag = own_links[2]
    patch_ids = jnp.arange(patch_count, dtype=jnp.int32)
    segment_faces = lax.all_gather(flat_faces[None], "blk", axis=0, tiled=True)
    count_here = segment_faces.shape[0]
    block_ids = jnp.arange(count_here, dtype=jnp.int32)
    selector = (source[:, None, None] == block_ids[None, :, None]) & (
        source_face[:, None, None] == patch_ids[None, None, :]
    )
    selector = selector.astype(jnp.bfloat16).reshape(patch_count, count_here * patch_count)
    gathered = segment_faces.reshape(count_here * patch_count, -1)
    received = jnp.dot(selector, gathered, preferred_element_type=jnp.float32)
    received = received.reshape(own_faces.shape)
    received = jnp.where((reversed_flag == 1)[:, None, None, None], received[..., ::-1], received)
    penalty = jnp.where(
        (source >= 0)[:, None, None, None],
        penalty_weight * (received - own_faces.astype(jnp.float32)),
        0.0,
    )
    z_parts = z_cells // PW
    y_parts = y_cells // PW

    def unfold(stacked, length):
        return jnp.transpose(stacked, (1, 2, 0, 3)).reshape(field_count, local_cells, length)

    plane_low_y = unfold(penalty[:z_parts], z_cells)
    plane_high_y = unfold(penalty[z_parts : 2 * z_parts], z_cells)
    plane_low_z = unfold(penalty[2 * z_parts : 2 * z_parts + y_parts], y_cells)
    plane_high_z = unfold(penalty[2 * z_parts + y_parts :], y_cells)
    y_index = jnp.arange(y_cells, dtype=jnp.int32)[:, None]
    z_index = jnp.arange(z_cells, dtype=jnp.int32)[None, :]
    components = []
    for component in range(5):
        total = parts_x[component] + parts_y[component] + parts_z[component]
        total = total + jnp.where(y_index == 0, plane_low_y[component][:, None, :], 0.0)
        total = total + jnp.where(y_index == y_cells - 1, plane_high_y[component][:, None, :], 0.0)
        total = total + jnp.where(z_index == 0, plane_low_z[component][:, :, None], 0.0)
        total = total + jnp.where(z_index == z_cells - 1, plane_high_z[component][:, :, None], 0.0)
        components.append(total.astype(jnp.bfloat16))
    return jnp.stack(components)[:, None]


def solution(mesh):
    in_specs = (
        P(None, "blk", "ax", None, None),
        P("blk", "ax", None, None),
        P(None, "blk", "ax", None, None),
        P("blk", "ax", None, None),
        P(None, "blk", "ax", None, None),
        P(),
    )
    out_specs = P(None, "blk", "ax", None, None)
    return jax.shard_map(body, mesh=mesh, in_specs=in_specs, out_specs=out_specs, check_vma=False)
```

profile of v0, /device:TPU:0, one launch (start us, length us, event | category | flops | bytes accessed | tf_op | source)
XLA Modules:
  0.0 1026.1 jit_solution(5644185625572482894)
XLA Ops:
  6.5 11.6 %copy.126 = bf16[5,1,64,64,128]{2,4,0,3,1:T(8,128)(2,1)} copy(bf16[5,1,64,64,128]{4,3,2,1,0:T(8,128)(2,1)} %param.14) | data formatting | bytes 10485760 | tf_op args[0]
  18.1 18.6 %fusion.711 = (bf16[5,2,64,128]{1,3,0,2:T(8,128)(2,1)}, bf16[5,2,64,128]{1,3,0,2:T(8,128)(2,1)}) fusion(bf16[5,64,64,128]{1,3,0,2:T(8,128)(2,1)} %bitcast.3019), kind=kLoop, calls=%fused_computation.1104 | loop fusion | bytes 655360 | tf_op jit(solution)/shard_map/slice | solution.py:21
  36.7 7.9 copy.127
  44.6 3.9 collective-permute-start
  48.5 8.6 copy.128
  120.6 26.1 %subtract_divide_fusion.41 = (f32[1,64]{1,0:T(1,128)S(1)}, f32[1,64]{1,0:T(1,128)S(1)}, f32[1,64]{1,0:T(1,128)S(1)}, f32[1,64]{1,0:T(1,128)S(1)}, f32[1,64]{1,0:...) fusion(f32[64,64]{1,0:T(8,128)S(1)} %fusion.240, ...), kind=kLoop, calls=%fused_computation.998 | loop fusion | flops 7872 | bytes 21576 | tf_op jit(solution)/shard_map/eval_jaxpr/div | solution.py:67
  174.0 40.1 %fusion.473 = (f32[1,64]{1,0:T(1,128)}, f32[64]{0:T(128)S(1)}, f32[64]{0:T(128)S(1)}, f32[64]{0:T(128)S(1)}, f32[64]{0:T(128)S(1)}, /*index=5*/f32[64]{0:T(128)S...) fusion(f32[]{:T(128)S(6)} %div.27446, ...), kind=kLoop, calls=%fused_computation.1062 | loop fusion | flops 12224 | bytes 27644 | tf_op jit(solution)/shard_map/while/body/broadcast_in_dim | solution.py:67
  214.1 39.3 %fusion.483 = (f32[1,64]{1,0:T(1,128)S(1)}, f32[64]{0:T(128)S(1)}, f32[64]{0:T(128)S(1)}, f32[64]{0:T(128)S(1)}, f32[64]{0:T(128)S(1)}, /*index=5*/f32[64]{0:T(1...) fusion(f32[]{:T(128)S(6)} %div.27446, ...), kind=kLoop, calls=%fused_computation.1072 | loop fusion | flops 12224 | bytes 27644 | tf_op jit(solution)/shard_map/while/body/broadcast_in_dim | solution.py:67
  258.6 13.8 %fusion.471 = (f32[1,64]{1,0:T(1,128)S(1)}, f32[64]{0:T(128)}) fusion(f32[64]{0:T(128)S(1)} %get-tuple-element.665, f32[64]{0:T(128)S(1)} %get-tuple-element.664, f32[64]{0:T(128)S(1)} %get-tuple-element.663, f32[64]{0:T(128)S(1)} %get-tuple-element.662, f32[64]{0:T(128)S(1)} %get-tuple-element.661, f32[64]{0:T(128)S(1)} %get-tuple-element.660, ...), kind=kLoop, calls=%fused_computation.1059 | loop fusion | flops 9600 | bytes 12628 | tf_op jit(solution)/shard_map/broadcast_in_dim | solution.py:67
  281.8 196.8 %while.40 = (s32[]{:T(128)}, f32[]{:T(128)}, f32[128]{0:T(128)S(1)}, f32[3,32]{1,0:T(4,128)S(1)}, f32[3,32,128]{2,1,0:T(8,128)S(1)}, /*index=5*/f32[3,32]{1,0:T(...) while((s32[]{:T(128)}, f32[]{:T(128)}, ...), condition=%wide.region_5.6_spmd, body=%wide.region_4.5_spmd.sunk | while | flops 12417 | bytes 103653 | solution.py:70
  325.1 20.2 %fusion.751 = (f32[128]{0:T(128)S(1)}, f32[128]{0:T(128)S(1)}, f32[128]{0:T(128)S(1)}, f32[128]{0:T(128)S(1)}, f32[128]{0:T(128)S(1)}, /*index=5*/f32[128]{0:T(1...) fusion(f32[3,32,128]{2,1,0:T(8,128)S(1)} %get-tuple-element.190, ...), kind=kLoop, calls=%fused_computation.40.clone.1 | loop fusion | flops 12288 | bytes 33664 | tf_op jit(solution)/shard_map/while/body/eval_jaxpr/div | solution.py:70
  390.7 20.2 %fusion.751 = (f32[128]{0:T(128)S(1)}, f32[128]{0:T(128)S(1)}, f32[128]{0:T(128)S(1)}, f32[128]{0:T(128)S(1)}, f32[128]{0:T(128)S(1)}, /*index=5*/f32[128]{0:T(1...) fusion(f32[3,32,128]{2,1,0:T(8,128)S(1)} %get-tuple-element.190, ...), kind=kLoop, calls=%fused_computation.40.clone.1 | loop fusion | flops 12288 | bytes 33664 | tf_op jit(solution)/shard_map/while/body/eval_jaxpr/div | solution.py:70
  456.3 20.2 %fusion.751 = (f32[128]{0:T(128)S(1)}, f32[128]{0:T(128)S(1)}, f32[128]{0:T(128)S(1)}, f32[128]{0:T(128)S(1)}, f32[128]{0:T(128)S(1)}, /*index=5*/f32[128]{0:T(1...) fusion(f32[3,32,128]{2,1,0:T(8,128)S(1)} %get-tuple-element.190, ...), kind=kLoop, calls=%fused_computation.40.clone.1 | loop fusion | flops 12288 | bytes 33664 | tf_op jit(solution)/shard_map/while/body/eval_jaxpr/div | solution.py:70
  522.5 19.2 %fusion.304 = (f32[128]{0:T(128)S(1)}, f32[128]{0:T(128)S(1)}, f32[128]{0:T(128)S(1)}, f32[128]{0:T(128)S(1)}, f32[128]{0:T(128)S(1)}, /*index=5*/f32[128]{0:T(1...) fusion(f32[128,128]{1,0:T(8,128)S(1)} %multiply_add_fusion, ...), kind=kLoop, calls=%fused_computation.516 | loop fusion | flops 11904 | bytes 32504 | tf_op jit(solution)/shard_map/eval_jaxpr/div | solution.py:70
  542.8 63.5 %while.41 = (s32[]{:T(128)}, f32[128]{0:T(128)S(1)}, f32[3,32,128]{2,1,0:T(8,128)S(1)}, f32[3,32,128]{2,1,0:T(8,128)S(1)}, f32[3,32]{1,0:T(4,128)S(1)}, /*index=...) while((s32[]{:T(128)}, f32[128]{0:T(128)S(1)}, ...), condition=%wide.region_7.8_spmd, body=%wide.region_6.7_spmd.sunk | while | flops 8226 | bytes 101333 | solution.py:70
  544.2 19.6 %fusion.754 = (f32[128]{0:T(128)S(1)}, f32[128]{0:T(128)S(1)}, f32[128]{0:T(128)S(1)}, f32[128]{0:T(128)S(1)}, f32[128]{0:T(128)S(1)}, /*index=5*/f32[128]{0:T(1...) fusion(f32[3,32,128]{2,1,0:T(8,128)S(1)} %get-tuple-element.201, ...), kind=kLoop, calls=%fused_computation.168.clone.1 | loop fusion | flops 8192 | bytes 33536 | tf_op jit(solution)/shard_map/while/body/eval_jaxpr/sub | solution.py:70
  565.4 19.6 %fusion.754 = (f32[128]{0:T(128)S(1)}, f32[128]{0:T(128)S(1)}, f32[128]{0:T(128)S(1)}, f32[128]{0:T(128)S(1)}, f32[128]{0:T(128)S(1)}, /*index=5*/f32[128]{0:T(1...) fusion(f32[3,32,128]{2,1,0:T(8,128)S(1)} %get-tuple-element.201, ...), kind=kLoop, calls=%fused_computation.168.clone.1 | loop fusion | flops 8192 | bytes 33536 | tf_op jit(solution)/shard_map/while/body/eval_jaxpr/sub | solution.py:70
  586.6 19.6 %fusion.754 = (f32[128]{0:T(128)S(1)}, f32[128]{0:T(128)S(1)}, f32[128]{0:T(128)S(1)}, f32[128]{0:T(128)S(1)}, f32[128]{0:T(128)S(1)}, /*index=5*/f32[128]{0:T(1...) fusion(f32[3,32,128]{2,1,0:T(8,128)S(1)} %get-tuple-element.201, ...), kind=kLoop, calls=%fused_computation.168.clone.1 | loop fusion | flops 8192 | bytes 33536 | tf_op jit(solution)/shard_map/while/body/eval_jaxpr/sub | solution.py:70
  610.3 2.7 fusion.506
  613.0 2.8 fusion.505
  615.8 2.7 fusion.504
  618.5 2.7 fusion.503
  621.1 2.7 fusion.502
  623.8 2.7 fusion.501
  626.5 2.6 fusion.500
  629.2 2.7 fusion.499
  631.9 2.8 fusion.498
  634.7 2.7 fusion.497
  637.4 2.6 fusion.496
  640.0 2.5 fusion.495
  642.5 2.6 fusion.494
  649.7 26.1 %subtract_divide_fusion = (f32[1,64]{1,0:T(1,128)S(1)}, f32[1,64]{1,0:T(1,128)S(1)}, f32[1,64]{1,0:T(1,128)S(1)}, f32[1,64]{1,0:T(1,128)S(1)}, f32[1,64]{1,0:T(1...) fusion(f32[64,64]{1,0:T(8,128)S(1)} %multiply_add_fusion.1, ...), kind=kLoop, calls=%fused_computation.895 | loop fusion | flops 7872 | bytes 21576 | tf_op jit(solution)/shard_map/eval_jaxpr/div | solution.py:67
  675.8 13.2 %fusion.472 = (f32[1,64]{1,0:T(1,128)S(1)}, f32[64]{0:T(128)S(1)}) fusion(f32[64]{0:T(128)S(1)} %get-tuple-element.810, f32[64]{0:T(128)S(1)} %get-tuple-element.809, f32[64]{0:T(128)S(1)} %get-tuple-element.808, f32[64]{0:T(128)S(1)} %get-tuple-element.807, f32[64]{0:T(128)S(1)} %get-tuple-element.806, f32[64]{0:T(128)S(1)} %get-tuple-element.805, ...), kind=kLoop, calls=%fused_computation.1060 | loop fusion | flops 9600 | bytes 12628 | tf_op jit(solution)/shard_map/broadcast_in_dim | solution.py:67
  689.0 13.5 %multiply_subtract_fusion.2 = (f32[1,64]{1,0:T(1,128)S(1)}, f32[1,64]{1,0:T(1,128)S(1)}, f32[1,64]{1,0:T(1,128)S(1)}, f32[1,64]{1,0:T(1,128)S(1)}, f32[1,64]{1,0...) fusion(f32[1,64]{1,0:T(1,128)S(1)} %get-tuple-element.911, ...), kind=kLoop, calls=%fused_computation.853 | loop fusion | flops 12160 | bytes 27304 | tf_op jit(solution)/shard_map/eval_jaxpr/sub | solution.py:67
  704.8 14.4 %multiply_subtract_fusion.64 = (f32[1,64]{1,0:T(1,128)}, f32[1,64]{1,0:T(1,128)}, f32[1,64]{1,0:T(1,128)}, f32[1,64]{1,0:T(1,128)}, f32[1,64]{1,0:T(1,128)}, /*i...) fusion(f32[1,64]{1,0:T(1,128)S(1)} %get-tuple-element.766, ...), kind=kLoop, calls=%fused_computation.956 | loop fusion | flops 12160 | bytes 27304 | tf_op jit(solution)/shard_map/eval_jaxpr/sub | solution.py:67
  719.5 8.9 fusion.167
  728.4 6.7 convolution_bitcast_fusion
  735.2 7.8 fusion.710
  744.1 13.9 %all-reduce.2 = (bf16[4]{0:T(256)(128)(2,1)}, bf16[4]{0:T(256)(128)(2,1)}) all-reduce(bf16[4]{0:T(256)(128)(2,1)S(1)} %dynamic-update-slice.1, bf16[4]{0:T(256)(128)(2,1)S(1)} %dynamic-update-slice), channel_id=1, replica_groups=mesh['blk'=32,'ax'=4] {'ax'}, use_global_device_ids=true, to_apply=%add.1 | all-reduce | flops 8 | bytes 32
  758.5 2.9 copy.132
  762.0 2.9 copy.151
  764.8 2.9 copy.152
  767.7 2.9 copy.161
  773.3 2.9 concatenate.63
  776.4 6.9 copy.129
  783.3 7.8 copy.130
  791.1 22.0 %maximum_convert_fusion = f32[5,68,64,128]{1,3,0,2:T(8,128)} fusion(bf16[5,2,64,128]{1,3,0,2:T(8,128)(2,1)} %copy.130, bf16[5,64,64,128]{1,3,0,2:T(8,128)(2,1)} %bitcast.3022, bf16[5,2,64,128]{1,3,0,2:T(8,128)(2,1)} %copy.129), kind=kLoop, calls=%fused_computation.241 | loop fusion | flops 16711680 | bytes 16711680 | tf_op jit(solution)/shard_map/convert_element_type | solution.py:127
  813.0 36.5 %fusion.163 = f32[5,64,64,128]{1,3,0,2:T(8,128)} fusion(f32[5,68,64,128]{1,3,0,2:T(8,128)} %maximum_convert_fusion), kind=kLoop, calls=%fused_computation.238 | loop fusion | flops 13107200 | bytes 52428800 | tf_op jit(solution)/shard_map/add | solution.py:129
  849.5 16.8 %copy.131 = f32[5,64,64,128]{3,2,1,0:T(8,128)} copy(f32[5,64,64,128]{1,3,0,2:T(8,128)} %fusion.163) | data formatting | bytes 20971520 | tf_op jit(solution)/shard_map/add | solution.py:129
  866.4 11.6 %reshape.2834 = f32[5,64,8192]{2,1,0:T(8,128)} reshape(f32[5,64,64,128]{3,2,1,0:T(8,128)} %copy.131) | data formatting | bytes 20971520 | tf_op jit(solution)/shard_map/reshape | solution.py:135
  878.0 12.0 %fusion.229 = f32[5,64,8192]{2,1,0:T(8,128)S(1)} fusion(f32[5,64,8192]{2,1,0:T(8,128)} %reshape.2834, f32[64,64]{1,0:T(8,128)S(1)} %concatenate.63), kind=kOutput, calls=%fused_computation.373 | convolution fusion | flops 2013265920 | bytes 20987904 | tf_op jit(solution)/shard_map/dot_general | solution.py:133
  890.0 6.1 copy.189
  897.8 12.4 %all-gather = bf16[20,1,64,128]{3,2,1,0:T(8,128)(2,1)S(1)} all-gather(bf16[5,1,64,128]{3,2,1,0:T(8,128)(2,1)S(1)} %fusion.227), channel_id=2, replica_groups=mesh['blk'=32,'ax'=4] {'ax'}, dimensions={0}, use_global_device_ids=true | all-gather | bytes 409600 | tf_op jit(solution)/shard_map/all_gather | solution.py:36
  910.2 5.3 while.42
  917.2 12.4 %all-gather.1 = bf16[20,64,128]{2,1,0:T(8,128)(2,1)S(1)} all-gather(bf16[5,64,128]{2,1,0:T(8,128)(2,1)S(1)} %fusion.235), channel_id=3, replica_groups=mesh['blk'=32,'ax'=4] {'ax'}, dimensions={0}, use_global_device_ids=true | all-gather | bytes 409600 | tf_op jit(solution)/shard_map/all_gather | solution.py:36
  929.6 5.6 while.43
  937.4 10.6 %multiply_subtract_fusion = f32[5,64,64,128]{3,2,1,0:T(8,128)} fusion(f32[64]{0:T(128)S(1)} %get-tuple-element.503, f32[5,64,128]{2,1,0:T(8,128)S(1)} %get-tuple-element.459, f32[64]{0:T(128)S(1)} %get-tuple-element.502, f32[5,64,128]{2,1,0:T(8,128)S(1)} %multiply_subtract_fusion.1, f32[5,64,64,128]{3,2,1,0:T(8,128)} %bitcast.3035), kind=kLoop, calls=%fused_computation.242 | loop fusion | flops 13107200 | bytes 21299712 | tf_op jit(solution)/shard_map/sub | solution.py:174
  948.1 10.6 %copy.141 = bf16[2560,1536]{1,0:T(8,128)(2,1)} copy(bf16[2560,1536]{0,1:T(8,128)(2,1)} %bitcast.3046) | data formatting | bytes 15728640 | tf_op jit(solution)/shard_map/dot_general | solution.py:206
  958.7 7.1 fusion.165
  971.4 10.1 bitcast_dynamic-update-slice_fusion.6
  982.4 10.5 %bitcast_dynamic-update-slice_fusion.5 = (bf16[5,64,64,128]{3,2,1,0:T(8,128)(2,1)}, f32[64,64,128]{2,1,0:T(8,128)}, f32[64,64,128]{2,1,0:T(8,128)}, f32[64,64,128]{2,1,0:T(8,128)}) fusion(bf16[5,64,64,128]{3,2,1,0:T(8,128)(2,1)} %get-tuple-element.620, f32[64,64,128]{2,1,0:T(8,128)} %get-tuple-element.623, f32[64,64,128]{2,1,0:T(8,128)} %bitcast.3038, ...), kind=kLoop, calls=%fused_computation.349 | loop fusion | flops 18350080 | bytes 37847424
  992.9 8.1 bitcast_dynamic-update-slice_fusion.4
  1001.1 7.8 bitcast_dynamic-update-slice_fusion.3
  1009.0 9.8 bitcast_dynamic-update-slice_fusion.2
  (348 shorter events, 72.9 us)
Async XLA Ops:
  6.5 941.5 %all-gather.4.cloned.1.call-start = ((), (), s32[]{:S(2)}) async-start(), calls=%async_computation | async-start | bytes 8110080 | tf_op jit(solution)/shard_map/all_gather | solution.py:198
  44.6 731.8 %collective-permute-start = (bf16[5,2,64,128]{3,2,1,0:T(8,128)(2,1)S(1)}, bf16[5,2,64,128]{3,2,1,0:T(8,128)(2,1)S(1)}, u32[]{:S(2)}, u32[]{:S(2)}) collective-permute-start(bf16[5,2,64,128]{3,2,1,0:T(8,128)(2,1)S(1)} %copy.127), channel_id=1, source_target_pairs={{0,1},{1,2},{2,3},{4,5},{5,6},{6,7},{8,9},{9,10},{10,11},{12,13},{... | collective-permute-start | bytes 491528 | tf_op jit(solution)/shard_map/ppermute | solution.py:24
  57.1 726.2 %collective-permute-start.1 = (bf16[5,2,64,128]{3,2,1,0:T(8,128)(2,1)}, bf16[5,2,64,128]{3,2,1,0:T(8,128)(2,1)}, u32[]{:S(2)}, u32[]{:S(2)}) collective-permute-start(bf16[5,2,64,128]{3,2,1,0:T(8,128)(2,1)} %copy.128), channel_id=1, source_target_pairs={{1,0},{2,1},{3,2},{5,4},{6,5},{7,6},{9,8},{10,9},{11,10},{13,12},{... | collective-permute-start | bytes 491528 | tf_op jit(solution)/shard_map/ppermute | solution.py:26
  255.2 24.1 %copy-start.8 = (f32[64]{0:T(128)}, f32[64]{0:T(128)S(1)}, u32[]{:S(2)}) copy-start(f32[64]{0:T(128)S(1)} %get-tuple-element.671) | copy-start | bytes 772
  255.8 2.8 copy-start.10
  257.0 24.7 %copy-start.14 = (f32[64]{0:T(128)}, f32[64]{0:T(128)S(1)}, u32[]{:S(2)}) copy-start(f32[64]{0:T(128)S(1)} %get-tuple-element.677) | copy-start | bytes 772
  257.5 24.2 %copy-start.16 = (f32[64]{0:T(128)}, f32[64]{0:T(128)S(1)}, u32[]{:S(2)}) copy-start(f32[64]{0:T(128)S(1)} %get-tuple-element.679) | copy-start | bytes 772
  258.0 23.8 %copy-start.18 = (f32[64]{0:T(128)}, f32[64]{0:T(128)S(1)}, u32[]{:S(2)}) copy-start(f32[64]{0:T(128)S(1)} %get-tuple-element.681) | copy-start | bytes 772
  478.6 130.5 %copy-start.2 = (f32[3,32,128]{2,1,0:T(8,128)}, f32[3,32,128]{2,1,0:T(8,128)S(1)}, u32[]{:S(2)}) copy-start(f32[3,32,128]{2,1,0:T(8,128)S(1)} %get-tuple-element.460) | copy-start | bytes 147460
  522.5 83.8 %copy-start.56 = (u32[128]{0:T(128)S(1)}, u32[128]{0:T(128)}, u32[]{:S(2)}) copy-start(u32[128]{0:T(128)} %constant.251) | copy-start | bytes 1540
  637.4 91.0 %slice-start.6 = ((s8[5242880]{0:T(1024)(128)(4,1)}), s8[1048576]{0:T(1024)(128)(4,1)S(1)}, s32[]{:S(2)}) async-start(s8[5242880]{0:T(1024)(128)(4,1)} %bitcast.3029), calls=%async_computation.7 | async-start | bytes 2097152
  719.5 8.9 slice-start.7
  770.7 2.3 copy-start.17
  770.7 2.3 copy-start.19
  770.7 2.3 copy-start.20
  770.7 2.3 copy-start.21
  770.7 2.3 copy-start.22
  770.7 2.3 copy-start.23
  770.7 2.3 copy-start.24
  770.7 2.3 copy-start.25
  770.7 2.3 copy-start.26
  770.7 2.3 copy-start.27
  770.8 2.3 copy-start.28
  770.8 2.3 copy-start.29
  770.8 2.3 copy-start.30
  770.8 2.3 copy-start.31
  770.8 2.3 copy-start.32
  770.8 2.3 copy-start.33
  770.8 2.3 copy-start.34
  770.8 2.3 copy-start.35
  770.8 2.3 copy-start.36
  770.8 2.3 copy-start.37
  770.9 2.3 copy-start.38
  770.9 2.3 copy-start.39
  770.9 2.3 copy-start.40
  770.9 2.3 copy-start.41
  770.9 2.3 copy-start.42
  770.9 2.3 copy-start.43
  770.9 2.3 copy-start.44
  770.9 2.3 copy-start.45
  770.9 2.3 copy-start.46
  770.9 2.3 copy-start.47
  771.0 2.3 copy-start.48
  771.0 2.3 copy-start.49
  771.0 2.3 copy-start.50
  771.0 2.3 copy-start.51
  771.0 2.3 copy-start.52
  890.0 20.2 %copy-start.58 = (bf16[4]{0:T(256)(128)(2,1)S(1)}, bf16[4]{0:T(256)(128)(2,1)}, u32[]{:S(2)}) copy-start(bf16[4]{0:T(256)(128)(2,1)} %get-tuple-element.551) | copy-start | bytes 28
  896.1 33.5 %copy-start.57 = (bf16[4]{0:T(256)(128)(2,1)S(1)}, bf16[4]{0:T(256)(128)(2,1)}, u32[]{:S(2)}) copy-start(bf16[4]{0:T(256)(128)(2,1)} %get-tuple-element.550) | copy-start | bytes 28
  958.7 7.1 copy-start.54
  958.7 7.1 copy-start.55
  971.3 10.1 slice-start
  971.3 10.1 slice-start.1
  971.3 10.8 %slice-start.2 = ((s8[10485760]{0:T(1024)(128)(4,1)}), s8[2097152]{0:T(1024)(128)(4,1)S(1)}, s32[]{:S(2)}) async-start(s8[10485760]{0:T(1024)(128)(4,1)} %bitcast.3023), calls=%async_computation.3 | async-start | bytes 4194304
  971.3 11.0 %copy-start.1 = (bf16[1,64,64,128]{3,2,1,0:T(8,128)(2,1)S(1)}, bf16[1,64,64,128]{3,2,1,0:T(8,128)(2,1)}, u32[]{:S(2)}) copy-start(bf16[1,64,64,128]{3,2,1,0:T(8,128)(2,1)} %param.15) | copy-start | bytes 3145732
  992.9 8.1 copy-start
  992.9 8.1 copy-start.3
  992.9 16.0 %slice-start.3 = ((s8[10485760]{0:T(1024)(128)(4,1)}), s8[4194304]{0:T(1024)(128)(4,1)S(1)}, s32[]{:S(2)}) async-start(s8[10485760]{0:T(1024)(128)(4,1)} %bitcast.3025), calls=%async_computation.4 | async-start | bytes 8388608
  992.9 16.0 %slice-start.4 = ((s8[10485760]{0:T(1024)(128)(4,1)}), s8[4194304]{0:T(1024)(128)(4,1)S(1)}, s32[]{:S(2)}) async-start(s8[10485760]{0:T(1024)(128)(4,1)} %bitcast.3025), calls=%async_computation.5 | async-start | bytes 8388608
  1001.0 7.9 slice-start.5
  1001.0 7.9 copy-start.4
  1001.1 7.9 copy-start.5
  1001.1 7.9 copy-start.6
  1001.1 7.9 copy-start.7
  (6 other events, 13.0 us)
Sparse Core Ops, SparseCore 0:
  62.7 55.4 all-gather.3
where the time goes:
time: 1050 us; the launch traced here: 1030 us
  other arithmetic  496 us (47%)
  local copies, waits for them, and re-layouts  180 us (17%)
  between operations  141 us (13%)
  loops' own time  130 us (12%)
  blocking collectives  38.6 us (4%)
  matrix products  34.7 us (3%)
    another operation x2, loops' own time, line_tables(): lax.linalg.tridiagonal_solve(sub_diag, middle, super_diag, stencil)  125 us
    broadcast_in_dim x21, other arithmetic, line_tables(): lax.linalg.tridiagonal_solve(sub_diag, middle, super_diag, jnp.eye(line_c...  112 us
    div x4, other arithmetic, line_tables(): lax.linalg.tridiagonal_solve(sub_diag, middle, super_diag, stencil)  79.9 us
    sub x3, other arithmetic, line_tables(): lax.linalg.tridiagonal_solve(sub_diag, middle, super_diag, stencil)  58.9 us
    div x2, other arithmetic, line_tables(): lax.linalg.tridiagonal_solve(sub_diag, middle, super_diag, jnp.eye(line_c...  52.1 us
    broadcast_in_dim x17, other arithmetic, line_tables(): lax.linalg.tridiagonal_solve(sub_diag, middle, super_diag, stencil)  40.5 us
    add x1, other arithmetic, body(): stencil_sum + far_coef * (padded[:, 4:local_cells + 4] - padded[:, 0:loca...  36.5 us
    unnamed x9, other arithmetic  36.4 us
  transfers between devices with their start and end apart: 3, of which 0 were waited for; matrix products, arithmetic and copies ran while one was open for 59% of the time, Pallas kernels for 0%

commit v1 on v0

v1 whole, which is shorter than its diff:
```python
import functools

import jax
import jax.numpy as jnp
import numpy as np
from jax import lax
from jax.experimental import pallas as pl
from jax.experimental.pallas import tpu as pltpu
from jax.sharding import PartitionSpec as P

PW = 8
ALPHA = 1.0 / 3.0
NEAR = 7.0 / 9.0
FAR = 1.0 / 36.0
HEAT = 1.4
PIVOT = (1.0 + np.sqrt(1.0 - 4.0 * ALPHA * ALPHA)) / 2.0
MULT = ALPHA / PIVOT
F32 = jnp.float32
BF16 = jnp.bfloat16
MIB = 1 << 20


def dense(n):
    eye = functools.partial(np.eye, n)
    left = eye() + ALPHA * (eye(k=1) + eye(k=-1))
    right = NEAR * (eye(k=1) - eye(k=-1)) + FAR * (eye(k=2) - eye(k=-2))
    return left, right


def split(table):
    high = table.astype(np.float32).astype(jnp.bfloat16)
    low = (table - high.astype(np.float64)).astype(jnp.bfloat16)
    return high, low


def lateral_tables(ny, nz):
    left, right = dense(ny)
    high, low = split(np.linalg.solve(left, right))
    along_y = np.concatenate([high, low], axis=1)
    left, right = dense(nz)
    high, low = split(np.linalg.solve(left, right).T)
    along_z = np.concatenate([high, low], axis=0)
    return along_y, along_z


def axial_tables(pieces, length):
    n = pieces * length
    left, right = dense(n)
    derivative = np.linalg.solve(left, right)
    rows = [np.arange(s * length, (s + 1) * length) for s in range(pieces)]
    edge = []
    for s in range(pieces):
        shifted = right[rows[s]].copy()
        for other in (np.arange(0, s * length), np.arange((s + 1) * length, n)):
            if other.size:
                gain = left[np.ix_(rows[s], other)] @ np.linalg.inv(left[np.ix_(other, other)])
                shifted -= gain @ right[other]
        edge.append(shifted)
    weights = np.zeros((pieces, 2 * length))
    scalars = np.zeros((pieces, 16))
    for s in range(pieces):
        own = rows[s]
        if s + 1 < pieces:
            weights[s, :length] = edge[s + 1][0, own]
        if s > 0:
            weights[s, length:] = edge[s - 1][-1, own]
        else:
            weights[s, length:] = -(1.0 - PIVOT) * derivative[0, own]
    unit = abs(edge[2][0, rows[0][-1]])
    for s in range(pieces):
        own = rows[s]
        if s + 2 < pieces:
            vector = edge[s + 2][0, own] / unit
            scalars[s, 0] = vector[0] / weights[s, 0]
            scalars[s, 2] = vector[-1] - scalars[s, 0] * weights[s, length - 1]
            rest = vector - scalars[s, 0] * weights[s, :length]
            rest[-1] = 0.0
        else:
            vector = edge[s - 2][-1, own] / unit
            scalars[s, 1] = vector[-1] / weights[s, -1]
            scalars[s, 3] = vector[0] - scalars[s, 1] * weights[s, length]
            rest = vector - scalars[s, 1] * weights[s, length:]
            rest[0] = 0.0
        assert np.abs(rest).max() < 1e-12
        if s > 0:
            scalars[s, 4] = edge[s][0, own[0]]
            scalars[s, 5] = edge[s][0, own[1]] - NEAR
        else:
            scalars[s, 6] = 1.0
            vector = -(1.0 - PIVOT) * derivative[0, rows[1]]
            scalars[s, 7] = vector[-1] / weights[1, -1]
            scalars[s, 8] = vector[0] - scalars[s, 7] * weights[1, length]
        if s + 1 < pieces:
            scalars[s, 9] = edge[s][-1, own[-1]]
            scalars[s, 10] = edge[s][-1, own[-2]] + NEAR
        scalars[s, 11] = unit if s >= 2 else 0.0
        scalars[s, 12] = unit if s < 2 else 0.0
        last = PIVOT - ALPHA * ALPHA / PIVOT if s + 1 < pieces else PIVOT
        scalars[s, 13] = (1.0 - PIVOT / last) / MULT
    return np.concatenate([weights, scalars], axis=1).astype(np.float32)


def lane_order():
    table = np.zeros((256, 256), np.float32)
    for pair in range(2):
        for x in range(64):
            table[128 * pair + 2 * x, 64 * pair + x] = 1.0
            table[128 * pair + (2 * x - 1) % 128, 128 + 64 * pair + x] = 1.0
    return table.astype(jnp.bfloat16)


def dot(a, b):
    return jnp.dot(a, b, preferred_element_type=F32)


def dot_nt(a, b):
    return lax.dot_general(a, b, (((1,), (1,)), ((), ())), preferred_element_type=F32)


def iota(shape, axis):
    return lax.broadcasted_iota(jnp.int32, shape, axis)


def split_two(value):
    high = value.astype(BF16)
    return high, (value - high.astype(F32)).astype(BF16)


def gather_kernel(
    fields, table, links, order, f_ref, send, right, left, far, face_y, face_z, keep_y, keep_z
):
    step = pl.program_id(0)
    place = lax.axis_index("ax")
    nx, ny, nz = f_ref.shape[2:]
    lane = iota((ny, nz), 1)

    def group(g, carry):
        to_right, to_left, columns = carry
        part = jnp.zeros((ny, nz), F32)
        for j in range(8):
            x = 8 * g + j
            tile = f_ref[0, 0, x].astype(F32)
            to_right = to_right + table[place, x] * tile
            to_left = to_left + table[place, nx + x] * tile
            turned = pltpu.roll(tile, 2 * j, 1) if j else tile
            part = jnp.where(((lane + 1 - 2 * j) & 127) < 2, turned, part)
        part = pltpu.roll(part, 16 * g, 1)
        columns = jnp.where(((lane + 1 - 16 * g) & 127) < 16, part, columns)
        return to_right, to_left, columns

    zero = jnp.zeros((ny, nz), F32)
    to_right, to_left, columns = lax.fori_loop(0, nx // 8, group, (zero, zero, zero))
    first = f_ref[0, 0, 0]
    last = f_ref[0, 0, nx - 1]
    right[0, 0] = last
    right[0, 1], right[0, 2] = split_two(to_right)
    left[0, 0] = first
    left[0, 1], left[0, 2] = split_two(to_left)
    base = 2 * nx
    far[0] = (
        table[place, base] * to_right
        + table[place, base + 1] * to_left
        + table[place, base + 2] * last.astype(F32)
        + table[place, base + 3] * first.astype(F32)
    ).astype(BF16)
    columns = columns.astype(BF16)
    face_z[0] = columns
    keep_z[step] = columns
    pick = iota((nx, 16 * nx), 1) - 16 * iota((nx, 16 * nx), 0)
    low = dot((pick == 0).astype(F32).astype(BF16), f_ref[0, 0, :, 0:16, :].reshape(16 * nx, nz))
    high = dot(
        (pick == 15).astype(F32).astype(BF16), f_ref[0, 0, :, ny - 16 : ny, :].reshape(16 * nx, nz)
    )
    faces = jnp.concatenate([low, high], axis=1).astype(BF16)
    face_y[0] = faces
    keep_y[step] = faces

    @pl.when(step == fields - 1)
    def _():
        own = lax.axis_index("blk")
        source = links[0]
        blocks, patches = source.shape
        hit = (source == own).astype(F32)
        before = (iota((patches, patches), 0) < iota((patches, patches), 1)).astype(F32)
        rank = dot(hit.astype(BF16), before.astype(BF16))
        face = links[1].astype(F32) + 1.0
        columns = []
        for c in range(2):
            chosen = jnp.where(rank == float(c), hit, 0.0) * face
            chosen = jnp.sum(chosen, axis=1, keepdims=True)
            columns.append(jnp.broadcast_to(chosen, (blocks, 128)))
        chosen = jnp.concatenate(columns, axis=0).astype(BF16)
        rows = 16 * blocks
        row = iota((rows, 2 * blocks), 0)
        slot = (row & 15) // 8 * blocks + row // 16
        spread = (slot == iota((rows, 2 * blocks), 1)).astype(F32).astype(BF16)
        chosen = dot(spread, chosen)
        cells = PW * patches
        target = (chosen.astype(jnp.int32) - 1) * PW + (iota((rows, 128), 0) & 7)
        target = jnp.concatenate([target] * (cells // 128), axis=1)
        chooser = (iota((rows, cells), 1) == target).astype(F32).astype(BF16)
        for pair in range((fields + 1) // 2):
            one = 2 * pair
            if one + 1 < fields:
                ys = jnp.concatenate([keep_y[one], keep_y[one + 1]], axis=0)
                zs = jnp.concatenate([keep_z[one], keep_z[one + 1]], axis=1)
            else:
                ys = jnp.concatenate([keep_y[one], jnp.zeros_like(keep_y[one])], axis=0)
                zs = jnp.concatenate([keep_z[one], jnp.zeros_like(keep_z[one])], axis=1)
            zs = dot(zs, order[...]).astype(BF16)
            zs = jnp.concatenate([zs[:, :128], zs[:, 128:]], axis=0)
            out = dot_nt(chooser[:, : 2 * nz], ys) + dot(chooser[:, 2 * nz :], zs)
            send[:, :, 128 * pair : 128 * pair + 128] = out.astype(BF16).reshape(blocks, 16, 128)


def flux(gradients, metric, density, velocity, pressure, sums):
    ka, kb, kc = metric
    speed = ka * velocity[0] + kb * velocity[1] + kc * velocity[2]
    coupled = density * gradients[0] + pressure * gradients[4]
    turned = ka * gradients[1] + kb * gradients[2] + kc * gradients[3]
    terms = [
        speed * gradients[0],
        speed * gradients[1] + ka * coupled,
        speed * gradients[2] + kb * coupled,
        speed * gradients[3] + kc * coupled,
        speed * gradients[4],
        turned,
    ]
    return terms if sums is None else [a + b for a, b in zip(sums, terms)]


def lateral_kernel(fields, along_y, along_z, f_ref, density, velocity, pressure, ky, kz, out):
    chunk, ny, nz = f_ref.shape[2:]

    def body(h, _):
        grads_y = []
        grads_z = []
        xs = (2 * h, 2 * h + 1)
        for f in range(fields):
            tiles = [f_ref[f, 0, x] for x in xs]
            rows = jnp.concatenate(tiles, axis=0)
            grads_z.append(dot(jnp.concatenate([rows, rows], axis=1), along_z[...]))
            wide = jnp.concatenate(tiles, axis=1)
            grads_y.append(dot(along_y[...], jnp.concatenate([wide, wide], axis=0)))
        for q, x in enumerate(xs):
            for y in range(0, ny, 16):
                at = slice(y, y + 16)
                rho = density[0, x, at, :].astype(F32)
                vel = [velocity[i, 0, x, at, :].astype(F32) for i in range(3)]
                press = HEAT * pressure[0, x, at, :].astype(F32)
                gy = [g[at, q * nz : (q + 1) * nz] for g in grads_y]
                gz = [g[q * ny + y : q * ny + y + 16] for g in grads_z]
                metric = [ky[i, 0, x, at, :].astype(F32) for i in range(3)]
                sums = flux(gy, metric, rho, vel, press, None)
                metric = [kz[i, 0, x, at, :].astype(F32) for i in range(3)]
                sums = flux(gz, metric, rho, vel, press, sums)
                for i in range(4):
                    out[i, x, at, :] = sums[i]
                out[4, x, at, :] = sums[4] + sums[5] / rho
        return 0

    lax.fori_loop(0, chunk // 2, body, 0)


def axial_kernel(
    fields,
    table,
    links,
    order,
    f_ref,
    density,
    velocity,
    pressure,
    kx,
    partial,
    received,
    right,
    left,
    far,
    own_left,
    face_y,
    face_z,
    out,
    line,
    pen_y,
    pen_z,
):
    step = pl.program_id(0)
    place = lax.axis_index("ax")
    nx, rows, nz = f_ref.shape[2:]
    ny = face_z.shape[1]

    @pl.when(step == 0)
    def _():
        own = lax.axis_index("blk")
        blocks, patches = links.shape[1:]
        cells = PW * patches
        source = links[0, pl.ds(own, 1), :]
        turn = links[2, pl.ds(own, 1), :]
        same = (patches, patches)
        wide = jnp.broadcast_to(source, same).astype(F32)
        tall = jnp.sum(
            jnp.where(iota(same, 0) == iota(same, 1), wide, 0.0), axis=1, keepdims=True
        )
        earlier = (iota(same, 0) < iota(same, 1)) & (wide == tall)
        slot = jnp.sum(earlier.astype(F32), axis=0, keepdims=True)
        live = (source >= 0).astype(F32)
        where = jnp.where(source >= 0, source.astype(F32) * 16.0 + slot * 8.0, -16.0)
        shape = (cells, patches)
        mine = (iota(shape, 0) // PW) == iota(shape, 1)

        def spread(value):
            value = jnp.where(mine, jnp.broadcast_to(value, shape), 0.0)
            return jnp.sum(value, axis=1, keepdims=True)

        cell = iota((cells, 1), 0) & 7
        cell = jnp.where(spread(turn.astype(F32)) > 0.5, 7 - cell, cell)
        target = spread(where).astype(jnp.int32) + cell
        slots = 16 * blocks
        chooser = (iota((cells, slots), 1) == target).astype(F32).astype(BF16)
        live_rows = spread(live)
        got = dot(chooser, received[...].reshape(slots, received.shape[2]))
        got_y = jnp.transpose(got[: 2 * nz])
        across = jnp.sum(
            jnp.where(
                iota((patches, 2 * nz), 0) == iota((patches, 2 * nz), 1) // PW,
                jnp.broadcast_to(
                    jnp.sum(
                        jnp.where(
                            iota(same, 0) == iota(same, 1), jnp.broadcast_to(live, same), 0.0
                        ),
                        axis=1,
                        keepdims=True,
                    ),
                    (patches, 2 * nz),
                ),
                0.0,
            ),
            axis=0,
            keepdims=True,
        )
        for f in range(fields):
            value = got_y[nx * f : nx * f + nx] - across * face_y[f].astype(F32)
            pen_y[0, nx * f : nx * f + nx, :] = value[:, :nz]
            pen_y[1, nx * f : nx * f + nx, :] = value[:, nz:]
        even = (iota((ny, 128), 1) & 1) == 0
        live_z = jnp.where(
            even, live_rows[2 * nz : 2 * nz + ny], live_rows[2 * nz + ny : 2 * nz + 2 * ny]
        )
        for pair in range((fields + 1) // 2):
            lanes = slice(128 * pair, 128 * pair + 128)
            both = jnp.concatenate(
                [got[2 * nz : 2 * nz + ny, lanes], got[2 * nz + ny :, lanes]], axis=1
            )
            both = dot_nt(both.astype(BF16), order[...])
            for q in range(2):
                f = 2 * pair + q
                if f < fields:
                    pen_z[f] = both[:, 128 * q : 128 * q + 128] - live_z * face_z[f].astype(F32)

    base = 2 * nx

    def scalar(i):
        return table[place, base + i]

    inverse = 1.0 / PIVOT
    near = NEAR * inverse
    far_coef = FAR * inverse

    def load(f, x):
        return f_ref[f, 0, x].astype(F32)

    def edges(f):
        right_fn = right[f, 1].astype(F32) + right[f, 2].astype(F32)
        left_fn = left[f, 1].astype(F32) + left[f, 2].astype(F32)
        own_fn = own_left[f, 1].astype(F32) + own_left[f, 2].astype(F32)
        right_last = right[f, 0].astype(F32)
        left_first = left[f, 0].astype(F32)
        far_plane = far[f].astype(F32)
        low = (
            right_fn
            + scalar(4) * load(f, 0)
            + scalar(5) * load(f, 1)
            + scalar(6) * own_fn
            + scalar(7) * left_fn
            + scalar(8) * left_first
            + scalar(11) * far_plane
        )
        high = (
            left_fn
            + scalar(9) * load(f, nx - 1)
            + scalar(10) * load(f, nx - 2)
            + scalar(12) * far_plane
        )
        return (
            low * inverse,
            -far_coef * right_last,
            far_coef * left_first,
            high * inverse,
        )

    for members in ((0, 1, 2), (3, 4)):
        edge = [edges(f) for f in members]
        state = []
        for q, f in enumerate(members):
            f0, f1, f2, f3 = [load(f, x) for x in range(4)]
            d0 = near * f1 + far_coef * f2 + edge[q][0]
            d1 = near * (f2 - f0) + far_coef * f3 + edge[q][1] - MULT * d0
            line[0, f] = d0
            line[1, f] = d1
            state.append((f0, f1, f2, f3, d1))

        def forward(x, state):
            new = []
            for q, f in enumerate(members):
                fm2, fm1, f0, fp1, d = state[q]
                fp2 = load(f, x + 2)
                d = (near * (fp1 - fm1) + far_coef * (fp2 - fm2)) - MULT * d
                line[x, f] = d
                new.append((fm1, f0, fp1, fp2, d))
            return tuple(new)

        state = lax.fori_loop(2, nx - 2, forward, tuple(state), unroll=4)
        for q, f in enumerate(members):
            fm2, fm1, f0, fp1, d = state[q]
            d = near * (fp1 - fm1) - far_coef * fm2 + edge[q][2] - MULT * d
            line[nx - 2, f] = d
            d = -near * f0 - far_coef * fm1 + edge[q][3] - MULT * d
            line[nx - 1, f] = d

    lane = iota((rows, nz), 1)
    at_z = ((lane + 1) & 127) < 2
    row = iota((rows, nz), 0)
    last_step = pl.num_programs(0) - 1
    at_y = ((row == 0) & (step == 0)) | ((row == rows - 1) & (step == last_step))
    side = (step == last_step).astype(jnp.int32)
    y_at = pl.multiple_of(step * rows, rows)

    def backward(k, g):
        x = nx - 1 - k
        g = [line[x, f] - MULT * g[f] for f in range(fields)]
        rho = density[0, x].astype(F32)
        vel = [velocity[i, 0, x].astype(F32) for i in range(3)]
        press = HEAT * pressure[0, x].astype(F32)
        metric = [kx[i, 0, x].astype(F32) for i in range(3)]
        sums = flux(g, metric, rho, vel, press, None)
        sums[4] = sums[4] + sums[5] / rho
        for f in range(fields):
            total = sums[f] + partial[f, x]
            total = total + jnp.where(at_y, pen_y[side, pl.ds(f * nx + x, 1), :], 0.0)
            turned = pltpu.roll(pen_z[f, pl.ds(y_at, rows), :], (128 - 2 * x) & 127, 1)
            total = total + jnp.where(at_z, turned, 0.0)
            out[f, 0, x] = total.astype(BF16)
        return g

    start = [scalar(13) * line[nx - 1, f] for f in range(fields)]
    lax.fori_loop(0, nx, backward, start, unroll=2)


def in_hbm(*arrays):
    return [pltpu.with_memory_space_constraint(a, pltpu.HBM) for a in arrays]


def whole(shape):
    return pl.BlockSpec(shape, lambda *_: (0,) * len(shape))


def body(tables, adjoint, density, velocity, pressure, metrics, links):
    fields, _, nx, ny, nz = adjoint.shape
    blocks, patches = links.shape[1:]
    along_y, along_z, axial, order = [jnp.asarray(t) for t in tables]
    smem = pl.BlockSpec(memory_space=pltpu.SMEM)
    lanes = 128 * ((fields + 1) // 2)
    shape = jax.ShapeDtypeStruct
    send, right, left, far, face_y, face_z = pl.pallas_call(
        functools.partial(gather_kernel, fields),
        grid=(fields,),
        in_specs=[
            smem,
            whole(links.shape),
            whole(order.shape),
            pl.BlockSpec((1, 1, nx, ny, nz), lambda i: (i, 0, 0, 0, 0)),
        ],
        out_specs=[
            whole((blocks, 16, lanes)),
            pl.BlockSpec((1, 3, ny, nz), lambda i: (i, 0, 0, 0)),
            pl.BlockSpec((1, 3, ny, nz), lambda i: (i, 0, 0, 0)),
            pl.BlockSpec((1, ny, nz), lambda i: (i, 0, 0)),
            pl.BlockSpec((1, nx, 2 * nz), lambda i: (i, 0, 0)),
            pl.BlockSpec((1, ny, 128), lambda i: (i, 0, 0)),
        ],
        out_shape=[
            shape((blocks, 16, lanes), BF16),
            shape((fields, 3, ny, nz), BF16),
            shape((fields, 3, ny, nz), BF16),
            shape((fields, ny, nz), BF16),
            shape((fields, nx, 2 * nz), BF16),
            shape((fields, ny, 128), BF16),
        ],
        scratch_shapes=[
            pltpu.VMEM((fields, nx, 2 * nz), BF16),
            pltpu.VMEM((fields, ny, 128), BF16),
        ],
        compiler_params=pltpu.CompilerParams(vmem_limit_bytes=16 * MIB),
        cost_estimate=pl.CostEstimate(flops=10**9, bytes_accessed=7 * 10**6, transcendentals=0),
    )(axial, *in_hbm(links, order, adjoint))
    received = lax.all_to_all(send, "blk", 0, 0)
    pieces = lax.axis_size("ax")
    from_left = lax.ppermute(right, "ax", [(i, i + 1) for i in range(pieces - 1)])
    from_right = lax.ppermute(left, "ax", [(i + 1, i) for i in range(pieces - 1)])
    from_far = lax.ppermute(far, "ax", [(i, (i + 2) % pieces) for i in range(pieces)])

    chunk = 8
    flow = [
        pl.BlockSpec((fields, 1, chunk, ny, nz), lambda i: (0, 0, i, 0, 0)),
        pl.BlockSpec((1, chunk, ny, nz), lambda i: (0, i, 0, 0)),
        pl.BlockSpec((3, 1, chunk, ny, nz), lambda i: (0, 0, i, 0, 0)),
        pl.BlockSpec((1, chunk, ny, nz), lambda i: (0, i, 0, 0)),
    ]
    partial = pl.pallas_call(
        functools.partial(lateral_kernel, fields),
        grid=(nx // chunk,),
        in_specs=[whole(along_y.shape), whole(along_z.shape)]
        + flow
        + [
            pl.BlockSpec((3, 1, chunk, ny, nz), lambda i: (1, 0, i, 0, 0)),
            pl.BlockSpec((3, 1, chunk, ny, nz), lambda i: (2, 0, i, 0, 0)),
        ],
        out_specs=pl.BlockSpec((fields, chunk, ny, nz), lambda i: (0, i, 0, 0)),
        out_shape=pltpu.VMEM((fields, nx, ny, nz), F32),
        compiler_params=pltpu.CompilerParams(vmem_limit_bytes=16 * MIB),
        cost_estimate=pl.CostEstimate(
            flops=10**10, bytes_accessed=27 * 10**6, transcendentals=0
        ),
    )(*in_hbm(along_y, along_z, adjoint, density, velocity, pressure, metrics, metrics))

    rows = 16
    return pl.pallas_call(
        functools.partial(axial_kernel, fields),
        grid=(ny // rows,),
        in_specs=[
            smem,
            whole(links.shape),
            whole(order.shape),
            pl.BlockSpec((fields, 1, nx, rows, nz), lambda i: (0, 0, 0, i, 0)),
            pl.BlockSpec((1, nx, rows, nz), lambda i: (0, 0, i, 0)),
            pl.BlockSpec((3, 1, nx, rows, nz), lambda i: (0, 0, 0, i, 0)),
            pl.BlockSpec((1, nx, rows, nz), lambda i: (0, 0, i, 0)),
            pl.BlockSpec((3, 1, nx, rows, nz), lambda i: (0, 0, 0, i, 0)),
            pl.BlockSpec((fields, nx, rows, nz), lambda i: (0, 0, i, 0)),
            whole(received.shape),
            pl.BlockSpec((fields, 3, rows, nz), lambda i: (0, 0, i, 0)),
            pl.BlockSpec((fields, 3, rows, nz), lambda i: (0, 0, i, 0)),
            pl.BlockSpec((fields, rows, nz), lambda i: (0, i, 0)),
            pl.BlockSpec((fields, 3, rows, nz), lambda i: (0, 0, i, 0)),
            whole(face_y.shape),
            whole(face_z.shape),
        ],
        out_specs=pl.BlockSpec((fields, 1, nx, rows, nz), lambda i: (0, 0, 0, i, 0)),
        out_shape=shape(adjoint.shape, BF16),
        scratch_shapes=[
            pltpu.VMEM((nx, fields, rows, nz), F32),
            pltpu.VMEM((2, fields * nx, nz), F32),
            pltpu.VMEM((fields, ny, 128), F32),
        ],
        compiler_params=pltpu.CompilerParams(vmem_limit_bytes=30 * MIB),
        cost_estimate=pl.CostEstimate(
            flops=10**10, bytes_accessed=30 * 10**6, transcendentals=0
        ),
    )(
        axial,
        *in_hbm(links, order, adjoint, density, velocity, pressure, metrics),
        pltpu.with_memory_space_constraint(partial, pltpu.VMEM),
        *in_hbm(received, from_left, from_right, from_far, left, face_y, face_z),
    )


def solution(mesh):
    in_specs = (
        P(None, "blk", "ax", None, None),
        P("blk", "ax", None, None),
        P(None, "blk", "ax", None, None),
        P("blk", "ax", None, None),
        P(None, "blk", "ax", None, None),
        P(),
    )
    out_specs = P(None, "blk", "ax", None, None)

    def run(*args):
        pieces = mesh.shape["ax"]
        nx, ny, nz = args[0].shape[2:]
        tables = (*lateral_tables(ny, nz), axial_tables(pieces, nx // pieces), lane_order())
        return jax.shard_map(
            functools.partial(body, tables),
            mesh=mesh,
            in_specs=in_specs,
            out_specs=out_specs,
            check_vma=False,
        )(*args)

    return run
```

time: 1050 us -> 73.1 us (0.07)
  the two profiles are of different devices: /device:TPU:0 before, /device:TPU:1 now
where the time goes in v1:
time: 73.1 us; the launch traced here: 72.2 us
  Pallas kernels  45 us (62%)
  starting transfers between devices  16.2 us (22%)
  local copies, waits for them, and re-layouts  10.9 us (15%)
    pallas_call x1, Pallas kernels, body(): pl.pallas_call(functools.partial(axial_kernel, fields), grid=(ny // rows,...  20.5 us
    pallas_call x1, Pallas kernels, body(): pl.pallas_call(functools.partial(lateral_kernel, fields), grid=(nx // chu...  13.2 us
    pallas_call x1, Pallas kernels, body(): pl.pallas_call(functools.partial(gather_kernel, fields), grid=(fields,),...  11.3 us
    unnamed x22, local copies, waits for them, and re-layouts  10.9 us
    all_to_all x1, starting transfers between devices, body(): received = lax.all_to_all(send, 'blk', 0, 0)  8.59 us
    ppermute x1, starting transfers between devices, body(): lax.ppermute(far, 'ax', [(i, (i + 2) % pieces) for i in range(pieces)])  3.67 us
    ppermute x1, starting transfers between devices, body(): lax.ppermute(right, 'ax', [(i, i + 1) for i in range(pieces - 1)])  2.65 us
  transfers between devices with their start and end apart: 4, of which 0 were waited for; matrix products, arithmetic and copies ran while one was open for 0% of the time, Pallas kernels for 18%

profile of v1, /device:TPU:1, one launch (start us, length us, event | category | flops | bytes accessed | tf_op | source)
XLA Modules:
  0.0 72.2 jit_solution(6713512820064790493)
XLA Ops:
  0.0 0.0 copy-start.5
  0.0 0.7 copy-done.5
  0.7 11.3 %shard_map.101 = (bf16[32,16,384]{2,1,0:T(8,128)(2,1)}, bf16[5,3,64,128]{3,2,1,0:T(8,128)(2,1)S(1)}, bf16[5,3,64,128]{3,2,1,0:T(8,128)(2,1)S(1)}, bf16[5,64,128]...) custom-call(f32[4,144]{1,0:T(4,128)S(1)} %copy-done.5, s32[3,32,48]{2,1,0:T(8,128)} %links.3, ...), custom_call_target="tpu_custom_call" | custom-call | flops 1000000000 | bytes 7000000 | tf_op jit(solution)/shard_map/pallas_call | solution.py:475
  12.0 0.0 copy-start.3
  12.0 0.7 copy-done.3
  12.7 0.0 copy-start.4
  12.7 0.6 copy-done.4
  13.3 0.0 copy-start.2
  13.3 8.6 %all-to-all-start = ((bf16[32,16,384]{2,1,0:T(8,128)(2,1)}), bf16[32,16,384]{2,1,0:T(8,128)(2,1)S(1)}, u32[]{:S(2)}, u32[]{:S(2)}) async-start(bf16[32,16,384]{2,1,0:T(8,128)(2,1)} %get-tuple-element.11), calls=%async_computation | async-start | bytes 786432 | tf_op jit(solution)/shard_map/all_to_all | solution.py:507
  21.9 3.7 %collective-permute-start.2 = (bf16[5,64,128]{2,1,0:T(8,128)(2,1)S(1)}, bf16[5,64,128]{2,1,0:T(8,128)(2,1)S(1)}, u32[]{:S(2)}, u32[]{:S(2)}) collective-permute-start(bf16[5,64,128]{2,1,0:T(8,128)(2,1)S(1)} %get-tuple-element.14), channel_id=1, source_target_pairs={{0,2},{1,3},{2,0},{3,1},{4,6},{5,7},{6,4},{7,5},{8,10},{9,11},{10,... | collective-permute-start | bytes 245768 | tf_op jit(solution)/shard_map/ppermute | solution.py:511
  25.6 2.6 %collective-permute-start = (bf16[5,3,64,128]{3,2,1,0:T(8,128)(2,1)S(1)}, bf16[5,3,64,128]{3,2,1,0:T(8,128)(2,1)S(1)}, u32[]{:S(2)}, u32[]{:S(2)}) collective-permute-start(bf16[5,3,64,128]{3,2,1,0:T(8,128)(2,1)S(1)} %get-tuple-element.12), channel_id=1, source_target_pairs={{0,1},{1,2},{2,3},{4,5},{5,6},{6,7},{8,9},{9,10},{10,11},{12,13},{... | collective-permute-start | bytes 737288 | tf_op jit(solution)/shard_map/ppermute | solution.py:509
  28.3 0.0 copy-start.6
  28.3 1.3 %collective-permute-start.1 = (bf16[5,3,64,128]{3,2,1,0:T(8,128)(2,1)S(1)}, bf16[5,3,64,128]{3,2,1,0:T(8,128)(2,1)S(1)}, u32[]{:S(2)}, u32[]{:S(2)}) collective-permute-start(bf16[5,3,64,128]{3,2,1,0:T(8,128)(2,1)S(1)} %get-tuple-element.13.own_left), channel_id=1, source_target_pairs={{1,0},{2,1},{3,2},{5,4},{6,5},{7,6},{9,8},{10,9},{11,10},{13,12},{... | collective-permute-start | bytes 737288 | tf_op jit(solution)/shard_map/ppermute | solution.py:510
  29.6 13.2 %shard_map.100.partial = f32[5,64,64,128]{3,2,1,0:T(8,128)S(1)} custom-call(bf16[64,128]{1,0:T(8,128)(2,1)} %constant.8.clone.along_y, bf16[256,128]{1,0:T(8,128)(2,1)} %constant.9.clone.along_z, bf16[5,1,64,64,128]{4,3,2,1,0:T(8,128)(2,1)} %f_ref.5, bf16[1,64,64,128]{3,2,1,0:T(8,128)(2,1)} %density.3, bf16[3,1,64,64,128]{4,3,2,1,0:T(8,128)(2,1)} %velocity.3, ...), custom_call_target="tpu_custom_call" | custom-call | flops 10000000000 | bytes 27000000 | tf_op jit(solution)/shard_map/pallas_call | solution.py:520
  42.8 0.0 copy-done.2
  42.8 0.0 copy-start
  42.8 4.0 %copy-done = f32[5,64,64,128]{3,2,1,0:T(8,128)} copy-done((f32[5,64,64,128]{3,2,1,0:T(8,128)}, f32[5,64,64,128]{3,2,1,0:T(8,128)S(1)}, u32[]{:S(2)}) %copy-start) | copy-done | bytes 10485784
  46.8 0.0 collective-permute-done.2.far
  46.8 0.0 copy-start.10
  46.8 0.0 collective-permute-done.right
  46.8 0.0 copy-start.8
  46.8 0.0 collective-permute-done.1.left
  46.8 0.0 copy-start.9
  46.8 0.0 all-to-all-done.received
  46.8 0.0 copy-start.7
  46.9 0.6 copy-done.10
  47.4 0.1 copy-done.8
  47.5 0.1 copy-done.9
  47.6 0.2 copy-done.7
  47.8 0.0 copy-done.6
  47.8 0.0 copy-start.1
  47.8 4.0 %copy-done.1 = f32[5,64,64,128]{3,2,1,0:T(8,128)S(1)} copy-done((f32[5,64,64,128]{3,2,1,0:T(8,128)S(1)}, f32[5,64,64,128]{3,2,1,0:T(8,128)}, u32[]{:S(2)}) %copy-start.1) | copy-done | bytes 10485784
  51.8 20.5 %shard_map.102 = bf16[5,1,64,64,128]{4,3,2,1,0:T(8,128)(2,1)} custom-call(f32[4,144]{1,0:T(4,128)S(1)} %copy-done.6, s32[3,32,48]{2,1,0:T(8,128)} %links.3, bf16[256,256]{1,0:T(8,128)(2,1)} %constant.11.clone.order, bf16[5,1,64,64,128]{4,3,2,1,0:T(8,128)(2,1)} %f_ref.5, bf16[1,64,64,128]{3,2,1,0:T(8,128)(2,1)} %density.3, ...), custom_call_target="tpu_custom_call" | custom-call | flops 10000000000 | bytes 30000000 | tf_op jit(solution)/shard_map/pallas_call | solution.py:538
Async XLA Ops:
  0.0 0.7 copy-start.5
  12.0 0.7 copy-start.3
  12.7 0.6 copy-start.4
  13.3 29.5 %copy-start.2 = (bf16[5,3,64,128]{3,2,1,0:T(8,128)(2,1)}, bf16[5,3,64,128]{3,2,1,0:T(8,128)(2,1)S(1)}, u32[]{:S(2)}) copy-start(bf16[5,3,64,128]{3,2,1,0:T(8,128)(2,1)S(1)} %get-tuple-element.13.own_left) | copy-start | bytes 737284
  13.3 33.5 %all-to-all-start = ((bf16[32,16,384]{2,1,0:T(8,128)(2,1)}), bf16[32,16,384]{2,1,0:T(8,128)(2,1)S(1)}, u32[]{:S(2)}, u32[]{:S(2)}) async-start(bf16[32,16,384]{2,1,0:T(8,128)(2,1)} %get-tuple-element.11), calls=%async_computation | async-start | bytes 786432 | tf_op jit(solution)/shard_map/all_to_all | solution.py:507
  21.9 24.9 %collective-permute-start.2 = (bf16[5,64,128]{2,1,0:T(8,128)(2,1)S(1)}, bf16[5,64,128]{2,1,0:T(8,128)(2,1)S(1)}, u32[]{:S(2)}, u32[]{:S(2)}) collective-permute-start(bf16[5,64,128]{2,1,0:T(8,128)(2,1)S(1)} %get-tuple-element.14), channel_id=1, source_target_pairs={{0,2},{1,3},{2,0},{3,1},{4,6},{5,7},{6,4},{7,5},{8,10},{9,11},{10,... | collective-permute-start | bytes 245768 | tf_op jit(solution)/shard_map/ppermute | solution.py:511
  25.6 21.2 %collective-permute-start = (bf16[5,3,64,128]{3,2,1,0:T(8,128)(2,1)S(1)}, bf16[5,3,64,128]{3,2,1,0:T(8,128)(2,1)S(1)}, u32[]{:S(2)}, u32[]{:S(2)}) collective-permute-start(bf16[5,3,64,128]{3,2,1,0:T(8,128)(2,1)S(1)} %get-tuple-element.12), channel_id=1, source_target_pairs={{0,1},{1,2},{2,3},{4,5},{5,6},{6,7},{8,9},{9,10},{10,11},{12,13},{... | collective-permute-start | bytes 737288 | tf_op jit(solution)/shard_map/ppermute | solution.py:509
  28.3 19.5 %copy-start.6 = (f32[4,144]{1,0:T(4,128)S(1)}, f32[4,144]{1,0:T(4,128)}, u32[]{:S(2)}) copy-start(f32[4,144]{1,0:T(4,128)} %constant.10.clone.table) | copy-start | bytes 6916
  28.3 18.5 %collective-permute-start.1 = (bf16[5,3,64,128]{3,2,1,0:T(8,128)(2,1)S(1)}, bf16[5,3,64,128]{3,2,1,0:T(8,128)(2,1)S(1)}, u32[]{:S(2)}, u32[]{:S(2)}) collective-permute-start(bf16[5,3,64,128]{3,2,1,0:T(8,128)(2,1)S(1)} %get-tuple-element.13.own_left), channel_id=1, source_target_pairs={{1,0},{2,1},{3,2},{5,4},{6,5},{7,6},{9,8},{10,9},{11,10},{13,12},{... | collective-permute-start | bytes 737288 | tf_op jit(solution)/shard_map/ppermute | solution.py:510
  42.8 4.0 %copy-start = (f32[5,64,64,128]{3,2,1,0:T(8,128)}, f32[5,64,64,128]{3,2,1,0:T(8,128)S(1)}, u32[]{:S(2)}) copy-start(f32[5,64,64,128]{3,2,1,0:T(8,128)S(1)} %shard_map.100.partial) | copy-start | bytes 31457284
  46.8 0.6 copy-start.10
  46.8 0.7 %copy-start.8 = (bf16[5,3,64,128]{3,2,1,0:T(8,128)(2,1)}, bf16[5,3,64,128]{3,2,1,0:T(8,128)(2,1)S(1)}, u32[]{:S(2)}) copy-start(bf16[5,3,64,128]{3,2,1,0:T(8,128)(2,1)S(1)} %collective-permute-done.right) | copy-start | bytes 737284
  46.8 0.8 %copy-start.9 = (bf16[5,3,64,128]{3,2,1,0:T(8,128)(2,1)}, bf16[5,3,64,128]{3,2,1,0:T(8,128)(2,1)S(1)}, u32[]{:S(2)}) copy-start(bf16[5,3,64,128]{3,2,1,0:T(8,128)(2,1)S(1)} %collective-permute-done.1.left) | copy-start | bytes 737284
  46.8 0.9 %copy-start.7 = (bf16[32,16,384]{2,1,0:T(8,128)(2,1)}, bf16[32,16,384]{2,1,0:T(8,128)(2,1)S(1)}, u32[]{:S(2)}) copy-start(bf16[32,16,384]{2,1,0:T(8,128)(2,1)S(1)} %all-to-all-done.received) | copy-start | bytes 1179652
  47.8 4.0 %copy-start.1 = (f32[5,64,64,128]{3,2,1,0:T(8,128)S(1)}, f32[5,64,64,128]{3,2,1,0:T(8,128)}, u32[]{:S(2)}) copy-start(f32[5,64,64,128]{3,2,1,0:T(8,128)} %copy-done) | copy-start | bytes 31457284

commit v2 on v1

v2 whole, which is shorter than its diff:
```python
import functools

import jax
import jax.numpy as jnp
import numpy as np
from jax import lax
from jax.experimental import pallas as pl
from jax.experimental.pallas import tpu as pltpu
from jax.sharding import PartitionSpec as P

PW = 8
ALPHA = 1.0 / 3.0
NEAR = 7.0 / 9.0
FAR = 1.0 / 36.0
HEAT = 1.4
PIVOT = (1.0 + np.sqrt(1.0 - 4.0 * ALPHA * ALPHA)) / 2.0
MULT = ALPHA / PIVOT
F32 = jnp.float32
BF16 = jnp.bfloat16
MIB = 1 << 20


def dense(n):
    eye = functools.partial(np.eye, n)
    left = eye() + ALPHA * (eye(k=1) + eye(k=-1))
    right = NEAR * (eye(k=1) - eye(k=-1)) + FAR * (eye(k=2) - eye(k=-2))
    return left, right


def split(table):
    high = table.astype(np.float32).astype(jnp.bfloat16)
    low = (table - high.astype(np.float64)).astype(jnp.bfloat16)
    return high, low


def lateral_tables(ny, nz):
    left, right = dense(ny)
    high, low = split(np.linalg.solve(left, right))
    along_y = np.concatenate([high, low], axis=1)
    left, right = dense(nz)
    high, low = split(np.linalg.solve(left, right).T)
    along_z = np.concatenate([high, low], axis=0)
    return along_y, along_z


def axial_tables(pieces, length):
    n = pieces * length
    left, right = dense(n)
    derivative = np.linalg.solve(left, right)
    rows = [np.arange(s * length, (s + 1) * length) for s in range(pieces)]
    edge = []
    for s in range(pieces):
        shifted = right[rows[s]].copy()
        for other in (np.arange(0, s * length), np.arange((s + 1) * length, n)):
            if other.size:
                gain = left[np.ix_(rows[s], other)] @ np.linalg.inv(left[np.ix_(other, other)])
                shifted -= gain @ right[other]
        edge.append(shifted)
    weights = np.zeros((pieces, 2 * length))
    scalars = np.zeros((pieces, 16))
    for s in range(pieces):
        own = rows[s]
        if s + 1 < pieces:
            weights[s, :length] = edge[s + 1][0, own]
        if s > 0:
            weights[s, length:] = edge[s - 1][-1, own]
        else:
            weights[s, length:] = -(1.0 - PIVOT) * derivative[0, own]
    unit = abs(edge[2][0, rows[0][-1]])
    for s in range(pieces):
        own = rows[s]
        if s + 2 < pieces:
            vector = edge[s + 2][0, own] / unit
            scalars[s, 0] = vector[0] / weights[s, 0]
            scalars[s, 2] = vector[-1] - scalars[s, 0] * weights[s, length - 1]
            rest = vector - scalars[s, 0] * weights[s, :length]
            rest[-1] = 0.0
        else:
            vector = edge[s - 2][-1, own] / unit
            scalars[s, 1] = vector[-1] / weights[s, -1]
            scalars[s, 3] = vector[0] - scalars[s, 1] * weights[s, length]
            rest = vector - scalars[s, 1] * weights[s, length:]
            rest[0] = 0.0
        assert np.abs(rest).max() < 1e-12
        if s > 0:
            scalars[s, 4] = edge[s][0, own[0]]
            scalars[s, 5] = edge[s][0, own[1]] - NEAR
        else:
            scalars[s, 6] = 1.0
            vector = -(1.0 - PIVOT) * derivative[0, rows[1]]
            scalars[s, 7] = vector[-1] / weights[1, -1]
            scalars[s, 8] = vector[0] - scalars[s, 7] * weights[1, length]
        if s + 1 < pieces:
            scalars[s, 9] = edge[s][-1, own[-1]]
            scalars[s, 10] = edge[s][-1, own[-2]] + NEAR
        scalars[s, 11] = unit if s >= 2 else 0.0
        scalars[s, 12] = unit if s < 2 else 0.0
        last = PIVOT - ALPHA * ALPHA / PIVOT if s + 1 < pieces else PIVOT
        scalars[s, 13] = (1.0 - PIVOT / last) / MULT
    return np.concatenate([weights, scalars], axis=1).astype(np.float32)


def lane_order():
    table = np.zeros((256, 256), np.float32)
    for pair in range(2):
        for x in range(64):
            table[128 * pair + 2 * x, 64 * pair + x] = 1.0
            table[128 * pair + (2 * x - 1) % 128, 128 + 64 * pair + x] = 1.0
    return table.astype(jnp.bfloat16)


def end_table(nz):
    table = np.zeros((256, nz), np.float32)
    for half, sign in ((0, 1.0), (128, -1.0)):
        table[half : half + 128 : 2, 0] = sign
        table[half + 1 : half + 128 : 2, nz - 1] = sign
    return table.astype(jnp.bfloat16)


def dot(a, b):
    return jnp.dot(a, b, preferred_element_type=F32)


def dot_nt(a, b):
    return lax.dot_general(a, b, (((1,), (1,)), ((), ())), preferred_element_type=F32)


def iota(shape, axis):
    return lax.broadcasted_iota(jnp.int32, shape, axis)


def split_two(value):
    high = value.astype(BF16)
    return high, (value - high.astype(F32)).astype(BF16)


def gather_kernel(
    fields, table, links, order, f_ref, send, right, left, far, face_y, face_z, keep_y, keep_z
):
    step = pl.program_id(0)
    place = lax.axis_index("ax")
    nx, ny, nz = f_ref.shape[2:]
    lane = iota((ny, nz), 1)

    def group(g, carry):
        to_right, to_left, columns = carry
        part = jnp.zeros((ny, nz), F32)
        for j in range(8):
            x = 8 * g + j
            tile = f_ref[0, 0, x].astype(F32)
            to_right = to_right + table[place, x] * tile
            to_left = to_left + table[place, nx + x] * tile
            turned = pltpu.roll(tile, 2 * j, 1) if j else tile
            part = jnp.where(((lane + 1 - 2 * j) & 127) < 2, turned, part)
        part = pltpu.roll(part, 16 * g, 1)
        columns = jnp.where(((lane + 1 - 16 * g) & 127) < 16, part, columns)
        return to_right, to_left, columns

    zero = jnp.zeros((ny, nz), F32)
    to_right, to_left, columns = lax.fori_loop(0, nx // 8, group, (zero, zero, zero))
    first = f_ref[0, 0, 0]
    last = f_ref[0, 0, nx - 1]
    right[0, 0] = last
    right[0, 1], right[0, 2] = split_two(to_right)
    left[0, 0] = first
    left[0, 1], left[0, 2] = split_two(to_left)
    base = 2 * nx
    far[0] = (
        table[place, base] * to_right
        + table[place, base + 1] * to_left
        + table[place, base + 2] * last.astype(F32)
        + table[place, base + 3] * first.astype(F32)
    ).astype(BF16)
    columns = columns.astype(BF16)
    face_z[0] = columns
    keep_z[step] = columns
    pick = iota((nx, 16 * nx), 1) - 16 * iota((nx, 16 * nx), 0)
    low = dot((pick == 0).astype(F32).astype(BF16), f_ref[0, 0, :, 0:16, :].reshape(16 * nx, nz))
    high = dot(
        (pick == 15).astype(F32).astype(BF16), f_ref[0, 0, :, ny - 16 : ny, :].reshape(16 * nx, nz)
    )
    faces = jnp.concatenate([low, high], axis=1).astype(BF16)
    face_y[0] = faces
    keep_y[step] = faces

    @pl.when(step == fields - 1)
    def _():
        own = lax.axis_index("blk")
        source = links[0]
        blocks, patches = source.shape
        hit = (source == own).astype(F32)
        before = (iota((patches, patches), 0) < iota((patches, patches), 1)).astype(F32)
        rank = dot(hit.astype(BF16), before.astype(BF16))
        face = links[1].astype(F32) + 1.0
        columns = []
        for c in range(2):
            chosen = jnp.where(rank == float(c), hit, 0.0) * face
            chosen = jnp.sum(chosen, axis=1, keepdims=True)
            columns.append(jnp.broadcast_to(chosen, (blocks, 128)))
        chosen = jnp.concatenate(columns, axis=0).astype(BF16)
        rows = 16 * blocks
        row = iota((rows, 2 * blocks), 0)
        slot = (row & 15) // 8 * blocks + row // 16
        spread = (slot == iota((rows, 2 * blocks), 1)).astype(F32).astype(BF16)
        chosen = dot(spread, chosen)
        cells = PW * patches
        target = (chosen.astype(jnp.int32) - 1) * PW + (iota((rows, 128), 0) & 7)
        target = jnp.concatenate([target] * (cells // 128), axis=1)
        chooser = (iota((rows, cells), 1) == target).astype(F32).astype(BF16)
        for pair in range((fields + 1) // 2):
            one = 2 * pair
            if one + 1 < fields:
                ys = jnp.concatenate([keep_y[one], keep_y[one + 1]], axis=0)
                zs = jnp.concatenate([keep_z[one], keep_z[one + 1]], axis=1)
            else:
                ys = jnp.concatenate([keep_y[one], jnp.zeros_like(keep_y[one])], axis=0)
                zs = jnp.concatenate([keep_z[one], jnp.zeros_like(keep_z[one])], axis=1)
            zs = dot(zs, order[...]).astype(BF16)
            zs = jnp.concatenate([zs[:, :128], zs[:, 128:]], axis=0)
            out = dot_nt(chooser[:, : 2 * nz], ys) + dot(chooser[:, 2 * nz :], zs)
            send[:, :, 128 * pair : 128 * pair + 128] = out.astype(BF16).reshape(blocks, 16, 128)


def flux(gradients, metric, density, velocity, pressure, sums):
    ka, kb, kc = metric
    speed = ka * velocity[0] + kb * velocity[1] + kc * velocity[2]
    coupled = density * gradients[0] + pressure * gradients[4]
    turned = ka * gradients[1] + kb * gradients[2] + kc * gradients[3]
    terms = [
        speed * gradients[0],
        speed * gradients[1] + ka * coupled,
        speed * gradients[2] + kb * coupled,
        speed * gradients[3] + kc * coupled,
        speed * gradients[4],
        turned,
    ]
    return terms if sums is None else [a + b for a, b in zip(sums, terms)]


def penalty_parts(fields, nx, links, order, received, face_y, face_z, pen_y, pair_z):
    ny, nz = face_z.shape[1:]
    own = lax.axis_index("blk")
    blocks, patches = links.shape[1:]
    cells = PW * patches
    source = links[0, pl.ds(own, 1), :]
    turn = links[2, pl.ds(own, 1), :]
    same = (patches, patches)
    diagonal = iota(same, 0) == iota(same, 1)

    def tall(value):
        value = jnp.where(diagonal, jnp.broadcast_to(value, same), 0.0)
        return jnp.sum(value, axis=1, keepdims=True)

    wide = jnp.broadcast_to(source, same).astype(F32)
    earlier = (iota(same, 0) < iota(same, 1)) & (wide == tall(source.astype(F32)))
    slot = jnp.sum(earlier.astype(F32), axis=0, keepdims=True)
    live = (source >= 0).astype(F32)
    where = jnp.where(source >= 0, source.astype(F32) * 16.0 + slot * 8.0, -16.0)
    shape = (cells, patches)
    mine = (iota(shape, 0) // PW) == iota(shape, 1)

    def spread(value):
        value = jnp.where(mine, jnp.broadcast_to(value, shape), 0.0)
        return jnp.sum(value, axis=1, keepdims=True)

    cell = iota((cells, 1), 0) & 7
    cell = jnp.where(spread(turn.astype(F32)) > 0.5, 7 - cell, cell)
    target = spread(where).astype(jnp.int32) + cell
    slots = 16 * blocks
    chooser = (iota((cells, slots), 1) == target).astype(F32).astype(BF16)
    live_rows = spread(live)
    got = dot(chooser, received[...].reshape(slots, received.shape[2]))
    got_y = jnp.transpose(got[: 2 * nz])
    shape = (patches, 2 * nz)
    across = jnp.where(
        iota(shape, 0) == iota(shape, 1) // PW, jnp.broadcast_to(tall(live), shape), 0.0
    )
    across = jnp.sum(across, axis=0, keepdims=True)
    for f in range(fields):
        value = got_y[nx * f : nx * f + nx] - across * face_y[f].astype(F32)
        pen_y[0, nx * f : nx * f + nx, :] = value[:, :nz]
        pen_y[1, nx * f : nx * f + nx, :] = value[:, nz:]
    even = (iota((ny, 128), 1) & 1) == 0
    live_z = jnp.where(
        even, live_rows[2 * nz : 2 * nz + ny], live_rows[2 * nz + ny : 2 * nz + 2 * ny]
    )
    for pair in range((fields + 1) // 2):
        lanes = slice(128 * pair, 128 * pair + 128)
        both = jnp.concatenate(
            [got[2 * nz : 2 * nz + ny, lanes], got[2 * nz + ny :, lanes]], axis=1
        )
        both = dot_nt(both.astype(BF16), order[...])
        for q in range(2):
            f = 2 * pair + q
            if f < fields:
                pair_z[f, :, :128] = both[:, 128 * q : 128 * q + 128].astype(BF16)
                pair_z[f, :, 128:] = (live_z * face_z[f].astype(F32)).astype(BF16)


def main_kernel(
    fields,
    table,
    links,
    order,
    along_y,
    along_z,
    ends,
    received,
    right,
    left,
    far,
    own_left,
    face_y,
    face_z,
    adjoint_hbm,
    density_hbm,
    velocity_hbm,
    pressure_hbm,
    metrics_hbm,
    out_hbm,
    f_ref,
    density,
    velocity,
    pressure,
    metrics,
    out,
    line,
    pen_y,
    pair_z,
    field_sem,
    flow_sem,
    out_sem,
):
    place = lax.axis_index("ax")
    nx, ny, nz = density.shape
    rows = 16
    bands = ny // rows
    chunk = 8
    chunks = nx // chunk

    def field_copy(c):
        at = pl.ds(pl.multiple_of(c * rows, rows), rows)
        return pltpu.make_async_copy(
            adjoint_hbm.at[:, 0, :, at, :], f_ref.at[:, :, at, :], field_sem.at[c]
        )

    def flow_copies(c):
        at = pl.ds(c * chunk, chunk)
        return [
            pltpu.make_async_copy(density_hbm.at[0, at], density.at[at], flow_sem.at[c, 0]),
            pltpu.make_async_copy(velocity_hbm.at[:, 0, at], velocity.at[:, at], flow_sem.at[c, 1]),
            pltpu.make_async_copy(pressure_hbm.at[0, at], pressure.at[at], flow_sem.at[c, 2]),
            pltpu.make_async_copy(metrics_hbm.at[:, 0, at], metrics.at[:, at], flow_sem.at[c, 3]),
        ]

    def out_copy(c):
        at = pl.ds(c * chunk, chunk)
        return pltpu.make_async_copy(out.at[:, at], out_hbm.at[:, 0, at], out_sem.at[c])

    for c in range(bands):
        field_copy(c).start()
    for c in reversed(range(chunks)):
        for copy in flow_copies(c):
            copy.start()

    penalty_parts(fields, nx, links, order, received, face_y, face_z, pen_y, pair_z)

    base = 2 * nx

    def scalar(i):
        return table[place, base + i]

    inverse = 1.0 / PIVOT
    near = NEAR * inverse
    far_coef = FAR * inverse

    def band(c, _):
        field_copy(c).wait()
        at = pl.ds(pl.multiple_of(c * rows, rows), rows)

        def load(f, x):
            return f_ref[f, x, at, :].astype(F32)

        def edges(f):
            right_fn = right[f, 1, at, :].astype(F32) + right[f, 2, at, :].astype(F32)
            left_fn = left[f, 1, at, :].astype(F32) + left[f, 2, at, :].astype(F32)
            own_fn = own_left[f, 1, at, :].astype(F32) + own_left[f, 2, at, :].astype(F32)
            right_last = right[f, 0, at, :].astype(F32)
            left_first = left[f, 0, at, :].astype(F32)
            far_plane = far[f, at, :].astype(F32)
            low = (
                right_fn
                + scalar(4) * load(f, 0)
                + scalar(5) * load(f, 1)
                + scalar(6) * own_fn
                + scalar(7) * left_fn
                + scalar(8) * left_first
                + scalar(11) * far_plane
            )
            high = (
                left_fn
                + scalar(9) * load(f, nx - 1)
                + scalar(10) * load(f, nx - 2)
                + scalar(12) * far_plane
            )
            return (
                low * inverse,
                -far_coef * right_last,
                far_coef * left_first,
                high * inverse,
            )

        for members in ((0, 1, 2), (3, 4)):
            edge = [edges(f) for f in members]
            state = []
            for q, f in enumerate(members):
                f0, f1, f2, f3 = [load(f, x) for x in range(4)]
                d0 = near * f1 + far_coef * f2 + edge[q][0]
                d1 = near * (f2 - f0) + far_coef * f3 + edge[q][1] - MULT * d0
                line[f, 0, at, :] = d0
                line[f, 1, at, :] = d1
                state.append((f0, f1, f2, f3, d1))

            def forward(x, state):
                new = []
                for q, f in enumerate(members):
                    fm2, fm1, f0, fp1, d = state[q]
                    fp2 = load(f, x + 2)
                    d = (near * (fp1 - fm1) + far_coef * (fp2 - fm2)) - MULT * d
                    line[f, x, at, :] = d
                    new.append((fm1, f0, fp1, fp2, d))
                return tuple(new)

            state = lax.fori_loop(2, nx - 2, forward, tuple(state), unroll=4)
            for q, f in enumerate(members):
                fm2, fm1, f0, fp1, d = state[q]
                d = near * (fp1 - fm1) - far_coef * fm2 + edge[q][2] - MULT * d
                line[f, nx - 2, at, :] = d
                d = -near * f0 - far_coef * fm1 + edge[q][3] - MULT * d
                line[f, nx - 1, at, :] = d
                line[f, nx, at, :] = scalar(13) * d
        return 0

    lax.fori_loop(0, bands, band, 0)

    lane = iota((ny, 2 * 128), 1)
    row = iota((rows, nz), 0)

    def two(h, _):
        grads_y = []
        grads_z = []
        pens = []
        xs = (2 * h, 2 * h + 1)
        for f in range(fields):
            tiles = [f_ref[f, x] for x in xs]
            both = jnp.concatenate(tiles, axis=0)
            grads_z.append(dot(jnp.concatenate([both, both], axis=1), along_z[...]))
            wide = jnp.concatenate(tiles, axis=1)
            grads_y.append(dot(along_y[...], jnp.concatenate([wide, wide], axis=0)))
            values = pair_z[f]
            chosen = [
                jnp.where(((lane + 1 - 2 * x) & 127) < 2, values, jnp.zeros_like(values)) for x in xs
            ]
            pens.append(dot(jnp.concatenate(chosen, axis=0), ends[...]))
        for q in (1, 0):
            x = xs[q]
            for y in range(0, ny, rows):
                at = slice(y, y + rows)
                rho = density[x, at, :].astype(F32)
                vel = [velocity[i, x, at, :].astype(F32) for i in range(3)]
                press = HEAT * pressure[x, at, :].astype(F32)
                gx = []
                for f in range(fields):
                    value = line[f, x, at, :] - MULT * line[f, x + 1, at, :]
                    line[f, x, at, :] = value
                    gx.append(value)
                gy = [g[at, q * nz : (q + 1) * nz] for g in grads_y]
                gz = [g[q * ny + y : q * ny + y + rows] for g in grads_z]
                sums = None
                for d, g in enumerate((gx, gy, gz)):
                    metric = [metrics[3 * d + i, x, at, :].astype(F32) for i in range(3)]
                    sums = flux(g, metric, rho, vel, press, sums)
                sums[4] = sums[4] + sums[5] / rho
                for f in range(fields):
                    total = sums[f] + pens[f][q * ny + y : q * ny + y + rows]
                    if y == 0:
                        line_y = pen_y[0, pl.ds(f * nx + x, 1), :]
                        total = total + jnp.where(row == 0, line_y, 0.0)
                    if y == ny - rows:
                        line_y = pen_y[1, pl.ds(f * nx + x, 1), :]
                        total = total + jnp.where(row == rows - 1, line_y, 0.0)
                    out[f, x, at, :] = total.astype(BF16)
        return 0

    def section(k, _):
        c = chunks - 1 - k
        for copy in flow_copies(c):
            copy.wait()
        lax.fori_loop(0, chunk // 2, lambda i, s: two(c * (chunk // 2) + chunk // 2 - 1 - i, s), 0)
        out_copy(c).start()
        return 0

    lax.fori_loop(0, chunks, section, 0)
    for c in range(chunks):
        out_copy(c).wait()


def in_hbm(*arrays):
    return [pltpu.with_memory_space_constraint(a, pltpu.HBM) for a in arrays]


def whole(shape):
    return pl.BlockSpec(shape, lambda *_: (0,) * len(shape))


def gather_call(table, order, links, adjoint):
    fields, _, nx, ny, nz = adjoint.shape
    blocks = links.shape[1]
    lanes = 128 * ((fields + 1) // 2)
    shape = jax.ShapeDtypeStruct
    return pl.pallas_call(
        functools.partial(gather_kernel, fields),
        grid=(fields,),
        in_specs=[
            pl.BlockSpec(memory_space=pltpu.SMEM),
            whole(links.shape),
            whole(order.shape),
            pl.BlockSpec((1, 1, nx, ny, nz), lambda i: (i, 0, 0, 0, 0)),
        ],
        out_specs=[
            whole((blocks, 16, lanes)),
            pl.BlockSpec((1, 3, ny, nz), lambda i: (i, 0, 0, 0)),
            pl.BlockSpec((1, 3, ny, nz), lambda i: (i, 0, 0, 0)),
            pl.BlockSpec((1, ny, nz), lambda i: (i, 0, 0)),
            pl.BlockSpec((1, nx, 2 * nz), lambda i: (i, 0, 0)),
            pl.BlockSpec((1, ny, 128), lambda i: (i, 0, 0)),
        ],
        out_shape=[
            shape((blocks, 16, lanes), BF16),
            shape((fields, 3, ny, nz), BF16),
            shape((fields, 3, ny, nz), BF16),
            shape((fields, ny, nz), BF16),
            shape((fields, nx, 2 * nz), BF16),
            shape((fields, ny, 128), BF16),
        ],
        scratch_shapes=[
            pltpu.VMEM((fields, nx, 2 * nz), BF16),
            pltpu.VMEM((fields, ny, 128), BF16),
        ],
        compiler_params=pltpu.CompilerParams(vmem_limit_bytes=16 * MIB),
        cost_estimate=pl.CostEstimate(flops=10**9, bytes_accessed=7 * 10**6, transcendentals=0),
    )(*in_hbm(table, links, order, adjoint))


def main_call(table, order, along_y, along_z, ends, links, flow, edges):
    adjoint = flow[0]
    fields, _, nx, ny, nz = adjoint.shape
    vmem = pl.BlockSpec(memory_space=pltpu.VMEM)
    hbm = pl.BlockSpec(memory_space=pltpu.HBM)
    small = [links, order, along_y, along_z, ends, *edges]
    return pl.pallas_call(
        functools.partial(main_kernel, fields),
        in_specs=[pl.BlockSpec(memory_space=pltpu.SMEM)] + [vmem] * len(small) + [hbm] * len(flow),
        out_specs=hbm,
        out_shape=jax.ShapeDtypeStruct(adjoint.shape, BF16),
        scratch_shapes=[
            pltpu.VMEM((fields, nx, ny, nz), BF16),
            pltpu.VMEM((nx, ny, nz), BF16),
            pltpu.VMEM((3, nx, ny, nz), BF16),
            pltpu.VMEM((nx, ny, nz), BF16),
            pltpu.VMEM((9, nx, ny, nz), BF16),
            pltpu.VMEM((fields, nx, ny, nz), BF16),
            pltpu.VMEM((fields, nx + 1, ny, nz), F32),
            pltpu.VMEM((2, fields * nx, nz), F32),
            pltpu.VMEM((fields, ny, 256), BF16),
            pltpu.SemaphoreType.DMA((ny // 16,)),
            pltpu.SemaphoreType.DMA((nx // 8, 4)),
            pltpu.SemaphoreType.DMA((nx // 8,)),
        ],
        compiler_params=pltpu.CompilerParams(vmem_limit_bytes=52 * MIB),
        cost_estimate=pl.CostEstimate(
            flops=10**10, bytes_accessed=26 * 10**6, transcendentals=0
        ),
    )(*in_hbm(table), *small, *in_hbm(*flow))


def body(tables, adjoint, density, velocity, pressure, metrics, links):
    along_y, along_z, table, order, ends = [jnp.asarray(t) for t in tables]
    send, right, left, far, face_y, face_z = gather_call(table, order, links, adjoint)
    received = lax.all_to_all(send, "blk", 0, 0)
    pieces = lax.axis_size("ax")
    from_left = lax.ppermute(right, "ax", [(i, i + 1) for i in range(pieces - 1)])
    from_right = lax.ppermute(left, "ax", [(i + 1, i) for i in range(pieces - 1)])
    from_far = lax.ppermute(far, "ax", [(i, (i + 2) % pieces) for i in range(pieces)])
    flow = (adjoint, density, velocity, pressure, metrics)
    edges = (received, from_left, from_right, from_far, left, face_y, face_z)
    return main_call(table, order, along_y, along_z, ends, links, flow, edges)


def solution(mesh):
    in_specs = (
        P(None, "blk", "ax", None, None),
        P("blk", "ax", None, None),
        P(None, "blk", "ax", None, None),
        P("blk", "ax", None, None),
        P(None, "blk", "ax", None, None),
        P(),
    )
    out_specs = P(None, "blk", "ax", None, None)

    def run(*args):
        pieces = mesh.shape["ax"]
        nx, ny, nz = args[0].shape[2:]
        tables = (*lateral_tables(ny, nz), axial_tables(pieces, nx // pieces), lane_order())
        tables = (*tables, end_table(nz))
        return jax.shard_map(
            functools.partial(body, tables),
            mesh=mesh,
            in_specs=in_specs,
            out_specs=out_specs,
            check_vma=False,
        )(*args)

    return run
```

time: 73.1 us -> 62.9 us (0.86)
  local copies, waits for them, and re-layouts: 10.9 us -> 0.02 us
  Pallas kernels: 45 us -> 38.7 us
  waiting for transfers between devices: 0.01 us -> 5.48 us
  starting transfers between devices: 16.2 us -> 17.5 us
    unnamed x22 -> x10, local copies, waits for them, and re-layouts: 10.9 us -> 0.02 us
    pallas_call x3 -> x2, Pallas kernels: 45 us -> 38.7 us  [the longest x1 27.2 us: main_call(): pl.pallas_call(functools.partial(main_kernel, fields), in_specs=[pl.Block...]
    ppermute x1, waiting for transfers between devices: 0.01 us -> 5.47 us  [body(): lax.ppermute(far, 'ax', [(i, (i + 2) % pieces) for i in range(pieces)])]
    ppermute x1, starting transfers between devices: 2.65 us -> 3.56 us  [body(): lax.ppermute(right, 'ax', [(i, i + 1) for i in range(pieces - 1)])]
  transfers between devices with their start and end apart: 4 -> 4, of which waited for: 0 -> 1; matrix products, arithmetic and copies ran while one was open for 0% -> 0% of each run, Pallas kernels for 18% -> 0%
where the time goes in v2:
time: 62.9 us; the launch traced here: 61.8 us
  Pallas kernels  38.7 us (62%)
  starting transfers between devices  17.5 us (28%)
  waiting for transfers between devices  5.48 us (9%)
    pallas_call x1, Pallas kernels, main_call(): pl.pallas_call(functools.partial(main_kernel, fields), in_specs=[pl.Block...  27.2 us
    pallas_call x1, Pallas kernels, gather_call(): pl.pallas_call(functools.partial(gather_kernel, fields), grid=(fields,),...  11.4 us
    all_to_all x1, starting transfers between devices, body(): received = lax.all_to_all(send, 'blk', 0, 0)  8.59 us
    ppermute x1, waiting for transfers between devices, body(): lax.ppermute(far, 'ax', [(i, (i + 2) % pieces) for i in range(pieces)])  5.47 us
    ppermute x1, starting transfers between devices, body(): lax.ppermute(far, 'ax', [(i, (i + 2) % pieces) for i in range(pieces)])  4.11 us
    ppermute x1, starting transfers between devices, body(): lax.ppermute(right, 'ax', [(i, i + 1) for i in range(pieces - 1)])  3.56 us
    ppermute x1, starting transfers between devices, body(): lax.ppermute(left, 'ax', [(i + 1, i) for i in range(pieces - 1)])  1.29 us
  transfers between devices with their start and end apart: 4, of which 1 were waited for; matrix products, arithmetic and copies ran while one was open for 0% of the time, Pallas kernels for 0%

profile of v2, /device:TPU:1, one launch (start us, length us, event | category | flops | bytes accessed | tf_op | source)
XLA Modules:
  0.0 61.8 jit_solution(15859152728811025198)
XLA Ops:
  0.0 0.0 copy-start
  0.0 0.0 copy-start.2
  0.0 0.0 copy-start.3
  0.0 0.0 copy-start.4
  0.0 0.0 copy-start.1
  0.0 11.4 %shard_map.109 = (bf16[32,16,384]{2,1,0:T(8,128)(2,1)}, bf16[5,3,64,128]{3,2,1,0:T(8,128)(2,1)S(1)}, bf16[5,3,64,128]{3,2,1,0:T(8,128)(2,1)S(1)}, bf16[5,64,128]...) custom-call(f32[4,144]{1,0:T(4,128)} %constant.12.clone.table, ...), custom_call_target="tpu_custom_call" | custom-call | flops 1000000000 | bytes 7000000 | tf_op jit(solution)/shard_map/pallas_call | solution.py:521
  11.5 8.6 %all-to-all-start = ((bf16[32,16,384]{2,1,0:T(8,128)(2,1)}), bf16[32,16,384]{2,1,0:T(8,128)(2,1)S(1)}, u32[]{:S(2)}, u32[]{:S(2)}) async-start(bf16[32,16,384]{2,1,0:T(8,128)(2,1)} %get-tuple-element.11), calls=%async_computation | async-start | bytes 786432 | tf_op jit(solution)/shard_map/all_to_all | solution.py:590
  20.1 3.6 %collective-permute-start = (bf16[5,3,64,128]{3,2,1,0:T(8,128)(2,1)S(1)}, bf16[5,3,64,128]{3,2,1,0:T(8,128)(2,1)S(1)}, u32[]{:S(2)}, u32[]{:S(2)}) collective-permute-start(bf16[5,3,64,128]{3,2,1,0:T(8,128)(2,1)S(1)} %get-tuple-element.12), channel_id=1, source_target_pairs={{0,1},{1,2},{2,3},{4,5},{5,6},{6,7},{8,9},{9,10},{10,11},{12,13},{... | collective-permute-start | bytes 737288 | tf_op jit(solution)/shard_map/ppermute | solution.py:592
  23.6 1.3 %collective-permute-start.1 = (bf16[5,3,64,128]{3,2,1,0:T(8,128)(2,1)S(1)}, bf16[5,3,64,128]{3,2,1,0:T(8,128)(2,1)S(1)}, u32[]{:S(2)}, u32[]{:S(2)}) collective-permute-start(bf16[5,3,64,128]{3,2,1,0:T(8,128)(2,1)S(1)} %get-tuple-element.13.own_left), channel_id=1, source_target_pairs={{1,0},{2,1},{3,2},{5,4},{6,5},{7,6},{9,8},{10,9},{11,10},{13,12},{... | collective-permute-start | bytes 737288 | tf_op jit(solution)/shard_map/ppermute | solution.py:593
  24.9 4.1 %collective-permute-start.2 = (bf16[5,64,128]{2,1,0:T(8,128)(2,1)S(1)}, bf16[5,64,128]{2,1,0:T(8,128)(2,1)S(1)}, u32[]{:S(2)}, u32[]{:S(2)}) collective-permute-start(bf16[5,64,128]{2,1,0:T(8,128)(2,1)S(1)} %get-tuple-element.14), channel_id=1, source_target_pairs={{0,2},{1,3},{2,0},{3,1},{4,6},{5,7},{6,4},{7,5},{8,10},{9,11},{10,... | collective-permute-start | bytes 245768 | tf_op jit(solution)/shard_map/ppermute | solution.py:594
  29.1 5.5 %collective-permute-done.2.far = bf16[5,64,128]{2,1,0:T(8,128)(2,1)S(1)} collective-permute-done((bf16[5,64,128]{2,1,0:T(8,128)(2,1)S(1)}, bf16[5,64,128]{2,1,0:T(8,128)(2,1)S(1)}, u32[]{:S(2)}, u32[]{:S(2)}) %collective-permute-start.2) | collective-permute-done | bytes 81952 | tf_op jit(solution)/shard_map/ppermute | solution.py:594
  34.5 0.0 collective-permute-done.right
  34.5 0.0 collective-permute-done.1.left
  34.5 0.0 all-to-all-done.received
  34.5 0.0 copy-done
  34.5 0.0 copy-done.2
  34.6 0.0 copy-done.3
  34.6 0.0 copy-done.4
  34.6 0.0 copy-done.1
  34.6 27.2 %shard_map.110 = bf16[5,1,64,64,128]{4,3,2,1,0:T(8,128)(2,1)} custom-call(f32[4,144]{1,0:T(4,128)} %constant.12.clone.table, s32[3,32,48]{2,1,0:T(8,128)S(1)} %copy-done.1, bf16[256,256]{1,0:T(8,128)(2,1)S(1)} %copy-done, bf16[64,128]{1,0:T(8,128)(2,1)S(1)} %copy-done.4, bf16[256,128]{1,0:T(8,128)(2,1)S(1)} %copy-done.3, bf16[256,128]{1,0:T(8,128)(2,1)S(1)} %copy-done.2, ...), custom_call_target="tpu_custom_call" | custom-call | flops 10000000000 | bytes 26000000 | tf_op jit(solution)/shard_map/pallas_call | solution.py:561
Async XLA Ops:
  0.0 34.5 %copy-start = (bf16[256,256]{1,0:T(8,128)(2,1)S(1)}, bf16[256,256]{1,0:T(8,128)(2,1)}, u32[]{:S(2)}) copy-start(bf16[256,256]{1,0:T(8,128)(2,1)} %constant.13.clone.order) | copy-start | bytes 393220
  0.0 34.5 %copy-start.2 = (bf16[256,128]{1,0:T(8,128)(2,1)S(1)}, bf16[256,128]{1,0:T(8,128)(2,1)}, u32[]{:S(2)}) copy-start(bf16[256,128]{1,0:T(8,128)(2,1)} %constant.14.clone.ends) | copy-start | bytes 196612
  0.0 34.6 %copy-start.3 = (bf16[256,128]{1,0:T(8,128)(2,1)S(1)}, bf16[256,128]{1,0:T(8,128)(2,1)}, u32[]{:S(2)}) copy-start(bf16[256,128]{1,0:T(8,128)(2,1)} %constant.11.clone.along_z) | copy-start | bytes 196612
  0.0 34.6 %copy-start.4 = (bf16[64,128]{1,0:T(8,128)(2,1)S(1)}, bf16[64,128]{1,0:T(8,128)(2,1)}, u32[]{:S(2)}) copy-start(bf16[64,128]{1,0:T(8,128)(2,1)} %constant.10.clone.along_y) | copy-start | bytes 49156
  0.0 34.6 %copy-start.1 = (s32[3,32,48]{2,1,0:T(8,128)S(1)}, s32[3,32,48]{2,1,0:T(8,128)}, u32[]{:S(2)}) copy-start(s32[3,32,48]{2,1,0:T(8,128)} %links.3) | copy-start | bytes 55300
  11.5 23.1 %all-to-all-start = ((bf16[32,16,384]{2,1,0:T(8,128)(2,1)}), bf16[32,16,384]{2,1,0:T(8,128)(2,1)S(1)}, u32[]{:S(2)}, u32[]{:S(2)}) async-start(bf16[32,16,384]{2,1,0:T(8,128)(2,1)} %get-tuple-element.11), calls=%async_computation | async-start | bytes 786432 | tf_op jit(solution)/shard_map/all_to_all | solution.py:590
  20.1 14.4 %collective-permute-start = (bf16[5,3,64,128]{3,2,1,0:T(8,128)(2,1)S(1)}, bf16[5,3,64,128]{3,2,1,0:T(8,128)(2,1)S(1)}, u32[]{:S(2)}, u32[]{:S(2)}) collective-permute-start(bf16[5,3,64,128]{3,2,1,0:T(8,128)(2,1)S(1)} %get-tuple-element.12), channel_id=1, source_target_pairs={{0,1},{1,2},{2,3},{4,5},{5,6},{6,7},{8,9},{9,10},{10,11},{12,13},{... | collective-permute-start | bytes 737288 | tf_op jit(solution)/shard_map/ppermute | solution.py:592
  23.6 10.9 %collective-permute-start.1 = (bf16[5,3,64,128]{3,2,1,0:T(8,128)(2,1)S(1)}, bf16[5,3,64,128]{3,2,1,0:T(8,128)(2,1)S(1)}, u32[]{:S(2)}, u32[]{:S(2)}) collective-permute-start(bf16[5,3,64,128]{3,2,1,0:T(8,128)(2,1)S(1)} %get-tuple-element.13.own_left), channel_id=1, source_target_pairs={{1,0},{2,1},{3,2},{5,4},{6,5},{7,6},{9,8},{10,9},{11,10},{13,12},{... | collective-permute-start | bytes 737288 | tf_op jit(solution)/shard_map/ppermute | solution.py:593
  24.9 9.6 %collective-permute-start.2 = (bf16[5,64,128]{2,1,0:T(8,128)(2,1)S(1)}, bf16[5,64,128]{2,1,0:T(8,128)(2,1)S(1)}, u32[]{:S(2)}, u32[]{:S(2)}) collective-permute-start(bf16[5,64,128]{2,1,0:T(8,128)(2,1)S(1)} %get-tuple-element.14), channel_id=1, source_target_pairs={{0,2},{1,3},{2,0},{3,1},{4,6},{5,7},{6,4},{7,5},{8,10},{9,11},{10,... | collective-permute-start | bytes 245768 | tf_op jit(solution)/shard_map/ppermute | solution.py:594

commit v3 on v2

--- a/solution.py
+++ b/solution.py
@@ -18,6 +18,7 @@
 F32 = jnp.float32
 BF16 = jnp.bfloat16
 MIB = 1 << 20
+BATCH = 32
 
 
 def dense(n):
@@ -135,90 +136,128 @@
 
 
 def gather_kernel(
-    fields, table, links, order, f_ref, send, right, left, far, face_y, face_z, keep_y, keep_z
+    fields,
+    table,
+    links,
+    order,
+    adjoint_hbm,
+    send,
+    right,
+    left,
+    far,
+    face_y,
+    face_z,
+    f_ref,
+    rows_y,
+    chooser,
+    field_sem,
 ):
-    step = pl.program_id(0)
     place = lax.axis_index("ax")
-    nx, ny, nz = f_ref.shape[2:]
-    lane = iota((ny, nz), 1)
-
-    def group(g, carry):
-        to_right, to_left, columns = carry
-        part = jnp.zeros((ny, nz), F32)
-        for j in range(8):
-            x = 8 * g + j
-            tile = f_ref[0, 0, x].astype(F32)
-            to_right = to_right + table[place, x] * tile
-            to_left = to_left + table[place, nx + x] * tile
-            turned = pltpu.roll(tile, 2 * j, 1) if j else tile
-            part = jnp.where(((lane + 1 - 2 * j) & 127) < 2, turned, part)
-        part = pltpu.roll(part, 16 * g, 1)
-        columns = jnp.where(((lane + 1 - 16 * g) & 127) < 16, part, columns)
-        return to_right, to_left, columns
-
-    zero = jnp.zeros((ny, nz), F32)
-    to_right, to_left, columns = lax.fori_loop(0, nx // 8, group, (zero, zero, zero))
-    first = f_ref[0, 0, 0]
-    last = f_ref[0, 0, nx - 1]
-    right[0, 0] = last
-    right[0, 1], right[0, 2] = split_two(to_right)
-    left[0, 0] = first
-    left[0, 1], left[0, 2] = split_two(to_left)
+    nx, ny, nz = f_ref.shape[1:]
+
+    def field_copy(f):
+        return pltpu.make_async_copy(adjoint_hbm.at[f, 0], f_ref.at[f], field_sem.at[f])
+
+    for f in range(fields):
+        field_copy(f).start()
+
+    own = lax.axis_index("blk")
+    source = links[0]
+    blocks, patches = source.shape
+    hit = (source == own).astype(F32)
+    before = (iota((patches, patches), 0) < iota((patches, patches), 1)).astype(F32)
+    rank = dot(hit.astype(BF16), before.astype(BF16))
+    face = links[1].astype(F32) + 1.0
+    chosen = []
+    for c in range(2):
+        value = jnp.where(rank == float(c), hit, 0.0) * face
+        value = jnp.sum(value, axis=1, keepdims=True)
+        chosen.append(jnp.broadcast_to(value, (blocks, 128)))
+    chosen = jnp.concatenate(chosen, axis=0).astype(BF16)
+    slots = 16 * blocks
+    row = iota((slots, 2 * blocks), 0)
+    slot = (row & 15) // 8 * blocks + row // 16
+    spread = (slot == iota((slots, 2 * blocks), 1)).astype(F32).astype(BF16)
+    chosen = dot(spread, chosen)
+    cells = PW * patches
+    target = (chosen.astype(jnp.int32) - 1) * PW + (iota((slots, 128), 0) & 7)
+    target = jnp.concatenate([target] * (cells // 128), axis=1)
+    chooser[...] = (iota((slots, cells), 1) == target).astype(F32).astype(BF16)
+
     base = 2 * nx
-    far[0] = (
-        table[place, base] * to_right
-        + table[place, base + 1] * to_left
-        + table[place, base + 2] * last.astype(F32)
-        + table[place, base + 3] * first.astype(F32)
-    ).astype(BF16)
-    columns = columns.astype(BF16)
-    face_z[0] = columns
-    keep_z[step] = columns
-    pick = iota((nx, 16 * nx), 1) - 16 * iota((nx, 16 * nx), 0)
-    low = dot((pick == 0).astype(F32).astype(BF16), f_ref[0, 0, :, 0:16, :].reshape(16 * nx, nz))
-    high = dot(
-        (pick == 15).astype(F32).astype(BF16), f_ref[0, 0, :, ny - 16 : ny, :].reshape(16 * nx, nz)
-    )
-    faces = jnp.concatenate([low, high], axis=1).astype(BF16)
-    face_y[0] = faces
-    keep_y[step] = faces
-
-    @pl.when(step == fields - 1)
-    def _():
-        own = lax.axis_index("blk")
-        source = links[0]
-        blocks, patches = source.shape
-        hit = (source == own).astype(F32)
-        before = (iota((patches, patches), 0) < iota((patches, patches), 1)).astype(F32)
-        rank = dot(hit.astype(BF16), before.astype(BF16))
-        face = links[1].astype(F32) + 1.0
-        columns = []
-        for c in range(2):
-            chosen = jnp.where(rank == float(c), hit, 0.0) * face
-            chosen = jnp.sum(chosen, axis=1, keepdims=True)
-            columns.append(jnp.broadcast_to(chosen, (blocks, 128)))
-        chosen = jnp.concatenate(columns, axis=0).astype(BF16)
-        rows = 16 * blocks
-        row = iota((rows, 2 * blocks), 0)
-        slot = (row & 15) // 8 * blocks + row // 16
-        spread = (slot == iota((rows, 2 * blocks), 1)).astype(F32).astype(BF16)
-        chosen = dot(spread, chosen)
-        cells = PW * patches
-        target = (chosen.astype(jnp.int32) - 1) * PW + (iota((rows, 128), 0) & 7)
-        target = jnp.concatenate([target] * (cells // 128), axis=1)
-        chooser = (iota((rows, cells), 1) == target).astype(F32).astype(BF16)
-        for pair in range((fields + 1) // 2):
-            one = 2 * pair
-            if one + 1 < fields:
-                ys = jnp.concatenate([keep_y[one], keep_y[one + 1]], axis=0)
-                zs = jnp.concatenate([keep_z[one], keep_z[one + 1]], axis=1)
-            else:
-                ys = jnp.concatenate([keep_y[one], jnp.zeros_like(keep_y[one])], axis=0)
-                zs = jnp.concatenate([keep_z[one], jnp.zeros_like(keep_z[one])], axis=1)
-            zs = dot(zs, order[...]).astype(BF16)
-            zs = jnp.concatenate([zs[:, :128], zs[:, 128:]], axis=0)
-            out = dot_nt(chooser[:, : 2 * nz], ys) + dot(chooser[:, 2 * nz :], zs)
-            send[:, :, 128 * pair : 128 * pair + 128] = out.astype(BF16).reshape(blocks, 16, 128)
+    row8 = iota((8, nz), 0)
+
+    def one_field(f, _):
+        field_copy(f).wait()
+
+        def group(g, carry):
+            to_right, to_left = carry
+            low = jnp.zeros((8, nz), F32)
+            high = jnp.zeros((8, nz), F32)
+            for j in range(8):
+                x = 8 * g + j
+                tile = f_ref[f, x].astype(F32)
+                to_right = to_right + table[place, x] * tile
+                to_left = to_left + table[place, nx + x] * tile
+                low = jnp.where(row8 == j, tile[0:1], low)
+                high = jnp.where(row8 == j, tile[ny - 1 : ny], high)
+            at = pl.ds(pl.multiple_of(8 * g, 8), 8)
+            rows_y[at, :nz] = low
+            rows_y[at, nz:] = high
+            return to_right, to_left
+
+        zero = jnp.zeros((ny, nz), F32)
+        to_right, to_left = lax.fori_loop(0, nx // 8, group, (zero, zero))
+        first = f_ref[f, 0]
+        last = f_ref[f, nx - 1]
+        right[f, 0] = last
+        right[f, 1], right[f, 2] = split_two(to_right)
+        left[f, 0] = first
+        left[f, 1], left[f, 2] = split_two(to_left)
+        far[f] = (
+            table[place, base] * to_right
+            + table[place, base + 1] * to_left
+            + table[place, base + 2] * last.astype(F32)
+            + table[place, base + 3] * first.astype(F32)
+        ).astype(BF16)
+        face_y[f] = rows_y[...].astype(BF16)
+        return 0
+
+    lax.fori_loop(0, fields, one_field, 0)
+
+    row16 = iota((16, 128), 0)
+    lane = iota((16, 128), 1)
+
+    def one_hot(mask):
+        return mask.astype(F32).astype(BF16)
+
+    def columns(h, total):
+        wide = []
+        table_rows = []
+        for j in range(BATCH):
+            x = BATCH * h + j
+            wide.append(jnp.concatenate([f_ref[f, x] for f in range(fields)], axis=0))
+            table_rows.append(one_hot((row16 == 0) & (lane == 2 * x)))
+            table_rows.append(jnp.zeros((nz - 32, 128), BF16))
+            table_rows.append(one_hot((row16 == 15) & (lane == ((2 * x - 1) & 127))))
+        return total + dot(jnp.concatenate(wide, axis=1), jnp.concatenate(table_rows, axis=0))
+
+    total = lax.fori_loop(0, nx // BATCH, columns, jnp.zeros((fields * ny, 128), F32))
+    for f in range(fields):
+        face_z[f] = total[f * ny : f * ny + ny].astype(BF16)
+
+    for pair in range((fields + 1) // 2):
+        one = 2 * pair
+        if one + 1 < fields:
+            ys = jnp.concatenate([face_y[one], face_y[one + 1]], axis=0)
+            zs = jnp.concatenate([face_z[one], face_z[one + 1]], axis=1)
+        else:
+            ys = jnp.concatenate([face_y[one], jnp.zeros_like(face_y[one])], axis=0)
+            zs = jnp.concatenate([face_z[one], jnp.zeros_like(face_z[one])], axis=1)
+        zs = dot(zs, order[...]).astype(BF16)
+        zs = jnp.concatenate([zs[:, :128], zs[:, 128:]], axis=0)
+        value = dot_nt(chooser[:, : 2 * nz], ys) + dot(chooser[:, 2 * nz :], zs)
+        send[:, :, 128 * pair : 128 * pair + 128] = value.astype(BF16).reshape(blocks, 16, 128)
 
 
 def flux(gradients, metric, density, velocity, pressure, sums):
@@ -327,6 +366,12 @@
     line,
     pen_y,
     pair_z,
+    now_y,
+    now_z,
+    now_p,
+    later_y,
+    later_z,
+    later_p,
     field_sem,
     flow_sem,
     out_sem,
@@ -443,29 +488,33 @@
 
     lax.fori_loop(0, bands, band, 0)
 
-    lane = iota((ny, 2 * 128), 1)
+    lane = iota((rows, 256), 1)
     row = iota((rows, nz), 0)
 
-    def two(h, _):
-        grads_y = []
-        grads_z = []
-        pens = []
+    def matmuls(h, parts):
+        grad_y, grad_z, pens = parts
         xs = (2 * h, 2 * h + 1)
+        masks = [(((lane + 1 - 2 * x) & 127) < 2).astype(F32).astype(BF16) for x in xs]
+        masks = [jnp.concatenate([mask] * (ny // rows), axis=0) for mask in masks]
         for f in range(fields):
-            tiles = [f_ref[f, x] for x in xs]
-            both = jnp.concatenate(tiles, axis=0)
-            grads_z.append(dot(jnp.concatenate([both, both], axis=1), along_z[...]))
-            wide = jnp.concatenate(tiles, axis=1)
-            grads_y.append(dot(along_y[...], jnp.concatenate([wide, wide], axis=0)))
-            values = pair_z[f]
-            chosen = [
-                jnp.where(((lane + 1 - 2 * x) & 127) < 2, values, jnp.zeros_like(values)) for x in xs
-            ]
-            pens.append(dot(jnp.concatenate(chosen, axis=0), ends[...]))
+            both = f_ref[f, pl.ds(2 * h, 2)].reshape(2 * ny, nz)
+            grad_z[f] = dot(jnp.concatenate([both, both], axis=1), along_z[...])
+        for f in range(fields):
+            chosen = [pair_z[f] * mask for mask in masks]
+            pens[f] = dot(jnp.concatenate(chosen, axis=0), ends[...])
+        for f in range(fields):
+            wide = jnp.concatenate([f_ref[f, x] for x in xs], axis=1)
+            got = dot(along_y[...], jnp.concatenate([wide, wide], axis=0))
+            grad_y[f, :ny, :] = got[:, :nz]
+            grad_y[f, ny:, :] = got[:, nz:]
+
+    def two_cells(h, parts):
+        grad_y, grad_z, pens = parts
         for q in (1, 0):
-            x = xs[q]
+            x = 2 * h + q
             for y in range(0, ny, rows):
                 at = slice(y, y + rows)
+                here = slice(q * ny + y, q * ny + y + rows)
                 rho = density[x, at, :].astype(F32)
                 vel = [velocity[i, x, at, :].astype(F32) for i in range(3)]
                 press = HEAT * pressure[x, at, :].astype(F32)
@@ -474,15 +523,15 @@
                     value = line[f, x, at, :] - MULT * line[f, x + 1, at, :]
                     line[f, x, at, :] = value
                     gx.append(value)
-                gy = [g[at, q * nz : (q + 1) * nz] for g in grads_y]
-                gz = [g[q * ny + y : q * ny + y + rows] for g in grads_z]
+                gy = [grad_y[f, here, :] for f in range(fields)]
+                gz = [grad_z[f, here, :] for f in range(fields)]
                 sums = None
                 for d, g in enumerate((gx, gy, gz)):
                     metric = [metrics[3 * d + i, x, at, :].astype(F32) for i in range(3)]
                     sums = flux(g, metric, rho, vel, press, sums)
                 sums[4] = sums[4] + sums[5] / rho
                 for f in range(fields):
-                    total = sums[f] + pens[f][q * ny + y : q * ny + y + rows]
+                    total = sums[f] + pens[f, here, :]
                     if y == 0:
                         line_y = pen_y[0, pl.ds(f * nx + x, 1), :]
                         total = total + jnp.where(row == 0, line_y, 0.0)
@@ -490,13 +539,24 @@
                         line_y = pen_y[1, pl.ds(f * nx + x, 1), :]
                         total = total + jnp.where(row == rows - 1, line_y, 0.0)
                     out[f, x, at, :] = total.astype(BF16)
-        return 0
+
+    now, later = (now_y, now_z, now_p), (later_y, later_z, later_p)
+    matmuls(nx // 2 - 1, now)
 
     def section(k, _):
         c = chunks - 1 - k
         for copy in flow_copies(c):
             copy.wait()
-        lax.fori_loop(0, chunk // 2, lambda i, s: two(c * (chunk // 2) + chunk // 2 - 1 - i, s), 0)
+
+        def four_cells(i, s):
+            h = (c + 1) * (chunk // 2) - 1 - 2 * i
+            matmuls(h - 1, later)
+            two_cells(h, now)
+            matmuls(jnp.maximum(h - 2, 0), now)
+            two_cells(h - 1, later)
+            return s
+
+        lax.fori_loop(0, chunk // 4, four_cells, 0)
         out_copy(c).start()
         return 0
 
@@ -509,32 +569,21 @@
     return [pltpu.with_memory_space_constraint(a, pltpu.HBM) for a in arrays]
 
 
-def whole(shape):
-    return pl.BlockSpec(shape, lambda *_: (0,) * len(shape))
-
-
 def gather_call(table, order, links, adjoint):
     fields, _, nx, ny, nz = adjoint.shape
-    blocks = links.shape[1]
+    blocks, patches = links.shape[1:]
     lanes = 128 * ((fields + 1) // 2)
     shape = jax.ShapeDtypeStruct
+    vmem = pl.BlockSpec(memory_space=pltpu.VMEM)
     return pl.pallas_call(
         functools.partial(gather_kernel, fields),
-        grid=(fields,),
         in_specs=[
             pl.BlockSpec(memory_space=pltpu.SMEM),
-            whole(links.shape),
-            whole(order.shape),
-            pl.BlockSpec((1, 1, nx, ny, nz), lambda i: (i, 0, 0, 0, 0)),
+            vmem,
+            vmem,
+            pl.BlockSpec(memory_space=pltpu.HBM),
         ],
-        out_specs=[
-            whole((blocks, 16, lanes)),
-            pl.BlockSpec((1, 3, ny, nz), lambda i: (i, 0, 0, 0)),
-            pl.BlockSpec((1, 3, ny, nz), lambda i: (i, 0, 0, 0)),
-            pl.BlockSpec((1, ny, nz), lambda i: (i, 0, 0)),
-            pl.BlockSpec((1, nx, 2 * nz), lambda i: (i, 0, 0)),
-            pl.BlockSpec((1, ny, 128), lambda i: (i, 0, 0)),
-        ],
+        out_specs=[vmem] * 6,
         out_shape=[
             shape((blocks, 16, lanes), BF16),
             shape((fields, 3, ny, nz), BF16),
@@ -544,12 +593,14 @@
             shape((fields, ny, 128), BF16),
         ],
         scratch_shapes=[
-            pltpu.VMEM((fields, nx, 2 * nz), BF16),
-            pltpu.VMEM((fields, ny, 128), BF16),
+            pltpu.VMEM((fields, nx, ny, nz), BF16),
+            pltpu.VMEM((nx, 2 * nz), F32),
+            pltpu.VMEM((16 * blocks, PW * patches), BF16),
+            pltpu.SemaphoreType.DMA((fields,)),
         ],
-        compiler_params=pltpu.CompilerParams(vmem_limit_bytes=16 * MIB),
+        compiler_params=pltpu.CompilerParams(vmem_limit_bytes=24 * MIB),
         cost_estimate=pl.CostEstimate(flops=10**9, bytes_accessed=7 * 10**6, transcendentals=0),
-    )(*in_hbm(table, links, order, adjoint))
+    )(*in_hbm(table), links, order, *in_hbm(adjoint))
 
 
 def main_call(table, order, along_y, along_z, ends, links, flow, edges):
@@ -573,6 +624,7 @@
             pltpu.VMEM((fields, nx + 1, ny, nz), F32),
             pltpu.VMEM((2, fields * nx, nz), F32),
             pltpu.VMEM((fields, ny, 256), BF16),
+            *[pltpu.VMEM((fields, 2 * ny, nz), F32) for _ in range(6)],
             pltpu.SemaphoreType.DMA((ny // 16,)),
             pltpu.SemaphoreType.DMA((nx // 8, 4)),
             pltpu.SemaphoreType.DMA((nx // 8,)),

time: 62.9 us -> 61 us (0.970)
  Pallas kernels: 38.7 us -> 35 us
  local copies, waits for them, and re-layouts: 0.02 us -> 1.72 us
    pallas_call x1, Pallas kernels: 11.4 us -> 7.78 us  [gather_call(): pl.pallas_call(functools.partial(gather_kernel, fields), in_specs=[pl.Blo...]
    unnamed x10 -> x14, local copies, waits for them, and re-layouts: 0.02 us -> 1.72 us
where the time goes in v3:
time: 61 us; the launch traced here: 59.9 us
  Pallas kernels  35 us (57%)
  starting transfers between devices  17.6 us (29%)
  waiting for transfers between devices  5.48 us (9%)
  local copies, waits for them, and re-layouts  1.72 us (3%)
    pallas_call x1, Pallas kernels, main_call(): pl.pallas_call(functools.partial(main_kernel, fields), in_specs=[pl.Block...  27.3 us
    all_to_all x1, starting transfers between devices, body(): received = lax.all_to_all(send, 'blk', 0, 0)  8.6 us
    pallas_call x1, Pallas kernels, gather_call(): pl.pallas_call(functools.partial(gather_kernel, fields), in_specs=[pl.Blo...  7.78 us
    ppermute x1, waiting for transfers between devices, body(): lax.ppermute(far, 'ax', [(i, (i + 2) % pieces) for i in range(pieces)])  5.47 us
    ppermute x1, starting transfers between devices, body(): lax.ppermute(far, 'ax', [(i, (i + 2) % pieces) for i in range(pieces)])  4.11 us
    ppermute x1, starting transfers between devices, body(): lax.ppermute(right, 'ax', [(i, i + 1) for i in range(pieces - 1)])  3.55 us
    unnamed x14, local copies, waits for them, and re-layouts  1.72 us
    ppermute x1, starting transfers between devices, body(): lax.ppermute(left, 'ax', [(i + 1, i) for i in range(pieces - 1)])  1.29 us
  transfers between devices with their start and end apart: 4, of which 1 were waited for; matrix products, arithmetic and copies ran while one was open for 0% of the time, Pallas kernels for 0%

profile of v3, /device:TPU:1, one launch (start us, length us, event | category | flops | bytes accessed | tf_op | source)
XLA Modules:
  0.0 59.9 jit_solution(11370083713670140993)
XLA Ops:
  0.0 0.0 copy-start
  0.0 0.9 %copy-done = bf16[256,256]{1,0:T(8,128)(2,1)S(1)} copy-done((bf16[256,256]{1,0:T(8,128)(2,1)S(1)}, bf16[256,256]{1,0:T(8,128)(2,1)}, u32[]{:S(2)}) %copy-start) | copy-done | bytes 131096
  0.9 0.0 copy-start.2
  0.9 0.8 %copy-done.2 = s32[3,32,48]{2,1,0:T(8,128)S(1)} copy-done((s32[3,32,48]{2,1,0:T(8,128)S(1)}, s32[3,32,48]{2,1,0:T(8,128)}, u32[]{:S(2)}) %copy-start.2) | copy-done | bytes 18456
  1.7 0.0 copy-start.1
  1.7 0.0 copy-start.3
  1.7 0.0 copy-start.4
  1.7 0.0 copy-start.5
  1.7 0.0 copy-start.6
  1.7 7.8 %shard_map.109 = (bf16[32,16,384]{2,1,0:T(8,128)(2,1)}, bf16[5,3,64,128]{3,2,1,0:T(8,128)(2,1)S(1)}, bf16[5,3,64,128]{3,2,1,0:T(8,128)(2,1)S(1)}, bf16[5,64,128]...) custom-call(f32[4,144]{1,0:T(4,128)} %constant.12.clone.table, ...), custom_call_target="tpu_custom_call" | custom-call | flops 1000000000 | bytes 7000000 | tf_op jit(solution)/shard_map/pallas_call | solution.py:578
  9.5 8.6 %all-to-all-start = ((bf16[32,16,384]{2,1,0:T(8,128)(2,1)}), bf16[32,16,384]{2,1,0:T(8,128)(2,1)S(1)}, u32[]{:S(2)}, u32[]{:S(2)}) async-start(bf16[32,16,384]{2,1,0:T(8,128)(2,1)} %get-tuple-element.11), calls=%async_computation | async-start | bytes 786432 | tf_op jit(solution)/shard_map/all_to_all | solution.py:642
  18.1 3.6 %collective-permute-start = (bf16[5,3,64,128]{3,2,1,0:T(8,128)(2,1)S(1)}, bf16[5,3,64,128]{3,2,1,0:T(8,128)(2,1)S(1)}, u32[]{:S(2)}, u32[]{:S(2)}) collective-permute-start(bf16[5,3,64,128]{3,2,1,0:T(8,128)(2,1)S(1)} %get-tuple-element.12), channel_id=1, source_target_pairs={{0,1},{1,2},{2,3},{4,5},{5,6},{6,7},{8,9},{9,10},{10,11},{12,13},{... | collective-permute-start | bytes 737288 | tf_op jit(solution)/shard_map/ppermute | solution.py:644
  21.7 1.3 %collective-permute-start.1 = (bf16[5,3,64,128]{3,2,1,0:T(8,128)(2,1)S(1)}, bf16[5,3,64,128]{3,2,1,0:T(8,128)(2,1)S(1)}, u32[]{:S(2)}, u32[]{:S(2)}) collective-permute-start(bf16[5,3,64,128]{3,2,1,0:T(8,128)(2,1)S(1)} %get-tuple-element.13.own_left), channel_id=1, source_target_pairs={{1,0},{2,1},{3,2},{5,4},{6,5},{7,6},{9,8},{10,9},{11,10},{13,12},{... | collective-permute-start | bytes 737288 | tf_op jit(solution)/shard_map/ppermute | solution.py:645
  23.0 4.1 %collective-permute-start.2 = (bf16[5,64,128]{2,1,0:T(8,128)(2,1)S(1)}, bf16[5,64,128]{2,1,0:T(8,128)(2,1)S(1)}, u32[]{:S(2)}, u32[]{:S(2)}) collective-permute-start(bf16[5,64,128]{2,1,0:T(8,128)(2,1)S(1)} %get-tuple-element.14), channel_id=1, source_target_pairs={{0,2},{1,3},{2,0},{3,1},{4,6},{5,7},{6,4},{7,5},{8,10},{9,11},{10,... | collective-permute-start | bytes 245768 | tf_op jit(solution)/shard_map/ppermute | solution.py:646
  27.1 5.5 %collective-permute-done.2.far = bf16[5,64,128]{2,1,0:T(8,128)(2,1)S(1)} collective-permute-done((bf16[5,64,128]{2,1,0:T(8,128)(2,1)S(1)}, bf16[5,64,128]{2,1,0:T(8,128)(2,1)S(1)}, u32[]{:S(2)}, u32[]{:S(2)}) %collective-permute-start.2) | collective-permute-done | bytes 81952 | tf_op jit(solution)/shard_map/ppermute | solution.py:646
  32.6 0.0 collective-permute-done.right
  32.6 0.0 collective-permute-done.1.left
  32.6 0.0 all-to-all-done.received
  32.6 0.0 copy-done.1
  32.6 0.0 copy-done.3
  32.6 0.0 copy-done.4
  32.6 0.0 copy-done.5
  32.6 0.0 copy-done.6
  32.6 27.3 %shard_map.110 = bf16[5,1,64,64,128]{4,3,2,1,0:T(8,128)(2,1)} custom-call(f32[4,144]{1,0:T(4,128)} %constant.12.clone.table, s32[3,32,48]{2,1,0:T(8,128)S(1)} %copy-done.3, bf16[256,256]{1,0:T(8,128)(2,1)S(1)} %copy-done.1, bf16[64,128]{1,0:T(8,128)(2,1)S(1)} %copy-done.6, bf16[256,128]{1,0:T(8,128)(2,1)S(1)} %copy-done.5, bf16[256,128]{1,0:T(8,128)(2,1)S(1)} %copy-done.4, ...), custom_call_target="tpu_custom_call" | custom-call | flops 10000000000 | bytes 26000000 | tf_op jit(solution)/shard_map/pallas_call | solution.py:612
Async XLA Ops:
  0.0 0.9 %copy-start = (bf16[256,256]{1,0:T(8,128)(2,1)S(1)}, bf16[256,256]{1,0:T(8,128)(2,1)}, u32[]{:S(2)}) copy-start(bf16[256,256]{1,0:T(8,128)(2,1)} %constant.13.clone.order) | copy-start | bytes 393220
  0.9 0.8 %copy-start.2 = (s32[3,32,48]{2,1,0:T(8,128)S(1)}, s32[3,32,48]{2,1,0:T(8,128)}, u32[]{:S(2)}) copy-start(s32[3,32,48]{2,1,0:T(8,128)} %links.3) | copy-start | bytes 55300
  1.7 30.9 %copy-start.1 = (bf16[256,256]{1,0:T(8,128)(2,1)S(1)}, bf16[256,256]{1,0:T(8,128)(2,1)}, u32[]{:S(2)}) copy-start(bf16[256,256]{1,0:T(8,128)(2,1)} %constant.13.clone.order) | copy-start | bytes 393220
  1.7 30.9 %copy-start.3 = (s32[3,32,48]{2,1,0:T(8,128)S(1)}, s32[3,32,48]{2,1,0:T(8,128)}, u32[]{:S(2)}) copy-start(s32[3,32,48]{2,1,0:T(8,128)} %links.3) | copy-start | bytes 55300
  1.7 30.9 %copy-start.4 = (bf16[256,128]{1,0:T(8,128)(2,1)S(1)}, bf16[256,128]{1,0:T(8,128)(2,1)}, u32[]{:S(2)}) copy-start(bf16[256,128]{1,0:T(8,128)(2,1)} %constant.14.clone.ends) | copy-start | bytes 196612
  1.7 30.9 %copy-start.5 = (bf16[256,128]{1,0:T(8,128)(2,1)S(1)}, bf16[256,128]{1,0:T(8,128)(2,1)}, u32[]{:S(2)}) copy-start(bf16[256,128]{1,0:T(8,128)(2,1)} %constant.11.clone.along_z) | copy-start | bytes 196612
  1.7 30.9 %copy-start.6 = (bf16[64,128]{1,0:T(8,128)(2,1)S(1)}, bf16[64,128]{1,0:T(8,128)(2,1)}, u32[]{:S(2)}) copy-start(bf16[64,128]{1,0:T(8,128)(2,1)} %constant.10.clone.along_y) | copy-start | bytes 49156
  9.5 23.1 %all-to-all-start = ((bf16[32,16,384]{2,1,0:T(8,128)(2,1)}), bf16[32,16,384]{2,1,0:T(8,128)(2,1)S(1)}, u32[]{:S(2)}, u32[]{:S(2)}) async-start(bf16[32,16,384]{2,1,0:T(8,128)(2,1)} %get-tuple-element.11), calls=%async_computation | async-start | bytes 786432 | tf_op jit(solution)/shard_map/all_to_all | solution.py:642
  18.1 14.4 %collective-permute-start = (bf16[5,3,64,128]{3,2,1,0:T(8,128)(2,1)S(1)}, bf16[5,3,64,128]{3,2,1,0:T(8,128)(2,1)S(1)}, u32[]{:S(2)}, u32[]{:S(2)}) collective-permute-start(bf16[5,3,64,128]{3,2,1,0:T(8,128)(2,1)S(1)} %get-tuple-element.12), channel_id=1, source_target_pairs={{0,1},{1,2},{2,3},{4,5},{5,6},{6,7},{8,9},{9,10},{10,11},{12,13},{... | collective-permute-start | bytes 737288 | tf_op jit(solution)/shard_map/ppermute | solution.py:644
  21.7 10.9 %collective-permute-start.1 = (bf16[5,3,64,128]{3,2,1,0:T(8,128)(2,1)S(1)}, bf16[5,3,64,128]{3,2,1,0:T(8,128)(2,1)S(1)}, u32[]{:S(2)}, u32[]{:S(2)}) collective-permute-start(bf16[5,3,64,128]{3,2,1,0:T(8,128)(2,1)S(1)} %get-tuple-element.13.own_left), channel_id=1, source_target_pairs={{1,0},{2,1},{3,2},{5,4},{6,5},{7,6},{9,8},{10,9},{11,10},{13,12},{... | collective-permute-start | bytes 737288 | tf_op jit(solution)/shard_map/ppermute | solution.py:645
  23.0 9.6 %collective-permute-start.2 = (bf16[5,64,128]{2,1,0:T(8,128)(2,1)S(1)}, bf16[5,64,128]{2,1,0:T(8,128)(2,1)S(1)}, u32[]{:S(2)}, u32[]{:S(2)}) collective-permute-start(bf16[5,64,128]{2,1,0:T(8,128)(2,1)S(1)} %get-tuple-element.14), channel_id=1, source_target_pairs={{0,2},{1,3},{2,0},{3,1},{4,6},{5,7},{6,4},{7,5},{8,10},{9,11},{10,... | collective-permute-start | bytes 245768 | tf_op jit(solution)/shard_map/ppermute | solution.py:646

commit v4 on v3

--- a/solution.py
+++ b/solution.py
@@ -19,6 +19,7 @@
 BF16 = jnp.bfloat16
 MIB = 1 << 20
 BATCH = 32
+BLOCK = 16
 
 
 def dense(n):
@@ -98,6 +99,8 @@
         scalars[s, 12] = unit if s < 2 else 0.0
         last = PIVOT - ALPHA * ALPHA / PIVOT if s + 1 < pieces else PIVOT
         scalars[s, 13] = (1.0 - PIVOT / last) / MULT
+        scalars[s, 14] = 1.0 if s > 0 else 0.0
+        scalars[s, 15] = 1.0 if s + 1 < pieces else 0.0
     return np.concatenate([weights, scalars], axis=1).astype(np.float32)
 
 
@@ -111,10 +114,10 @@
 
 
 def end_table(nz):
-    table = np.zeros((256, nz), np.float32)
+    table = np.zeros((256, 2 * nz), np.float32)
     for half, sign in ((0, 1.0), (128, -1.0)):
-        table[half : half + 128 : 2, 0] = sign
-        table[half + 1 : half + 128 : 2, nz - 1] = sign
+        for lane, column in enumerate((0, 2 * nz - 1, nz, nz - 1)):
+            table[half + lane : half + 128 : 4, column] = sign
     return table.astype(jnp.bfloat16)
 
 
@@ -138,8 +141,8 @@
 def gather_kernel(
     fields,
     table,
-    links,
-    order,
+    links_hbm,
+    order_hbm,
     adjoint_hbm,
     send,
     right,
@@ -150,7 +153,10 @@
     f_ref,
     rows_y,
     chooser,
+    links,
+    order,
     field_sem,
+    small_sem,
 ):
     place = lax.axis_index("ax")
     nx, ny, nz = f_ref.shape[1:]
@@ -158,8 +164,13 @@
     def field_copy(f):
         return pltpu.make_async_copy(adjoint_hbm.at[f, 0], f_ref.at[f], field_sem.at[f])
 
+    links_copy = pltpu.make_async_copy(links_hbm, links, small_sem.at[0])
+    order_copy = pltpu.make_async_copy(order_hbm, order, small_sem.at[1])
+    links_copy.start()
     for f in range(fields):
         field_copy(f).start()
+    order_copy.start()
+    links_copy.wait()
 
     own = lax.axis_index("blk")
     source = links[0]
@@ -246,6 +257,7 @@
     for f in range(fields):
         face_z[f] = total[f * ny : f * ny + ny].astype(BF16)
 
+    order_copy.wait()
     for pair in range((fields + 1) // 2):
         one = 2 * pair
         if one + 1 < fields:
@@ -434,7 +446,7 @@
             left_first = left[f, 0, at, :].astype(F32)
             far_plane = far[f, at, :].astype(F32)
             low = (
-                right_fn
+                scalar(14) * right_fn
                 + scalar(4) * load(f, 0)
                 + scalar(5) * load(f, 1)
                 + scalar(6) * own_fn
@@ -443,15 +455,15 @@
                 + scalar(11) * far_plane
             )
             high = (
-                left_fn
+                scalar(15) * left_fn
                 + scalar(9) * load(f, nx - 1)
                 + scalar(10) * load(f, nx - 2)
                 + scalar(12) * far_plane
             )
             return (
                 low * inverse,
-                -far_coef * right_last,
-                far_coef * left_first,
+                (scalar(14) * -far_coef) * right_last,
+                (scalar(15) * far_coef) * left_first,
                 high * inverse,
             )
 
@@ -476,7 +488,7 @@
                     new.append((fm1, f0, fp1, fp2, d))
                 return tuple(new)
 
-            state = lax.fori_loop(2, nx - 2, forward, tuple(state), unroll=4)
+            state = lax.fori_loop(2, nx - 2, forward, tuple(state), unroll=10)
             for q, f in enumerate(members):
                 fm2, fm1, f0, fp1, d = state[q]
                 d = near * (fp1 - fm1) - far_coef * fm2 + edge[q][2] - MULT * d
@@ -489,32 +501,43 @@
     lax.fori_loop(0, bands, band, 0)
 
     lane = iota((rows, 256), 1)
-    row = iota((rows, nz), 0)
+    row = iota((BLOCK, nz), 0)
 
     def matmuls(h, parts):
         grad_y, grad_z, pens = parts
-        xs = (2 * h, 2 * h + 1)
-        masks = [(((lane + 1 - 2 * x) & 127) < 2).astype(F32).astype(BF16) for x in xs]
-        masks = [jnp.concatenate([mask] * (ny // rows), axis=0) for mask in masks]
-        for f in range(fields):
+        mask = (((lane + 1 - 4 * h) & 127) < 4).astype(F32).astype(BF16)
+        mask = jnp.concatenate([mask] * (ny // rows), axis=0)
+
+        def along_z_of(f):
             both = f_ref[f, pl.ds(2 * h, 2)].reshape(2 * ny, nz)
             grad_z[f] = dot(jnp.concatenate([both, both], axis=1), along_z[...])
-        for f in range(fields):
-            chosen = [pair_z[f] * mask for mask in masks]
-            pens[f] = dot(jnp.concatenate(chosen, axis=0), ends[...])
-        for f in range(fields):
-            wide = jnp.concatenate([f_ref[f, x] for x in xs], axis=1)
+
+        def pens_of(f):
+            got = dot(pair_z[f] * mask, ends[...])
+            pens[f, :ny, :] = got[:, :nz]
+            pens[f, ny:, :] = got[:, nz:]
+
+        def along_y_of(f):
+            wide = jnp.concatenate([f_ref[f, 2 * h], f_ref[f, 2 * h + 1]], axis=1)
             got = dot(along_y[...], jnp.concatenate([wide, wide], axis=0))
             grad_y[f, :ny, :] = got[:, :nz]
             grad_y[f, ny:, :] = got[:, nz:]
 
-    def two_cells(h, parts):
+        kinds = (along_z_of, pens_of, along_y_of)
+        return [functools.partial(kind, f) for kind in kinds for f in range(fields)]
+
+    def two_cells(h, parts, tasks):
         grad_y, grad_z, pens = parts
+        blocks = 2 * ny // BLOCK
+        number = 0
         for q in (1, 0):
             x = 2 * h + q
-            for y in range(0, ny, rows):
-                at = slice(y, y + rows)
-                here = slice(q * ny + y, q * ny + y + rows)
+            for y in range(0, ny, BLOCK):
+                number += 1
+                for task in tasks[len(tasks) * (number - 1) // blocks : len(tasks) * number // blocks]:
+                    task()
+                at = slice(y, y + BLOCK)
+                here = slice(q * ny + y, q * ny + y + BLOCK)
                 rho = density[x, at, :].astype(F32)
                 vel = [velocity[i, x, at, :].astype(F32) for i in range(3)]
                 press = HEAT * pressure[x, at, :].astype(F32)
@@ -535,13 +558,14 @@
                     if y == 0:
                         line_y = pen_y[0, pl.ds(f * nx + x, 1), :]
                         total = total + jnp.where(row == 0, line_y, 0.0)
-                    if y == ny - rows:
+                    if y == ny - BLOCK:
                         line_y = pen_y[1, pl.ds(f * nx + x, 1), :]
-                        total = total + jnp.where(row == rows - 1, line_y, 0.0)
+                        total = total + jnp.where(row == BLOCK - 1, line_y, 0.0)
                     out[f, x, at, :] = total.astype(BF16)
 
     now, later = (now_y, now_z, now_p), (later_y, later_z, later_p)
-    matmuls(nx // 2 - 1, now)
+    for task in matmuls(nx // 2 - 1, now):
+        task()
 
     def section(k, _):
         c = chunks - 1 - k
@@ -550,10 +574,8 @@
 
         def four_cells(i, s):
             h = (c + 1) * (chunk // 2) - 1 - 2 * i
-            matmuls(h - 1, later)
-            two_cells(h, now)
-            matmuls(jnp.maximum(h - 2, 0), now)
-            two_cells(h - 1, later)
+            two_cells(h, now, matmuls(h - 1, later))
+            two_cells(h - 1, later, matmuls(jnp.maximum(h - 2, 0), now))
             return s
 
         lax.fori_loop(0, chunk // 4, four_cells, 0)
@@ -577,12 +599,8 @@
     vmem = pl.BlockSpec(memory_space=pltpu.VMEM)
     return pl.pallas_call(
         functools.partial(gather_kernel, fields),
-        in_specs=[
-            pl.BlockSpec(memory_space=pltpu.SMEM),
-            vmem,
-            vmem,
-            pl.BlockSpec(memory_space=pltpu.HBM),
-        ],
+        in_specs=[pl.BlockSpec(memory_space=pltpu.SMEM)]
+        + [pl.BlockSpec(memory_space=pltpu.HBM)] * 3,
         out_specs=[vmem] * 6,
         out_shape=[
             shape((blocks, 16, lanes), BF16),
@@ -596,11 +614,14 @@
             pltpu.VMEM((fields, nx, ny, nz), BF16),
             pltpu.VMEM((nx, 2 * nz), F32),
             pltpu.VMEM((16 * blocks, PW * patches), BF16),
+            pltpu.VMEM(links.shape, jnp.int32),
+            pltpu.VMEM(order.shape, BF16),
             pltpu.SemaphoreType.DMA((fields,)),
+            pltpu.SemaphoreType.DMA((2,)),
         ],
         compiler_params=pltpu.CompilerParams(vmem_limit_bytes=24 * MIB),
         cost_estimate=pl.CostEstimate(flops=10**9, bytes_accessed=7 * 10**6, transcendentals=0),
-    )(*in_hbm(table), links, order, *in_hbm(adjoint))
+    )(*in_hbm(table, links, order, adjoint))
 
 
 def main_call(table, order, along_y, along_z, ends, links, flow, edges):
@@ -641,8 +662,8 @@
     send, right, left, far, face_y, face_z = gather_call(table, order, links, adjoint)
     received = lax.all_to_all(send, "blk", 0, 0)
     pieces = lax.axis_size("ax")
-    from_left = lax.ppermute(right, "ax", [(i, i + 1) for i in range(pieces - 1)])
-    from_right = lax.ppermute(left, "ax", [(i + 1, i) for i in range(pieces - 1)])
+    from_left = lax.ppermute(right, "ax", [(i, (i + 1) % pieces) for i in range(pieces)])
+    from_right = lax.ppermute(left, "ax", [((i + 1) % pieces, i) for i in range(pieces)])
     from_far = lax.ppermute(far, "ax", [(i, (i + 2) % pieces) for i in range(pieces)])
     flow = (adjoint, density, velocity, pressure, metrics)
     edges = (received, from_left, from_right, from_far, left, face_y, face_z)

time: 61 us -> 57.1 us (0.936); the launches traced: 59.9 us -> 56.8 us
  starting transfers between devices: 17.6 us -> 13.7 us
  waiting for transfers between devices: 5.48 us -> 7.5 us
  local copies, waits for them, and re-layouts: 1.72 us -> 0.02 us
    ppermute x1, starting transfers between devices: 4.11 us -> 1.22 us  [body(): lax.ppermute(far, 'ax', [(i, (i + 2) % pieces) for i in range(pieces)])]
    ppermute x1, waiting for transfers between devices: 5.47 us -> 7.49 us  [body(): lax.ppermute(far, 'ax', [(i, (i + 2) % pieces) for i in range(pieces)])]
    unnamed x14 -> x10, local copies, waits for them, and re-layouts: 1.72 us -> 0.02 us
    pallas_call x1, Pallas kernels: 7.78 us -> 8.79 us  [gather_call(): pl.pallas_call(functools.partial(gather_kernel, fields), in_specs=[pl.Blo...]
    ppermute x2, starting transfers between devices: 4.85 us -> 3.91 us  [the longest x1 2.2 us: body(): lax.ppermute(left, 'ax', [((i + 1) % pieces, i) for i in range(pieces)])]
where the time goes in v4:
time: 57.1 us; the launch traced here: 56.8 us
  Pallas kernels  35.5 us (62%)
  starting transfers between devices  13.7 us (24%)
  waiting for transfers between devices  7.5 us (13%)
    pallas_call x1, Pallas kernels, main_call(): pl.pallas_call(functools.partial(main_kernel, fields), in_specs=[pl.Block...  26.7 us
    pallas_call x1, Pallas kernels, gather_call(): pl.pallas_call(functools.partial(gather_kernel, fields), in_specs=[pl.Blo...  8.79 us
    all_to_all x1, starting transfers between devices, body(): received = lax.all_to_all(send, 'blk', 0, 0)  8.6 us
    ppermute x1, waiting for transfers between devices, body(): lax.ppermute(far, 'ax', [(i, (i + 2) % pieces) for i in range(pieces)])  7.49 us
    ppermute x1, starting transfers between devices, body(): lax.ppermute(left, 'ax', [((i + 1) % pieces, i) for i in range(pieces)])  2.2 us
    ppermute x1, starting transfers between devices, body(): lax.ppermute(right, 'ax', [(i, (i + 1) % pieces) for i in range(pieces)])  1.71 us
    ppermute x1, starting transfers between devices, body(): lax.ppermute(far, 'ax', [(i, (i + 2) % pieces) for i in range(pieces)])  1.22 us
  transfers between devices with their start and end apart: 4, of which 1 were waited for; matrix products, arithmetic and copies ran while one was open for 0% of the time, Pallas kernels for 0%

profile of v4, /device:TPU:1, one launch (start us, length us, event | category | flops | bytes accessed | tf_op | source)
XLA Modules:
  0.0 56.8 jit_solution(12621469073115432865)
XLA Ops:
  0.0 0.0 copy-start
  0.0 0.0 copy-start.2
  0.0 0.0 copy-start.3
  0.0 0.0 copy-start.4
  0.0 0.0 copy-start.1
  0.0 8.8 %shard_map.109 = (bf16[32,16,384]{2,1,0:T(8,128)(2,1)}, bf16[5,3,64,128]{3,2,1,0:T(8,128)(2,1)S(1)}, bf16[5,3,64,128]{3,2,1,0:T(8,128)(2,1)S(1)}, bf16[5,64,128]...) custom-call(f32[4,144]{1,0:T(4,128)} %constant.12.clone.table, ...), custom_call_target="tpu_custom_call" | custom-call | flops 1000000000 | bytes 7000000 | tf_op jit(solution)/shard_map/pallas_call | solution.py:600
  8.8 8.6 %all-to-all-start = ((bf16[32,16,384]{2,1,0:T(8,128)(2,1)}), bf16[32,16,384]{2,1,0:T(8,128)(2,1)S(1)}, u32[]{:S(2)}, u32[]{:S(2)}) async-start(bf16[32,16,384]{2,1,0:T(8,128)(2,1)} %get-tuple-element.11), calls=%async_computation | async-start | bytes 786432 | tf_op jit(solution)/shard_map/all_to_all | solution.py:663
  17.4 1.7 %collective-permute-start = (bf16[5,3,64,128]{3,2,1,0:T(8,128)(2,1)S(1)}, bf16[5,3,64,128]{3,2,1,0:T(8,128)(2,1)S(1)}, u32[]{:S(2)}, u32[]{:S(2)}) collective-permute-start(bf16[5,3,64,128]{3,2,1,0:T(8,128)(2,1)S(1)} %get-tuple-element.12), channel_id=1, source_target_pairs={{0,1},{1,2},{2,3},{3,0},{4,5},{5,6},{6,7},{7,4},{8,9},{9,10},{10,1... | collective-permute-start | bytes 737288 | tf_op jit(solution)/shard_map/ppermute | solution.py:665
  19.1 2.2 %collective-permute-start.1 = (bf16[5,3,64,128]{3,2,1,0:T(8,128)(2,1)S(1)}, bf16[5,3,64,128]{3,2,1,0:T(8,128)(2,1)S(1)}, u32[]{:S(2)}, u32[]{:S(2)}) collective-permute-start(bf16[5,3,64,128]{3,2,1,0:T(8,128)(2,1)S(1)} %get-tuple-element.13.own_left), channel_id=1, source_target_pairs={{1,0},{2,1},{3,2},{0,3},{5,4},{6,5},{7,6},{4,7},{9,8},{10,9},{11,1... | collective-permute-start | bytes 737288 | tf_op jit(solution)/shard_map/ppermute | solution.py:666
  21.4 1.2 %collective-permute-start.2 = (bf16[5,64,128]{2,1,0:T(8,128)(2,1)S(1)}, bf16[5,64,128]{2,1,0:T(8,128)(2,1)S(1)}, u32[]{:S(2)}, u32[]{:S(2)}) collective-permute-start(bf16[5,64,128]{2,1,0:T(8,128)(2,1)S(1)} %get-tuple-element.14), channel_id=1, source_target_pairs={{0,2},{1,3},{2,0},{3,1},{4,6},{5,7},{6,4},{7,5},{8,10},{9,11},{10,... | collective-permute-start | bytes 245768 | tf_op jit(solution)/shard_map/ppermute | solution.py:667
  22.6 7.5 %collective-permute-done.2.far = bf16[5,64,128]{2,1,0:T(8,128)(2,1)S(1)} collective-permute-done((bf16[5,64,128]{2,1,0:T(8,128)(2,1)S(1)}, bf16[5,64,128]{2,1,0:T(8,128)(2,1)S(1)}, u32[]{:S(2)}, u32[]{:S(2)}) %collective-permute-start.2) | collective-permute-done | bytes 81952 | tf_op jit(solution)/shard_map/ppermute | solution.py:667
  30.1 0.0 collective-permute-done.right
  30.1 0.0 collective-permute-done.1.left
  30.1 0.0 all-to-all-done.received
  30.1 0.0 copy-done
  30.1 0.0 copy-done.2
  30.1 0.0 copy-done.3
  30.1 0.0 copy-done.4
  30.1 0.0 copy-done.1
  30.1 26.7 %shard_map.110 = bf16[5,1,64,64,128]{4,3,2,1,0:T(8,128)(2,1)} custom-call(f32[4,144]{1,0:T(4,128)} %constant.12.clone.table, s32[3,32,48]{2,1,0:T(8,128)S(1)} %copy-done.1, bf16[256,256]{1,0:T(8,128)(2,1)S(1)} %copy-done, bf16[64,128]{1,0:T(8,128)(2,1)S(1)} %copy-done.4, bf16[256,128]{1,0:T(8,128)(2,1)S(1)} %copy-done.3, bf16[256,256]{1,0:T(8,128)(2,1)S(1)} %copy-done.2, ...), custom_call_target="tpu_custom_call" | custom-call | flops 10000000000 | bytes 26000000 | tf_op jit(solution)/shard_map/pallas_call | solution.py:633
Async XLA Ops:
  0.0 30.1 %copy-start = (bf16[256,256]{1,0:T(8,128)(2,1)S(1)}, bf16[256,256]{1,0:T(8,128)(2,1)}, u32[]{:S(2)}) copy-start(bf16[256,256]{1,0:T(8,128)(2,1)} %constant.13.clone.order_hbm.order) | copy-start | bytes 393220
  0.0 30.1 %copy-start.2 = (bf16[256,256]{1,0:T(8,128)(2,1)S(1)}, bf16[256,256]{1,0:T(8,128)(2,1)}, u32[]{:S(2)}) copy-start(bf16[256,256]{1,0:T(8,128)(2,1)} %constant.14.clone.ends) | copy-start | bytes 393220
  0.0 30.1 %copy-start.3 = (bf16[256,128]{1,0:T(8,128)(2,1)S(1)}, bf16[256,128]{1,0:T(8,128)(2,1)}, u32[]{:S(2)}) copy-start(bf16[256,128]{1,0:T(8,128)(2,1)} %constant.11.clone.along_z) | copy-start | bytes 196612
  0.0 30.1 %copy-start.4 = (bf16[64,128]{1,0:T(8,128)(2,1)S(1)}, bf16[64,128]{1,0:T(8,128)(2,1)}, u32[]{:S(2)}) copy-start(bf16[64,128]{1,0:T(8,128)(2,1)} %constant.10.clone.along_y) | copy-start | bytes 49156
  0.0 30.1 %copy-start.1 = (s32[3,32,48]{2,1,0:T(8,128)S(1)}, s32[3,32,48]{2,1,0:T(8,128)}, u32[]{:S(2)}) copy-start(s32[3,32,48]{2,1,0:T(8,128)} %links.1) | copy-start | bytes 55300
  8.8 21.2 %all-to-all-start = ((bf16[32,16,384]{2,1,0:T(8,128)(2,1)}), bf16[32,16,384]{2,1,0:T(8,128)(2,1)S(1)}, u32[]{:S(2)}, u32[]{:S(2)}) async-start(bf16[32,16,384]{2,1,0:T(8,128)(2,1)} %get-tuple-element.11), calls=%async_computation | async-start | bytes 786432 | tf_op jit(solution)/shard_map/all_to_all | solution.py:663
  17.4 12.6 %collective-permute-start = (bf16[5,3,64,128]{3,2,1,0:T(8,128)(2,1)S(1)}, bf16[5,3,64,128]{3,2,1,0:T(8,128)(2,1)S(1)}, u32[]{:S(2)}, u32[]{:S(2)}) collective-permute-start(bf16[5,3,64,128]{3,2,1,0:T(8,128)(2,1)S(1)} %get-tuple-element.12), channel_id=1, source_target_pairs={{0,1},{1,2},{2,3},{3,0},{4,5},{5,6},{6,7},{7,4},{8,9},{9,10},{10,1... | collective-permute-start | bytes 737288 | tf_op jit(solution)/shard_map/ppermute | solution.py:665
  19.1 10.9 %collective-permute-start.1 = (bf16[5,3,64,128]{3,2,1,0:T(8,128)(2,1)S(1)}, bf16[5,3,64,128]{3,2,1,0:T(8,128)(2,1)S(1)}, u32[]{:S(2)}, u32[]{:S(2)}) collective-permute-start(bf16[5,3,64,128]{3,2,1,0:T(8,128)(2,1)S(1)} %get-tuple-element.13.own_left), channel_id=1, source_target_pairs={{1,0},{2,1},{3,2},{0,3},{5,4},{6,5},{7,6},{4,7},{9,8},{10,9},{11,1... | collective-permute-start | bytes 737288 | tf_op jit(solution)/shard_map/ppermute | solution.py:666
  21.4 8.7 %collective-permute-start.2 = (bf16[5,64,128]{2,1,0:T(8,128)(2,1)S(1)}, bf16[5,64,128]{2,1,0:T(8,128)(2,1)S(1)}, u32[]{:S(2)}, u32[]{:S(2)}) collective-permute-start(bf16[5,64,128]{2,1,0:T(8,128)(2,1)S(1)} %get-tuple-element.14), channel_id=1, source_target_pairs={{0,2},{1,3},{2,0},{3,1},{4,6},{5,7},{6,4},{7,5},{8,10},{9,11},{10,... | collective-permute-start | bytes 245768 | tf_op jit(solution)/shard_map/ppermute | solution.py:667

commit v5 on v4

--- a/solution.py
+++ b/solution.py
@@ -20,6 +20,8 @@
 MIB = 1 << 20
 BATCH = 32
 BLOCK = 16
+READY = 24
+LATERAL_CHUNK = 8
 
 
 def dense(n):
@@ -288,6 +290,40 @@
     return terms if sums is None else [a + b for a, b in zip(sums, terms)]
 
 
+def lateral_kernel(fields, along_y, along_z, f_ref, density, velocity, pressure, ky, kz, out):
+    chunk, ny, nz = f_ref.shape[2:]
+
+    def body(h, _):
+        grads_y = []
+        grads_z = []
+        xs = (2 * h, 2 * h + 1)
+        for f in range(fields):
+            tiles = [f_ref[f, 0, x] for x in xs]
+            both = jnp.concatenate(tiles, axis=0)
+            grads_z.append(dot(jnp.concatenate([both, both], axis=1), along_z[...]))
+        for f in range(fields):
+            wide = jnp.concatenate([f_ref[f, 0, x] for x in xs], axis=1)
+            grads_y.append(dot(along_y[...], jnp.concatenate([wide, wide], axis=0)))
+        for q, x in enumerate(xs):
+            for y in range(0, ny, 16):
+                at = slice(y, y + 16)
+                rho = density[0, x, at, :].astype(F32)
+                vel = [velocity[i, 0, x, at, :].astype(F32) for i in range(3)]
+                press = HEAT * pressure[0, x, at, :].astype(F32)
+                gy = [g[at, q * nz : (q + 1) * nz] for g in grads_y]
+                gz = [g[q * ny + y : q * ny + y + 16] for g in grads_z]
+                sums = None
+                for g, k in ((gy, ky), (gz, kz)):
+                    metric = [k[i, 0, x, at, :].astype(F32) for i in range(3)]
+                    sums = flux(g, metric, rho, vel, press, sums)
+                for i in range(4):
+                    out[i, x, at, :] = sums[i]
+                out[4, x, at, :] = sums[4] + sums[5] / rho
+        return 0
+
+    lax.fori_loop(0, chunk // 2, body, 0)
+
+
 def penalty_parts(fields, nx, links, order, received, face_y, face_z, pen_y, pair_z):
     ny, nz = face_z.shape[1:]
     own = lax.axis_index("blk")
@@ -368,12 +404,14 @@
     velocity_hbm,
     pressure_hbm,
     metrics_hbm,
+    partial_hbm,
     out_hbm,
     f_ref,
     density,
     velocity,
     pressure,
     metrics,
+    partial,
     out,
     line,
     pen_y,
@@ -401,14 +439,24 @@
             adjoint_hbm.at[:, 0, :, at, :], f_ref.at[:, :, at, :], field_sem.at[c]
         )
 
-    def flow_copies(c):
+    ready = partial.shape[1] // chunk
+
+    def flow_copies(c, done):
         at = pl.ds(c * chunk, chunk)
-        return [
+        some = pl.ds(0, 3 if done else 9)
+        copies = [
             pltpu.make_async_copy(density_hbm.at[0, at], density.at[at], flow_sem.at[c, 0]),
             pltpu.make_async_copy(velocity_hbm.at[:, 0, at], velocity.at[:, at], flow_sem.at[c, 1]),
             pltpu.make_async_copy(pressure_hbm.at[0, at], pressure.at[at], flow_sem.at[c, 2]),
-            pltpu.make_async_copy(metrics_hbm.at[:, 0, at], metrics.at[:, at], flow_sem.at[c, 3]),
+            pltpu.make_async_copy(
+                metrics_hbm.at[some, 0, at], metrics.at[some, at], flow_sem.at[c, 3]
+            ),
         ]
+        if done:
+            copies.append(
+                pltpu.make_async_copy(partial_hbm.at[:, at], partial.at[:, at], flow_sem.at[c, 4])
+            )
+        return copies
 
     def out_copy(c):
         at = pl.ds(c * chunk, chunk)
@@ -417,7 +465,7 @@
     for c in range(bands):
         field_copy(c).start()
     for c in reversed(range(chunks)):
-        for copy in flow_copies(c):
+        for copy in flow_copies(c, c < ready):
             copy.start()
 
     penalty_parts(fields, nx, links, order, received, face_y, face_z, pen_y, pair_z)
@@ -503,7 +551,7 @@
     lane = iota((rows, 256), 1)
     row = iota((BLOCK, nz), 0)
 
-    def matmuls(h, parts):
+    def matmuls(h, parts, done=False):
         grad_y, grad_z, pens = parts
         mask = (((lane + 1 - 4 * h) & 127) < 4).astype(F32).astype(BF16)
         mask = jnp.concatenate([mask] * (ny // rows), axis=0)
@@ -523,10 +571,10 @@
             grad_y[f, :ny, :] = got[:, :nz]
             grad_y[f, ny:, :] = got[:, nz:]
 
-        kinds = (along_z_of, pens_of, along_y_of)
+        kinds = (pens_of,) if done else (along_z_of, pens_of, along_y_of)
         return [functools.partial(kind, f) for kind in kinds for f in range(fields)]
 
-    def two_cells(h, parts, tasks):
+    def two_cells(h, parts, tasks, done=False):
         grad_y, grad_z, pens = parts
         blocks = 2 * ny // BLOCK
         number = 0
@@ -546,15 +594,19 @@
                     value = line[f, x, at, :] - MULT * line[f, x + 1, at, :]
                     line[f, x, at, :] = value
                     gx.append(value)
-                gy = [grad_y[f, here, :] for f in range(fields)]
-                gz = [grad_z[f, here, :] for f in range(fields)]
+                grads = [gx]
+                if not done:
+                    grads.append([grad_y[f, here, :] for f in range(fields)])
+                    grads.append([grad_z[f, here, :] for f in range(fields)])
                 sums = None
-                for d, g in enumerate((gx, gy, gz)):
+                for d, g in enumerate(grads):
                     metric = [metrics[3 * d + i, x, at, :].astype(F32) for i in range(3)]
                     sums = flux(g, metric, rho, vel, press, sums)
                 sums[4] = sums[4] + sums[5] / rho
                 for f in range(fields):
                     total = sums[f] + pens[f, here, :]
+                    if done:
+                        total = total + partial[f, x, at, :]
                     if y == 0:
                         line_y = pen_y[0, pl.ds(f * nx + x, 1), :]
                         total = total + jnp.where(row == 0, line_y, 0.0)
@@ -567,22 +619,23 @@
     for task in matmuls(nx // 2 - 1, now):
         task()
 
-    def section(k, _):
+    def section(k, _, done=False):
         c = chunks - 1 - k
-        for copy in flow_copies(c):
+        for copy in flow_copies(c, done):
             copy.wait()
 
         def four_cells(i, s):
             h = (c + 1) * (chunk // 2) - 1 - 2 * i
-            two_cells(h, now, matmuls(h - 1, later))
-            two_cells(h - 1, later, matmuls(jnp.maximum(h - 2, 0), now))
+            two_cells(h, now, matmuls(h - 1, later, done), done)
+            two_cells(h - 1, later, matmuls(jnp.maximum(h - 2, 0), now, done), done)
             return s
 
         lax.fori_loop(0, chunk // 4, four_cells, 0)
         out_copy(c).start()
         return 0
 
-    lax.fori_loop(0, chunks, section, 0)
+    lax.fori_loop(0, chunks - ready, section, 0)
+    lax.fori_loop(chunks - ready, chunks, functools.partial(section, done=True), 0)
     for c in range(chunks):
         out_copy(c).wait()
 
@@ -624,7 +677,33 @@
     )(*in_hbm(table, links, order, adjoint))
 
 
-def main_call(table, order, along_y, along_z, ends, links, flow, edges):
+def lateral_call(along_y, along_z, adjoint, density, velocity, pressure, metrics):
+    fields, _, nx, ny, nz = adjoint.shape
+    chunk = LATERAL_CHUNK
+    fixed = (lambda i: (0, 0))
+    return pl.pallas_call(
+        functools.partial(lateral_kernel, fields),
+        grid=(READY // chunk,),
+        in_specs=[
+            pl.BlockSpec(along_y.shape, fixed),
+            pl.BlockSpec(along_z.shape, fixed),
+            pl.BlockSpec((fields, 1, chunk, ny, nz), lambda i: (0, 0, i, 0, 0)),
+            pl.BlockSpec((1, chunk, ny, nz), lambda i: (0, i, 0, 0)),
+            pl.BlockSpec((3, 1, chunk, ny, nz), lambda i: (0, 0, i, 0, 0)),
+            pl.BlockSpec((1, chunk, ny, nz), lambda i: (0, i, 0, 0)),
+            pl.BlockSpec((3, 1, chunk, ny, nz), lambda i: (1, 0, i, 0, 0)),
+            pl.BlockSpec((3, 1, chunk, ny, nz), lambda i: (2, 0, i, 0, 0)),
+        ],
+        out_specs=pl.BlockSpec((fields, chunk, ny, nz), lambda i: (0, i, 0, 0)),
+        out_shape=pltpu.HBM((fields, READY, ny, nz), F32),
+        compiler_params=pltpu.CompilerParams(vmem_limit_bytes=24 * MIB),
+        cost_estimate=pl.CostEstimate(
+            flops=10**10, bytes_accessed=27 * 10**6, transcendentals=0
+        ),
+    )(*in_hbm(along_y, along_z, adjoint, density, velocity, pressure, metrics, metrics))
+
+
+def main_call(table, order, along_y, along_z, ends, links, flow, partial, edges):
     adjoint = flow[0]
     fields, _, nx, ny, nz = adjoint.shape
     vmem = pl.BlockSpec(memory_space=pltpu.VMEM)
@@ -632,7 +711,9 @@
     small = [links, order, along_y, along_z, ends, *edges]
     return pl.pallas_call(
         functools.partial(main_kernel, fields),
-        in_specs=[pl.BlockSpec(memory_space=pltpu.SMEM)] + [vmem] * len(small) + [hbm] * len(flow),
+        in_specs=[pl.BlockSpec(memory_space=pltpu.SMEM)]
+        + [vmem] * len(small)
+        + [hbm] * (len(flow) + 1),
         out_specs=hbm,
         out_shape=jax.ShapeDtypeStruct(adjoint.shape, BF16),
         scratch_shapes=[
@@ -641,20 +722,21 @@
             pltpu.VMEM((3, nx, ny, nz), BF16),
             pltpu.VMEM((nx, ny, nz), BF16),
             pltpu.VMEM((9, nx, ny, nz), BF16),
+            pltpu.VMEM(partial.shape, F32),
             pltpu.VMEM((fields, nx, ny, nz), BF16),
             pltpu.VMEM((fields, nx + 1, ny, nz), F32),
             pltpu.VMEM((2, fields * nx, nz), F32),
             pltpu.VMEM((fields, ny, 256), BF16),
             *[pltpu.VMEM((fields, 2 * ny, nz), F32) for _ in range(6)],
             pltpu.SemaphoreType.DMA((ny // 16,)),
-            pltpu.SemaphoreType.DMA((nx // 8, 4)),
+            pltpu.SemaphoreType.DMA((nx // 8, 5)),
             pltpu.SemaphoreType.DMA((nx // 8,)),
         ],
         compiler_params=pltpu.CompilerParams(vmem_limit_bytes=52 * MIB),
         cost_estimate=pl.CostEstimate(
             flops=10**10, bytes_accessed=26 * 10**6, transcendentals=0
         ),
-    )(*in_hbm(table), *small, *in_hbm(*flow))
+    )(*in_hbm(table), *small, *in_hbm(*flow, partial))
 
 
 def body(tables, adjoint, density, velocity, pressure, metrics, links):
@@ -666,8 +748,9 @@
     from_right = lax.ppermute(left, "ax", [((i + 1) % pieces, i) for i in range(pieces)])
     from_far = lax.ppermute(far, "ax", [(i, (i + 2) % pieces) for i in range(pieces)])
     flow = (adjoint, density, velocity, pressure, metrics)
+    partial = lateral_call(along_y, along_z, *flow)
     edges = (received, from_left, from_right, from_far, left, face_y, face_z)
-    return main_call(table, order, along_y, along_z, ends, links, flow, edges)
+    return main_call(table, order, along_y, along_z, ends, links, flow, partial, edges)
 
 
 def solution(mesh):

time: 57.1 us -> 55.5 us (0.972)
  waiting for transfers between devices: 7.5 us -> 0.01 us
  Pallas kernels: 35.5 us -> 40 us
  starting transfers between devices: 13.7 us -> 15 us
    ppermute x1, waiting for transfers between devices: 7.49 us -> 0.01 us  [body(): lax.ppermute(far, 'ax', [(i, (i + 2) % pieces) for i in range(pieces)])]
    pallas_call x0 -> x1, Pallas kernels: none -> 7.25 us  [lateral_call(): pl.pallas_call(functools.partial(lateral_kernel, fields), grid=(READY //...]
    pallas_call x1, Pallas kernels: 26.7 us -> 24.1 us  [main_call(): pl.pallas_call(functools.partial(main_kernel, fields), in_specs=[pl.Block...]
    ppermute x1, starting transfers between devices: 1.22 us -> 3.68 us  [body(): lax.ppermute(far, 'ax', [(i, (i + 2) % pieces) for i in range(pieces)])]
    ppermute x1, starting transfers between devices: 1.71 us -> 0.74 us  [body(): lax.ppermute(right, 'ax', [(i, (i + 1) % pieces) for i in range(pieces)])]
  transfers between devices with their start and end apart: 4 -> 4, of which waited for: 1 -> 0; matrix products, arithmetic and copies ran while one was open for 0% -> 0% of each run, Pallas kernels for 0% -> 13%
where the time goes in v5:
time: 55.5 us; the launch traced here: 55.2 us
  Pallas kernels  40 us (72%)
  starting transfers between devices  15 us (27%)
    pallas_call x1, Pallas kernels, main_call(): pl.pallas_call(functools.partial(main_kernel, fields), in_specs=[pl.Block...  24.1 us
    pallas_call x1, Pallas kernels, gather_call(): pl.pallas_call(functools.partial(gather_kernel, fields), in_specs=[pl.Blo...  8.65 us
    all_to_all x1, starting transfers between devices, body(): received = lax.all_to_all(send, 'blk', 0, 0)  8.6 us
    pallas_call x1, Pallas kernels, lateral_call(): pl.pallas_call(functools.partial(lateral_kernel, fields), grid=(READY //...  7.25 us
    ppermute x1, starting transfers between devices, body(): lax.ppermute(far, 'ax', [(i, (i + 2) % pieces) for i in range(pieces)])  3.68 us
    ppermute x1, starting transfers between devices, body(): lax.ppermute(left, 'ax', [((i + 1) % pieces, i) for i in range(pieces)])  2 us
  transfers between devices with their start and end apart: 4, of which 0 were waited for; matrix products, arithmetic and copies ran while one was open for 0% of the time, Pallas kernels for 13%

profile of v5, /device:TPU:1, one launch (start us, length us, event | category | flops | bytes accessed | tf_op | source)
XLA Modules:
  0.0 55.2 jit_solution(8595095975122724180)
XLA Ops:
  0.0 8.7 %shard_map.109 = (bf16[32,16,384]{2,1,0:T(8,128)(2,1)}, bf16[5,3,64,128]{3,2,1,0:T(8,128)(2,1)S(1)}, bf16[5,3,64,128]{3,2,1,0:T(8,128)(2,1)S(1)}, bf16[5,64,128]...) custom-call(f32[4,144]{1,0:T(4,128)} %constant.12.clone.table, ...), custom_call_target="tpu_custom_call" | custom-call | flops 1000000000 | bytes 7000000 | tf_op jit(solution)/shard_map/pallas_call | solution.py:653
  8.7 8.6 %all-to-all-start = ((bf16[32,16,384]{2,1,0:T(8,128)(2,1)}), bf16[32,16,384]{2,1,0:T(8,128)(2,1)S(1)}, u32[]{:S(2)}, u32[]{:S(2)}) async-start(bf16[32,16,384]{2,1,0:T(8,128)(2,1)} %get-tuple-element.11), calls=%async_computation | async-start | bytes 786432 | tf_op jit(solution)/shard_map/all_to_all | solution.py:745
  17.3 3.7 %collective-permute-start.2 = (bf16[5,64,128]{2,1,0:T(8,128)(2,1)S(1)}, bf16[5,64,128]{2,1,0:T(8,128)(2,1)S(1)}, u32[]{:S(2)}, u32[]{:S(2)}) collective-permute-start(bf16[5,64,128]{2,1,0:T(8,128)(2,1)S(1)} %get-tuple-element.14), channel_id=1, source_target_pairs={{0,2},{1,3},{2,0},{3,1},{4,6},{5,7},{6,4},{7,5},{8,10},{9,11},{10,... | collective-permute-start | bytes 245768 | tf_op jit(solution)/shard_map/ppermute | solution.py:749
  20.9 0.7 %collective-permute-start = (bf16[5,3,64,128]{3,2,1,0:T(8,128)(2,1)S(1)}, bf16[5,3,64,128]{3,2,1,0:T(8,128)(2,1)S(1)}, u32[]{:S(2)}, u32[]{:S(2)}) collective-permute-start(bf16[5,3,64,128]{3,2,1,0:T(8,128)(2,1)S(1)} %get-tuple-element.12), channel_id=1, source_target_pairs={{0,1},{1,2},{2,3},{3,0},{4,5},{5,6},{6,7},{7,4},{8,9},{9,10},{10,1... | collective-permute-start | bytes 737288 | tf_op jit(solution)/shard_map/ppermute | solution.py:747
  21.7 0.0 copy-start
  21.7 0.0 copy-start.1
  21.7 0.0 copy-start.2
  21.7 0.0 copy-start.3
  21.7 0.0 copy-start.4
  21.7 2.0 %collective-permute-start.1 = (bf16[5,3,64,128]{3,2,1,0:T(8,128)(2,1)S(1)}, bf16[5,3,64,128]{3,2,1,0:T(8,128)(2,1)S(1)}, u32[]{:S(2)}, u32[]{:S(2)}) collective-permute-start(bf16[5,3,64,128]{3,2,1,0:T(8,128)(2,1)S(1)} %get-tuple-element.13.own_left), channel_id=1, source_target_pairs={{1,0},{2,1},{3,2},{0,3},{5,4},{6,5},{7,6},{4,7},{9,8},{10,9},{11,1... | collective-permute-start | bytes 737288 | tf_op jit(solution)/shard_map/ppermute | solution.py:748
  23.7 7.3 %shard_map.110.partial_hbm = f32[5,24,64,128]{3,2,1,0:T(8,128)} custom-call(bf16[64,128]{1,0:T(8,128)(2,1)} %constant.10.clone.along_y, bf16[256,128]{1,0:T(8,128)(2,1)} %constant.11.clone.along_z, bf16[5,1,64,64,128]{4,3,2,1,0:T(8,128)(2,1)} %adjoint_hbm.3, bf16[1,64,64,128]{3,2,1,0:T(8,128)(2,1)} %density_hbm.1, bf16[3,1,64,64,128]{4,3,2,1,0:T(8,128)(2,1)} %velocity_hbm.1, ...), custom_call_target="tpu_custom_call" | custom-call | flops 10000000000 | bytes 27000000 | tf_op jit(solution)/shard_map/pallas_call | solution.py:684
  31.0 0.0 collective-permute-done.2.far
  31.0 0.0 collective-permute-done.right
  31.0 0.0 collective-permute-done.1.left
  31.0 0.0 all-to-all-done.received
  31.0 0.0 copy-done
  31.0 0.0 copy-done.1
  31.0 0.0 copy-done.2
  31.0 0.0 copy-done.3
  31.0 0.0 copy-done.4
  31.1 24.1 %shard_map.111 = bf16[5,1,64,64,128]{4,3,2,1,0:T(8,128)(2,1)} custom-call(f32[4,144]{1,0:T(4,128)} %constant.12.clone.table, s32[3,32,48]{2,1,0:T(8,128)S(1)} %copy-done.1, bf16[256,256]{1,0:T(8,128)(2,1)S(1)} %copy-done, bf16[64,128]{1,0:T(8,128)(2,1)S(1)} %copy-done.4, bf16[256,128]{1,0:T(8,128)(2,1)S(1)} %copy-done.3, bf16[256,256]{1,0:T(8,128)(2,1)S(1)} %copy-done.2, ...), custom_call_target="tpu_custom_call" | custom-call | flops 10000000000 | bytes 26000000 | tf_op jit(solution)/shard_map/pallas_call | solution.py:712
Async XLA Ops:
  8.7 22.3 %all-to-all-start = ((bf16[32,16,384]{2,1,0:T(8,128)(2,1)}), bf16[32,16,384]{2,1,0:T(8,128)(2,1)S(1)}, u32[]{:S(2)}, u32[]{:S(2)}) async-start(bf16[32,16,384]{2,1,0:T(8,128)(2,1)} %get-tuple-element.11), calls=%async_computation | async-start | bytes 786432 | tf_op jit(solution)/shard_map/all_to_all | solution.py:745
  17.3 13.7 %collective-permute-start.2 = (bf16[5,64,128]{2,1,0:T(8,128)(2,1)S(1)}, bf16[5,64,128]{2,1,0:T(8,128)(2,1)S(1)}, u32[]{:S(2)}, u32[]{:S(2)}) collective-permute-start(bf16[5,64,128]{2,1,0:T(8,128)(2,1)S(1)} %get-tuple-element.14), channel_id=1, source_target_pairs={{0,2},{1,3},{2,0},{3,1},{4,6},{5,7},{6,4},{7,5},{8,10},{9,11},{10,... | collective-permute-start | bytes 245768 | tf_op jit(solution)/shard_map/ppermute | solution.py:749
  20.9 10.0 %collective-permute-start = (bf16[5,3,64,128]{3,2,1,0:T(8,128)(2,1)S(1)}, bf16[5,3,64,128]{3,2,1,0:T(8,128)(2,1)S(1)}, u32[]{:S(2)}, u32[]{:S(2)}) collective-permute-start(bf16[5,3,64,128]{3,2,1,0:T(8,128)(2,1)S(1)} %get-tuple-element.12), channel_id=1, source_target_pairs={{0,1},{1,2},{2,3},{3,0},{4,5},{5,6},{6,7},{7,4},{8,9},{9,10},{10,1... | collective-permute-start | bytes 737288 | tf_op jit(solution)/shard_map/ppermute | solution.py:747
  21.7 9.3 %copy-start = (bf16[256,256]{1,0:T(8,128)(2,1)S(1)}, bf16[256,256]{1,0:T(8,128)(2,1)}, u32[]{:S(2)}) copy-start(bf16[256,256]{1,0:T(8,128)(2,1)} %constant.13.clone.order_hbm.order) | copy-start | bytes 393220
  21.7 9.3 %copy-start.1 = (s32[3,32,48]{2,1,0:T(8,128)S(1)}, s32[3,32,48]{2,1,0:T(8,128)}, u32[]{:S(2)}) copy-start(s32[3,32,48]{2,1,0:T(8,128)} %links.1) | copy-start | bytes 55300
  21.7 9.3 %copy-start.2 = (bf16[256,256]{1,0:T(8,128)(2,1)S(1)}, bf16[256,256]{1,0:T(8,128)(2,1)}, u32[]{:S(2)}) copy-start(bf16[256,256]{1,0:T(8,128)(2,1)} %constant.14.clone.ends) | copy-start | bytes 393220
  21.7 9.3 %copy-start.3 = (bf16[256,128]{1,0:T(8,128)(2,1)S(1)}, bf16[256,128]{1,0:T(8,128)(2,1)}, u32[]{:S(2)}) copy-start(bf16[256,128]{1,0:T(8,128)(2,1)} %constant.11.clone.along_z) | copy-start | bytes 196612
  21.7 9.3 %copy-start.4 = (bf16[64,128]{1,0:T(8,128)(2,1)S(1)}, bf16[64,128]{1,0:T(8,128)(2,1)}, u32[]{:S(2)}) copy-start(bf16[64,128]{1,0:T(8,128)(2,1)} %constant.10.clone.along_y) | copy-start | bytes 49156
  21.7 9.3 %collective-permute-start.1 = (bf16[5,3,64,128]{3,2,1,0:T(8,128)(2,1)S(1)}, bf16[5,3,64,128]{3,2,1,0:T(8,128)(2,1)S(1)}, u32[]{:S(2)}, u32[]{:S(2)}) collective-permute-start(bf16[5,3,64,128]{3,2,1,0:T(8,128)(2,1)S(1)} %get-tuple-element.13.own_left), channel_id=1, source_target_pairs={{1,0},{2,1},{3,2},{0,3},{5,4},{6,5},{7,6},{4,7},{9,8},{10,9},{11,1... | collective-permute-start | bytes 737288 | tf_op jit(solution)/shard_map/ppermute | solution.py:748

commit v6 on v5

--- a/solution.py
+++ b/solution.py
@@ -21,7 +21,7 @@
 BATCH = 32
 BLOCK = 16
 READY = 24
-LATERAL_CHUNK = 8
+LATERAL_CHUNK = 12
 
 
 def dense(n):
@@ -220,7 +220,7 @@
             return to_right, to_left
 
         zero = jnp.zeros((ny, nz), F32)
-        to_right, to_left = lax.fori_loop(0, nx // 8, group, (zero, zero))
+        to_right, to_left = lax.fori_loop(0, nx // 8, group, (zero, zero), unroll=2)
         first = f_ref[f, 0]
         last = f_ref[f, nx - 1]
         right[f, 0] = last
@@ -630,7 +630,7 @@
             two_cells(h - 1, later, matmuls(jnp.maximum(h - 2, 0), now, done), done)
             return s
 
-        lax.fori_loop(0, chunk // 4, four_cells, 0)
+        lax.fori_loop(0, chunk // 4, four_cells, 0, unroll=2)
         out_copy(c).start()
         return 0
 

time: 55.5 us -> 55.1 us (level)
  no operation moved by 1% of the time
where the time goes in v6:
time: 55.1 us; the launch traced here: 54.9 us
  Pallas kernels  39.7 us (72%)
  starting transfers between devices  15 us (27%)
    pallas_call x1, Pallas kernels, main_call(): pl.pallas_call(functools.partial(main_kernel, fields), in_specs=[pl.Block...  24.1 us
    all_to_all x1, starting transfers between devices, body(): received = lax.all_to_all(send, 'blk', 0, 0)  8.6 us
    pallas_call x1, Pallas kernels, gather_call(): pl.pallas_call(functools.partial(gather_kernel, fields), in_specs=[pl.Blo...  8.48 us
    pallas_call x1, Pallas kernels, lateral_call(): pl.pallas_call(functools.partial(lateral_kernel, fields), grid=(READY //...  7.15 us
    ppermute x1, starting transfers between devices, body(): lax.ppermute(far, 'ax', [(i, (i + 2) % pieces) for i in range(pieces)])  3.68 us
    ppermute x1, starting transfers between devices, body(): lax.ppermute(left, 'ax', [((i + 1) % pieces, i) for i in range(pieces)])  2 us
  transfers between devices with their start and end apart: 4, of which 0 were waited for; matrix products, arithmetic and copies ran while one was open for 0% of the time, Pallas kernels for 13%

profile of v6, /device:TPU:1, one launch (start us, length us, event | category | flops | bytes accessed | tf_op | source)
XLA Modules:
  0.0 54.9 jit_solution(12796710808568933957)
XLA Ops:
  0.0 8.5 %shard_map.109 = (bf16[32,16,384]{2,1,0:T(8,128)(2,1)}, bf16[5,3,64,128]{3,2,1,0:T(8,128)(2,1)S(1)}, bf16[5,3,64,128]{3,2,1,0:T(8,128)(2,1)S(1)}, bf16[5,64,128]...) custom-call(f32[4,144]{1,0:T(4,128)} %constant.12.clone.table, ...), custom_call_target="tpu_custom_call" | custom-call | flops 1000000000 | bytes 7000000 | tf_op jit(solution)/shard_map/pallas_call | solution.py:653
  8.5 8.6 %all-to-all-start = ((bf16[32,16,384]{2,1,0:T(8,128)(2,1)}), bf16[32,16,384]{2,1,0:T(8,128)(2,1)S(1)}, u32[]{:S(2)}, u32[]{:S(2)}) async-start(bf16[32,16,384]{2,1,0:T(8,128)(2,1)} %get-tuple-element.11), calls=%async_computation | async-start | bytes 786432 | tf_op jit(solution)/shard_map/all_to_all | solution.py:745
  17.1 3.7 %collective-permute-start.2 = (bf16[5,64,128]{2,1,0:T(8,128)(2,1)S(1)}, bf16[5,64,128]{2,1,0:T(8,128)(2,1)S(1)}, u32[]{:S(2)}, u32[]{:S(2)}) collective-permute-start(bf16[5,64,128]{2,1,0:T(8,128)(2,1)S(1)} %get-tuple-element.14), channel_id=1, source_target_pairs={{0,2},{1,3},{2,0},{3,1},{4,6},{5,7},{6,4},{7,5},{8,10},{9,11},{10,... | collective-permute-start | bytes 245768 | tf_op jit(solution)/shard_map/ppermute | solution.py:749
  20.8 0.7 %collective-permute-start = (bf16[5,3,64,128]{3,2,1,0:T(8,128)(2,1)S(1)}, bf16[5,3,64,128]{3,2,1,0:T(8,128)(2,1)S(1)}, u32[]{:S(2)}, u32[]{:S(2)}) collective-permute-start(bf16[5,3,64,128]{3,2,1,0:T(8,128)(2,1)S(1)} %get-tuple-element.12), channel_id=1, source_target_pairs={{0,1},{1,2},{2,3},{3,0},{4,5},{5,6},{6,7},{7,4},{8,9},{9,10},{10,1... | collective-permute-start | bytes 737288 | tf_op jit(solution)/shard_map/ppermute | solution.py:747
  21.5 0.0 copy-start
  21.5 0.0 copy-start.1
  21.5 0.0 copy-start.2
  21.5 0.0 copy-start.3
  21.5 0.0 copy-start.4
  21.5 2.0 %collective-permute-start.1 = (bf16[5,3,64,128]{3,2,1,0:T(8,128)(2,1)S(1)}, bf16[5,3,64,128]{3,2,1,0:T(8,128)(2,1)S(1)}, u32[]{:S(2)}, u32[]{:S(2)}) collective-permute-start(bf16[5,3,64,128]{3,2,1,0:T(8,128)(2,1)S(1)} %get-tuple-element.13.own_left), channel_id=1, source_target_pairs={{1,0},{2,1},{3,2},{0,3},{5,4},{6,5},{7,6},{4,7},{9,8},{10,9},{11,1... | collective-permute-start | bytes 737288 | tf_op jit(solution)/shard_map/ppermute | solution.py:748
  23.5 7.2 %shard_map.110.partial_hbm = f32[5,24,64,128]{3,2,1,0:T(8,128)} custom-call(bf16[64,128]{1,0:T(8,128)(2,1)} %constant.10.clone.along_y, bf16[256,128]{1,0:T(8,128)(2,1)} %constant.11.clone.along_z, bf16[5,1,64,64,128]{4,3,2,1,0:T(8,128)(2,1)} %adjoint_hbm.3, bf16[1,64,64,128]{3,2,1,0:T(8,128)(2,1)} %density_hbm.1, bf16[3,1,64,64,128]{4,3,2,1,0:T(8,128)(2,1)} %velocity_hbm.1, ...), custom_call_target="tpu_custom_call" | custom-call | flops 10000000000 | bytes 27000000 | tf_op jit(solution)/shard_map/pallas_call | solution.py:684
  30.7 0.0 collective-permute-done.2.far
  30.7 0.0 collective-permute-done.right
  30.7 0.0 collective-permute-done.1.left
  30.7 0.0 all-to-all-done.received
  30.7 0.0 copy-done
  30.7 0.0 copy-done.1
  30.8 0.0 copy-done.2
  30.8 0.0 copy-done.3
  30.8 0.0 copy-done.4
  30.8 24.1 %shard_map.111 = bf16[5,1,64,64,128]{4,3,2,1,0:T(8,128)(2,1)} custom-call(f32[4,144]{1,0:T(4,128)} %constant.12.clone.table, s32[3,32,48]{2,1,0:T(8,128)S(1)} %copy-done.1, bf16[256,256]{1,0:T(8,128)(2,1)S(1)} %copy-done, bf16[64,128]{1,0:T(8,128)(2,1)S(1)} %copy-done.4, bf16[256,128]{1,0:T(8,128)(2,1)S(1)} %copy-done.3, bf16[256,256]{1,0:T(8,128)(2,1)S(1)} %copy-done.2, ...), custom_call_target="tpu_custom_call" | custom-call | flops 10000000000 | bytes 26000000 | tf_op jit(solution)/shard_map/pallas_call | solution.py:712
Async XLA Ops:
  8.5 22.2 %all-to-all-start = ((bf16[32,16,384]{2,1,0:T(8,128)(2,1)}), bf16[32,16,384]{2,1,0:T(8,128)(2,1)S(1)}, u32[]{:S(2)}, u32[]{:S(2)}) async-start(bf16[32,16,384]{2,1,0:T(8,128)(2,1)} %get-tuple-element.11), calls=%async_computation | async-start | bytes 786432 | tf_op jit(solution)/shard_map/all_to_all | solution.py:745
  17.1 13.6 %collective-permute-start.2 = (bf16[5,64,128]{2,1,0:T(8,128)(2,1)S(1)}, bf16[5,64,128]{2,1,0:T(8,128)(2,1)S(1)}, u32[]{:S(2)}, u32[]{:S(2)}) collective-permute-start(bf16[5,64,128]{2,1,0:T(8,128)(2,1)S(1)} %get-tuple-element.14), channel_id=1, source_target_pairs={{0,2},{1,3},{2,0},{3,1},{4,6},{5,7},{6,4},{7,5},{8,10},{9,11},{10,... | collective-permute-start | bytes 245768 | tf_op jit(solution)/shard_map/ppermute | solution.py:749
  20.8 9.9 %collective-permute-start = (bf16[5,3,64,128]{3,2,1,0:T(8,128)(2,1)S(1)}, bf16[5,3,64,128]{3,2,1,0:T(8,128)(2,1)S(1)}, u32[]{:S(2)}, u32[]{:S(2)}) collective-permute-start(bf16[5,3,64,128]{3,2,1,0:T(8,128)(2,1)S(1)} %get-tuple-element.12), channel_id=1, source_target_pairs={{0,1},{1,2},{2,3},{3,0},{4,5},{5,6},{6,7},{7,4},{8,9},{9,10},{10,1... | collective-permute-start | bytes 737288 | tf_op jit(solution)/shard_map/ppermute | solution.py:747
  21.5 9.2 %copy-start = (bf16[256,256]{1,0:T(8,128)(2,1)S(1)}, bf16[256,256]{1,0:T(8,128)(2,1)}, u32[]{:S(2)}) copy-start(bf16[256,256]{1,0:T(8,128)(2,1)} %constant.13.clone.order_hbm.order) | copy-start | bytes 393220
  21.5 9.2 %copy-start.1 = (s32[3,32,48]{2,1,0:T(8,128)S(1)}, s32[3,32,48]{2,1,0:T(8,128)}, u32[]{:S(2)}) copy-start(s32[3,32,48]{2,1,0:T(8,128)} %links.1) | copy-start | bytes 55300
  21.5 9.2 %copy-start.2 = (bf16[256,256]{1,0:T(8,128)(2,1)S(1)}, bf16[256,256]{1,0:T(8,128)(2,1)}, u32[]{:S(2)}) copy-start(bf16[256,256]{1,0:T(8,128)(2,1)} %constant.14.clone.ends) | copy-start | bytes 393220
  21.5 9.2 %copy-start.3 = (bf16[256,128]{1,0:T(8,128)(2,1)S(1)}, bf16[256,128]{1,0:T(8,128)(2,1)}, u32[]{:S(2)}) copy-start(bf16[256,128]{1,0:T(8,128)(2,1)} %constant.11.clone.along_z) | copy-start | bytes 196612
  21.5 9.3 %copy-start.4 = (bf16[64,128]{1,0:T(8,128)(2,1)S(1)}, bf16[64,128]{1,0:T(8,128)(2,1)}, u32[]{:S(2)}) copy-start(bf16[64,128]{1,0:T(8,128)(2,1)} %constant.10.clone.along_y) | copy-start | bytes 49156
  21.5 9.2 %collective-permute-start.1 = (bf16[5,3,64,128]{3,2,1,0:T(8,128)(2,1)S(1)}, bf16[5,3,64,128]{3,2,1,0:T(8,128)(2,1)S(1)}, u32[]{:S(2)}, u32[]{:S(2)}) collective-permute-start(bf16[5,3,64,128]{3,2,1,0:T(8,128)(2,1)S(1)} %get-tuple-element.13.own_left), channel_id=1, source_target_pairs={{1,0},{2,1},{3,2},{0,3},{5,4},{6,5},{7,6},{4,7},{9,8},{10,9},{11,1... | collective-permute-start | bytes 737288 | tf_op jit(solution)/shard_map/ppermute | solution.py:748
